TPU v7x, 32 devices: a whole 2x2x4 slice. The times are simulated.
32 devices in a mesh: dp: 4 (over y, x), ctx: 8 (over z, core).
Axes of the slice: x: 2, y: 2, z: 4, core: 2. Of those that a mesh axis runs over, the one named last changes fastest.
Arguments:
- queries: bfloat16 [6144, 4096], P(('dp', 'ctx')), may hold values from -6.5 to 6.5
- keys: bfloat16 [6144, 512], P(('dp', 'ctx')), may hold values from -4 to 4
- values: bfloat16 [6144, 512], P(('dp', 'ctx')), may hold values from -6 to 6
- out_grad: bfloat16 [6144, 4096], P(('dp', 'ctx')), may hold values from -6 to 6
- hidden: bfloat16 [6144, 8192], P(('dp', 'ctx')), may hold values from -6 to 6
Outputs:
- query_grad: bfloat16 [6144, 4096], P(('dp', 'ctx'))
- key_grad: bfloat16 [6144, 512], P(('dp', 'ctx'))
- value_grad: bfloat16 [6144, 512], P(('dp', 'ctx'))
- key_weight_grad: float32 [8192, 512], P(('dp', 'ctx'))
- value_weight_grad: float32 [8192, 512], P(('dp', 'ctx'))
All inputs are finite; a program needn't handle non-finite values.
Results may differ from a plain program's by a relative error of at most 0.02.
Values may be sent and summed in bfloat16 or wider, within the bound.
No kernel may reach another device: no remote copies, remote signals or barrier semaphores. Data moves between devices by JAX's collectives and lax.ppermute only.
A program may use at most 256 MiB of HBM per device.

v0:
```python
import math

import jax
import jax.numpy as jnp
from jax import lax
from jax.sharding import PartitionSpec as P

HD = 128
BLOCK = 512


def on_device(queries, keys, values, out_grad, hidden):
    tok_rows = queries.shape[0]
    ctx_size = lax.axis_size("ctx")
    kv_heads = keys.shape[1] // HD
    replicas = ctx_size // kv_heads
    score_scale = 1.0 / math.sqrt(HD)
    query_slab, grad_slab = (
        lax.all_to_all(queries, "ctx", split_axis=1, concat_axis=0, tiled=True),
        lax.all_to_all(out_grad, "ctx", split_axis=1, concat_axis=0, tiled=True),
    )
    seq_len = query_slab.shape[0]
    per_dev = query_slab.shape[1] // HD
    key_all, value_all = (
        lax.all_gather(keys, "ctx", axis=0, tiled=True),
        lax.all_gather(values, "ctx", axis=0, tiled=True),
    )
    offset = lax.axis_index("ctx") // replicas * HD
    key_head = lax.dynamic_slice_in_dim(key_all, offset, HD, 1)
    value_head = lax.dynamic_slice_in_dim(value_all, offset, HD, 1)
    query_heads = query_slab.reshape(seq_len, per_dev, HD)
    grad_heads = grad_slab.reshape(seq_len, per_dev, HD)
    key_total = jnp.zeros((seq_len, HD), jnp.float32)
    value_total = jnp.zeros((seq_len, HD), jnp.float32)
    pieces = []
    for block_index in range(seq_len // BLOCK):
        low_row = block_index * BLOCK
        high_row = low_row + BLOCK
        query_block = query_heads[low_row:high_row]
        grad_block = grad_heads[low_row:high_row]
        key_block = key_head[:high_row]
        value_block = value_head[:high_row]
        scores = (
            jnp.einsum("qhd,kd->hqk", query_block, key_block, preferred_element_type=jnp.float32)
            * score_scale
        )
        row_ids = lax.broadcasted_iota(jnp.int32, (BLOCK, high_row), 0) + low_row
        col_ids = lax.broadcasted_iota(jnp.int32, (BLOCK, high_row), 1)
        scores = jnp.where((col_ids <= row_ids)[None], scores, -jnp.inf)
        row_max = jnp.max(scores, axis=2, keepdims=True)
        exponent = jnp.exp(scores - row_max)
        probability = exponent / jnp.sum(exponent, axis=2, keepdims=True)
        prob_low = probability.astype(jnp.bfloat16)
        attended = jnp.einsum(
            "hqk,kd->hqd", prob_low, value_block, preferred_element_type=jnp.float32
        )
        grad_major = jnp.transpose(grad_block, (1, 0, 2)).astype(jnp.float32)
        row_delta = jnp.sum(grad_major * attended, axis=2, keepdims=True)
        prob_grad = jnp.einsum(
            "qhd,kd->hqk", grad_block, value_block, preferred_element_type=jnp.float32
        )
        score_grad = (probability * (prob_grad - row_delta)).astype(jnp.bfloat16)
        query_piece = (
            jnp.einsum("hqk,kd->qhd", score_grad, key_block, preferred_element_type=jnp.float32)
            * score_scale
        )
        pieces.append(query_piece.astype(jnp.bfloat16))
        key_total = key_total.at[:high_row].add(
            jnp.einsum("hqk,qhd->kd", score_grad, query_block, preferred_element_type=jnp.float32)
            * score_scale
        )
        value_total = value_total.at[:high_row].add(
            jnp.einsum("hqk,qhd->kd", prob_low, grad_block, preferred_element_type=jnp.float32)
        )
    query_local = jnp.concatenate(pieces, 0).reshape(seq_len, per_dev * HD)
    query_grad = lax.all_to_all(query_local, "ctx", split_axis=0, concat_axis=1, tiled=True)
    key_slots, value_slots = (
        lax.all_to_all(
            key_total.astype(jnp.bfloat16), "ctx", split_axis=0, concat_axis=1, tiled=True
        ),
        lax.all_to_all(
            value_total.astype(jnp.bfloat16), "ctx", split_axis=0, concat_axis=1, tiled=True
        ),
    )

    def fold_slots(slot_array):
        summed = jnp.sum(
            slot_array.reshape(tok_rows, kv_heads, replicas, HD).astype(jnp.float32), axis=2
        )
        return summed.astype(jnp.bfloat16).reshape(tok_rows, kv_heads * HD)

    key_grad = fold_slots(key_slots)
    value_grad = fold_slots(value_slots)
    kv_grads = jnp.concatenate([key_grad, value_grad], 1)
    contract = (((0,), (0,)), ((), ()))
    width_share = lax.all_to_all(hidden, "dp", split_axis=1, concat_axis=0, tiled=True)
    grads_across = lax.all_gather(kv_grads, "dp", axis=0, tiled=True)
    gradients = lax.psum_scatter(
        lax.dot_general(
            width_share, grads_across, contract, preferred_element_type=jnp.float32
        ).astype(jnp.bfloat16),
        "ctx",
        scatter_dimension=0,
        tiled=True,
    ).astype(jnp.float32)
    kv_width = kv_heads * HD
    return (query_grad, key_grad, value_grad, gradients[:, :kv_width], gradients[:, kv_width:])


def solution(mesh):
    return jax.shard_map(
        on_device,
        mesh=mesh,
        in_specs=(
            P(("dp", "ctx"), None),
            P(("dp", "ctx"), None),
            P(("dp", "ctx"), None),
            P(("dp", "ctx"), None),
            P(("dp", "ctx"), None),
        ),
        out_specs=(
            P(("dp", "ctx"), None),
            P(("dp", "ctx"), None),
            P(("dp", "ctx"), None),
            P(("dp", "ctx"), None),
            P(("dp", "ctx"), None),
        ),
        check_vma=False,
    )
```

profile of v0, /device:TPU:0, one launch (start us, length us, event | category | flops | bytes accessed | tf_op | source)
XLA Modules:
  0.0 383.7 jit_solution(6427103710686018292)
XLA Ops:
  7.2 2.8 copy.217
  10.0 6.3 %all-to-all-start = ((bf16[192,8,512]{2,0,1:T(8,128)(2,1)}), bf16[192,8,512]{2,0,1:T(8,128)(2,1)S(1)}, u32[]{:S(2)}, u32[]{:S(2)}) async-start(bf16[192,8,512]{2,0,1:T(8,128)(2,1)} %bitcast.191), calls=%async_computation | async-start | bytes 3145728 | tf_op jit(solution)/shard_map/all_to_all | solution.py:19
  18.4 48.4 %all-to-all-done = bf16[192,8,512]{2,0,1:T(8,128)(2,1)S(1)} async-done(((bf16[192,8,512]{2,0,1:T(8,128)(2,1)}), bf16[192,8,512]{2,0,1:T(8,128)(2,1)S(1)}, u32[]{:S(2)}, u32[]{:S(2)}) %all-to-all-start) | async-done | bytes 1572896 | tf_op jit(solution)/shard_map/all_to_all | solution.py:19
  66.8 3.6 all-to-all-start.1
  75.8 45.0 %all-to-all-done.1 = bf16[192,8,512]{2,0,1:T(8,128)(2,1)S(1)} async-done(((bf16[192,8,512]{2,0,1:T(8,128)(2,1)}), bf16[192,8,512]{2,0,1:T(8,128)(2,1)S(1)}, u32[]{:S(2)}, u32[]{:S(2)}) %all-to-all-start.1) | async-done | bytes 1572896 | tf_op jit(solution)/shard_map/all_to_all | solution.py:20
  127.3 2.1 fusion.104
  129.5 1.9 copy-done.5
  132.8 2.1 fusion.33
  134.9 3.1 fusion.14
  140.4 7.4 %fusion.99 = (f32[4,512]{1,0:T(4,128)S(1)}, f32[4,512,1024]{1,2,0:T(8,128)}) fusion(pred[512,1024]{0,1:T(8,128)(4,1)S(1)} %copy-done.14, bf16[512,4,128]{2,1,0:T(4,128)(2,1)} %get-tuple-element.122, bf16[1536,512]{1,0:T(8,128)(2,1)} %all-gather.4.cloned.1.call-done, s32[]{:T(128)S(6)} %select_n.22), kind=kOutput, calls=%fused_computation.135 | convolution fusion | flops 545260544 | bytes 9707524 | tf_op jit(solution)/shard_map/sub | solution.py:51
  147.8 4.6 %fusion.18 = bf16[4,512,1024]{1,2,0:T(8,128)(2,1)S(1)} fusion(f32[4,512,1024]{1,2,0:T(8,128)} %get-tuple-element.129, f32[4,512]{1,0:T(4,128)S(1)} %get-tuple-element.128), kind=kLoop, calls=%fused_computation.30 | loop fusion | flops 4194304 | bytes 12591104 | tf_op jit(solution)/shard_map/convert_element_type | solution.py:53
  152.5 7.7 %fusion.47 = f32[1536,512,4]{1,0,2:T(8,128)} fusion(bf16[512,4,128]{2,1,0:T(4,128)(2,1)S(1)} %copy-done.8, bf16[1536,512]{1,0:T(8,128)(2,1)} %all-gather.4.cloned.1.call-done, s32[]{:T(128)S(6)} %select_n.22), kind=kOutput, calls=%fused_computation.78 | convolution fusion | flops 805306368 | bytes 13500420 | tf_op jit(solution)/shard_map/qhd,kd->hqk/dot_general | solution.py:44
  160.2 13.9 %fusion.98 = (f32[4,512]{1,0:T(4,128)S(1)}, f32[4,512,1536]{1,2,0:T(8,128)}) fusion(f32[1536,512,4]{1,0,2:T(8,128)} %fusion.47, pred[512,1536]{0,1:T(8,128)(4,1)S(1)} %copy-done.11), kind=kOutput, calls=%fused_computation.134 | output fusion | flops 18875904 | bytes 25960448 | tf_op jit(solution)/shard_map/sub | solution.py:51
  174.1 9.0 %fusion.12 = bf16[4,512,1536]{1,2,0:T(8,128)(2,1)} fusion(f32[4,512,1536]{1,2,0:T(8,128)} %get-tuple-element.127, f32[4,512]{1,0:T(4,128)S(1)} %get-tuple-element.126), kind=kLoop, calls=%fused_computation.19 | loop fusion | flops 6291456 | bytes 18882560 | tf_op jit(solution)/shard_map/convert_element_type | solution.py:53
  186.0 2.6 fusion.23
  188.6 3.7 all-to-all-start.4
  192.2 3.8 fusion.32
  196.0 5.1 %fusion.34 = f32[4,512]{1,0:T(4,128)S(1)} fusion(bf16[4,512,1536]{1,2,0:T(8,128)(2,1)} %fusion.12, bf16[512,4,128]{2,1,0:T(4,128)(2,1)S(1)} %copy-done.16, bf16[1536,512]{1,0:T(8,128)(2,1)} %all-gather.6.cloned.1.call-done, s32[]{:T(128)S(6)} %select_n.22), kind=kOutput, calls=%fused_computation.61 | convolution fusion | flops 806090752 | bytes 7217156 | tf_op jit(solution)/shard_map/hqk,kd->hqd/dot_general | solution.py:54
  201.1 6.8 %fusion.7 = bf16[4,512,1024]{1,2,0:T(8,128)(2,1)} fusion(f32[4,512]{1,0:T(4,128)S(1)} %fusion.32, f32[4,512,1024]{1,2,0:T(8,128)} %get-tuple-element.129, f32[4,512]{1,0:T(4,128)S(1)} %get-tuple-element.128, bf16[512,4,128]{2,1,0:T(4,128)(2,1)S(1)} %get-tuple-element.119, bf16[1536,512]{1,0:T(8,128)(2,1)} %all-gather.6.cloned.1.call-done, s32[]{:T(128)S(6)} %select_n.22), kind=kOutput, calls=%fused_computation.11 | convolution fusion | flops 545259520 | bytes 13385732 | tf_op jit(solution)/shard_map/qhd,kd->hqk/dot_general | solution.py:59
  208.0 3.1 fusion.4
  211.2 6.6 %fusion.40 = f32[1536,128]{1,0:T(8,128)} fusion(f32[1536,128]{1,0:T(8,128)} %scatter-add.14, bf16[4,512,1024]{1,2,0:T(8,128)(2,1)} %fusion.7, bf16[512,4,128]{2,1,0:T(4,128)(2,1)S(1)} %copy-done.15), kind=kOutput, calls=%fused_computation.69 | convolution fusion | flops 537133056 | bytes 5767168 | tf_op jit(solution)/shard_map/hqk,qhd->kd/dot_general | solution.py:69
  217.8 3.9 %fusion.24 = bf16[1536,128]{1,0:T(8,128)(2,1)} fusion(f32[1536,128]{1,0:T(8,128)} %fusion.40, bf16[4,512,1536]{1,2,0:T(8,128)(2,1)S(1)} %fusion.4, bf16[512,4,128]{2,1,0:T(4,128)(2,1)S(1)} %copy-done.9), kind=kOutput, calls=%fused_computation.40 | convolution fusion | flops 805896192 | bytes 7995392 | tf_op jit(solution)/shard_map/hqk,qhd->kd/dot_general | solution.py:69
  221.7 4.8 %all-to-all-start.3 = ((bf16[8,192,128]{2,1,0:T(8,128)(2,1)}), bf16[8,192,128]{2,1,0:T(8,128)(2,1)}, u32[]{:S(2)}, u32[]{:S(2)}) async-start(bf16[8,192,128]{2,1,0:T(8,128)(2,1)} %bitcast.204), calls=%async_computation.3 | async-start | bytes 786432 | tf_op jit(solution)/shard_map/all_to_all | solution.py:78
  226.5 1.9 copy.215
  228.5 10.6 %all-to-all-done.3 = bf16[8,192,128]{2,1,0:T(8,128)(2,1)} async-done(((bf16[8,192,128]{2,1,0:T(8,128)(2,1)}), bf16[8,192,128]{2,1,0:T(8,128)(2,1)}, u32[]{:S(2)}, u32[]{:S(2)}) %all-to-all-start.3) | async-done | bytes 393248 | tf_op jit(solution)/shard_map/all_to_all | solution.py:78
  239.1 3.7 all-to-all-start.5
  244.9 46.2 %all-to-all-done.5 = bf16[192,4,2048]{2,0,1:T(8,128)(2,1)S(1)} async-done(((bf16[192,4,2048]{2,0,1:T(8,128)(2,1)}), bf16[192,4,2048]{2,0,1:T(8,128)(2,1)S(1)}, u32[]{:S(2)}, u32[]{:S(2)}) %all-to-all-start.5) | async-done | bytes 3145760 | tf_op jit(solution)/shard_map/all_to_all | solution.py:96
  292.0 6.5 %convert_bitcast_fusion = bf16[2048,1024]{0,1:T(8,128)(2,1)} fusion(bf16[768,1024]{1,0:T(8,128)(2,1)} %all-gather.8.cloned.1.call-done, bf16[768,2048]{1,0:T(8,128)(2,1)S(1)} %bitcast.200), kind=kOutput, calls=%fused_computation.24 | convolution fusion | flops 3223322624 | bytes 8912896 | tf_op jit(solution)/shard_map/dot_general | solution.py:99
  298.5 2.3 fusion.37
  300.8 3.5 fusion.36
  304.3 2.0 fusion.35
  308.2 64.5 %all_to_all.102 = bf16[8,192,512]{2,1,0:T(8,128)(2,1)S(1)} all-to-all(bf16[8,192,512]{2,1,0:T(8,128)(2,1)S(1)} %all_to_all.82), channel_id=1, replica_groups=mesh['dp'=4,'ctx'=8] {'ctx'}, dimensions={0} | all-to-all | bytes 3145728 | tf_op jit(solution)/shard_map/all_to_all | solution.py:76
  (89 shorter events, 29.7 us)
Async XLA Ops:
  7.2 9.9 %copy-start.10 = (bf16[192,4096]{1,0:T(8,128)(2,1)S(1)}, bf16[192,4096]{1,0:T(8,128)(2,1)}, u32[]{:S(2)}) copy-start(bf16[192,4096]{1,0:T(8,128)(2,1)} %param.24) | copy-start | bytes 4718596
  10.0 56.8 %all-to-all-start = ((bf16[192,8,512]{2,0,1:T(8,128)(2,1)}), bf16[192,8,512]{2,0,1:T(8,128)(2,1)S(1)}, u32[]{:S(2)}, u32[]{:S(2)}) async-start(bf16[192,8,512]{2,0,1:T(8,128)(2,1)} %bitcast.191), calls=%async_computation | async-start | bytes 3145728 | tf_op jit(solution)/shard_map/all_to_all | solution.py:19
  16.3 109.3 %all-gather.4.cloned.1.call-start = ((), (), s32[]{:S(2)}) async-start(), calls=%async_computation.7 | async-start | bytes 1769472 | tf_op jit(solution)/shard_map/all_gather | solution.py:25
  66.8 54.0 %all-to-all-start.1 = ((bf16[192,8,512]{2,0,1:T(8,128)(2,1)}), bf16[192,8,512]{2,0,1:T(8,128)(2,1)S(1)}, u32[]{:S(2)}, u32[]{:S(2)}) async-start(bf16[192,8,512]{2,0,1:T(8,128)(2,1)} %bitcast.190), calls=%async_computation.1 | async-start | bytes 3145728 | tf_op jit(solution)/shard_map/all_to_all | solution.py:20
  70.4 62.4 %all-gather.6.cloned.1.call-start = ((), (), s32[]{:S(2)}) async-start(), calls=%async_computation.8 | async-start | bytes 1769472 | tf_op jit(solution)/shard_map/all_gather | solution.py:26
  75.8 46.8 %copy-start.2 = (bf16[1536,4,128]{2,1,0:T(4,128)(2,1)S(1)}, bf16[1536,4,128]{2,1,0:T(4,128)(2,1)}, u32[]{:S(2)}) copy-start(bf16[1536,4,128]{2,1,0:T(4,128)(2,1)} %reshape.239) | copy-start | bytes 4718596
  122.6 1.5 copy-start.3
  129.4 1.9 copy-start.5
  129.4 2.6 copy-start.17
  138.1 1.3 copy-start.7
  138.1 2.3 copy-start.14
  147.8 4.7 %copy-start.8 = (bf16[512,4,128]{2,1,0:T(4,128)(2,1)S(1)}, bf16[512,4,128]{2,1,0:T(4,128)(2,1)}, u32[]{:S(2)}) copy-start(bf16[512,4,128]{2,1,0:T(4,128)(2,1)} %get-tuple-element.123) | copy-start | bytes 1572868
  152.4 30.7 %copy-start = (bf16[4,512,1024]{1,2,0:T(8,128)(2,1)}, bf16[4,512,1024]{1,2,0:T(8,128)(2,1)S(1)}, u32[]{:S(2)}) copy-start(bf16[4,512,1024]{1,2,0:T(8,128)(2,1)S(1)} %fusion.18) | copy-start | bytes 12582916
  152.5 7.7 %copy-start.11 = (pred[512,1536]{0,1:T(8,128)(4,1)S(1)}, pred[512,1536]{0,1:T(8,128)(4,1)}, u32[]{:S(2)}) copy-start(pred[512,1536]{0,1:T(8,128)(4,1)} %iota_compare_fusion) | copy-start | bytes 2359300
  183.1 2.8 copy-start.4
  183.1 2.9 copy-start.16
  188.6 33.1 %all-to-all-start.4 = ((bf16[8,192,128]{2,1,0:T(8,128)(2,1)}), bf16[8,192,128]{2,1,0:T(8,128)(2,1)S(1)}, u32[]{:S(2)}, u32[]{:S(2)}) async-start(bf16[8,192,128]{2,1,0:T(8,128)(2,1)} %bitcast.36), calls=%async_computation.4 | async-start | bytes 786432 | tf_op jit(solution)/shard_map/all_to_all | solution.py:81
  196.0 11.9 %slice-start = ((s8[12582912]{0:T(1024)(128)(4,1)}), s8[4194304]{0:T(1024)(128)(4,1)S(1)}, s32[]{:S(2)}) async-start(s8[12582912]{0:T(1024)(128)(4,1)} %bitcast.192), calls=%async_computation.11 | async-start | bytes 8388608
  201.1 6.8 %slice-start.1 = ((s8[12582912]{0:T(1024)(128)(4,1)}), s8[4194304]{0:T(1024)(128)(4,1)S(1)}, s32[]{:S(2)}) async-start(s8[12582912]{0:T(1024)(128)(4,1)} %bitcast.192), calls=%async_computation.12 | async-start | bytes 8388608
  201.1 6.8 %slice-start.2 = ((s8[12582912]{0:T(1024)(128)(4,1)}), s8[4194304]{0:T(1024)(128)(4,1)S(1)}, s32[]{:S(2)}) async-start(s8[12582912]{0:T(1024)(128)(4,1)} %bitcast.192), calls=%async_computation.13 | async-start | bytes 8388608
  208.0 3.1 copy-start.15
  211.1 6.7 %copy-start.1 = (bf16[4,512,1536]{1,2,0:T(8,128)(2,1)}, bf16[4,512,1536]{1,2,0:T(8,128)(2,1)S(1)}, u32[]{:S(2)}) copy-start(bf16[4,512,1536]{1,2,0:T(8,128)(2,1)S(1)} %fusion.4) | copy-start | bytes 18874372
  211.1 6.7 %copy-start.9 = (bf16[512,4,128]{2,1,0:T(4,128)(2,1)S(1)}, bf16[512,4,128]{2,1,0:T(4,128)(2,1)}, u32[]{:S(2)}) copy-start(bf16[512,4,128]{2,1,0:T(4,128)(2,1)} %get-tuple-element.123) | copy-start | bytes 1572868
  217.8 8.7 %copy-start.6 = (bf16[192,8192]{1,0:T(8,128)(2,1)S(1)}, bf16[192,8192]{1,0:T(8,128)(2,1)}, u32[]{:S(2)}) copy-start(bf16[192,8192]{1,0:T(8,128)(2,1)} %param.25) | copy-start | bytes 9437188
  221.7 17.4 %all-to-all-start.3 = ((bf16[8,192,128]{2,1,0:T(8,128)(2,1)}), bf16[8,192,128]{2,1,0:T(8,128)(2,1)}, u32[]{:S(2)}, u32[]{:S(2)}) async-start(bf16[8,192,128]{2,1,0:T(8,128)(2,1)} %bitcast.204), calls=%async_computation.3 | async-start | bytes 786432 | tf_op jit(solution)/shard_map/all_to_all | solution.py:78
  228.5 16.3 %copy-start.12 = (bf16[192,512]{1,0:T(8,128)(2,1)}, bf16[192,512]{1,0:T(8,128)(2,1)S(1)}, u32[]{:S(2)}) copy-start(bf16[192,512]{1,0:T(8,128)(2,1)S(1)} %copy_bitcast_fusion.3) | copy-start | bytes 589828
  239.1 51.9 %all-to-all-start.5 = ((bf16[192,4,2048]{2,0,1:T(8,128)(2,1)}), bf16[192,4,2048]{2,0,1:T(8,128)(2,1)S(1)}, u32[]{:S(2)}, u32[]{:S(2)}) async-start(bf16[192,4,2048]{2,0,1:T(8,128)(2,1)} %bitcast.189), calls=%async_computation.5 | async-start | bytes 6291456 | tf_op jit(solution)/shard_map/all_to_all | solution.py:96
  242.8 49.1 %all-gather.8.cloned.1.call-start = ((), (), s32[]{:S(2)}) async-start(), calls=%async_computation.9 | async-start | bytes 1966080 | tf_op jit(solution)/shard_map/all_gather | solution.py:97
  244.0 54.4 %copy-start.13 = (bf16[192,512]{1,0:T(8,128)(2,1)}, bf16[192,512]{1,0:T(8,128)(2,1)S(1)}, u32[]{:S(2)}) copy-start(bf16[192,512]{1,0:T(8,128)(2,1)S(1)} %copy_bitcast_fusion.4) | copy-start | bytes 589828
  244.8 129.2 %reduce-scatter.2.cloned.1.call-start = ((), (), s32[]{:S(2)}) async-start(), calls=%async_computation.10 | async-start | bytes 4718592 | tf_op jit(solution)/shard_map/reduce_scatter | solution.py:98
  298.4 5.9 %slice-start.3 = ((s8[6291456]{0:T(1024)(128)(4,1)}), s8[2097152]{0:T(1024)(128)(4,1)S(1)}, s32[]{:S(2)}) async-start(s8[6291456]{0:T(1024)(128)(4,1)} %bitcast.194), calls=%async_computation.14 | async-start | bytes 4194304
  298.5 5.8 %slice-start.4 = ((s8[6291456]{0:T(1024)(128)(4,1)}), s8[4194304]{0:T(1024)(128)(4,1)S(1)}, s32[]{:S(2)}) async-start(s8[6291456]{0:T(1024)(128)(4,1)} %bitcast.194), calls=%async_computation.15 | async-start | bytes 8388608
Sparse Core Ops, SparseCore 0:
  18.8 44.8 all-gather.3
  72.9 44.7 all-gather.5
  246.1 45.8 all-gather.7
  298.6 72.9 reduce-scatter.1
where the time goes:
time: 389 us; the launch traced here: 384 us
  waiting for transfers between devices  153 us (39%)
  matrix products  70.9 us (18%)
  blocking collectives  64.5 us (17%)
  other arithmetic  35.2 us (9%)
  local copies, waits for them, and re-layouts  24.2 us (6%)
  starting transfers between devices  22.2 us (6%)
  between operations  14.2 us (4%)
    all_to_all x1, blocking collectives, on_device(): lax.all_to_all(query_local, 'ctx', split_axis=0, concat_axis=1, tiled=True)  64.5 us
    all_to_all x1, waiting for transfers between devices, on_device(): lax.all_to_all(queries, 'ctx', split_axis=1, concat_axis=0, tiled=True)  48.4 us
    all_to_all x1, waiting for transfers between devices, on_device(): lax.all_to_all(hidden, 'dp', split_axis=1, concat_axis=0, tiled=True)  46.2 us
    all_to_all x1, waiting for transfers between devices, on_device(): lax.all_to_all(out_grad, 'ctx', split_axis=1, concat_axis=0, tiled=True)  45 us
    sub x2, other arithmetic, on_device(): exponent = jnp.exp(scores - row_max)  16.1 us
    convert_element_type x3, other arithmetic, on_device(): prob_low = probability.astype(jnp.bfloat16)  14.3 us
    dot_general x3, matrix products, on_device(): jnp.einsum('qhd,kd->hqk', grad_block, value_block, preferred_element_type...  13.1 us
    dot_general x3, matrix products, on_device(): jnp.einsum('hqk,qhd->kd', score_grad, query_block, preferred_element_type...  11.2 us
  transfers between devices with their start and end apart: 9, of which 5 were waited for; matrix products, arithmetic and copies ran while one was open for 16% of the time, Pallas kernels for 0%

commit v1 on v0

v1 whole, which is shorter than its diff:
```python
import functools
import math

import jax
import jax.numpy as jnp
from jax import lax
from jax.experimental import pallas as pl
from jax.experimental.pallas import tpu as pltpu
from jax.sharding import PartitionSpec as P

HD = 128
PAIR = 2
F32, BF16 = jnp.float32, jnp.bfloat16
NT = (((1,), (1,)), ((), ()))
TN = (((0,), (0,)), ((), ()))


def xor_permute(array, axis, size, mask):
    return lax.ppermute(array, axis, [(i, i ^ mask) for i in range(size)])


def attention_kernel(
    chips, tok, group, head, pos_ref, q_own, q_rx, g_own, g_rx, *refs
):
    kv_in = refs[:chips]
    dq_own, dq_oth = refs[chips : chips + 2]
    dkv_out = refs[chips + 2 : 2 * chips + 2]
    qs, gs, kv, acc, es, ds, ms, dqa, dqs, sems = refs[2 * chips + 2 :]
    span = PAIR * tok
    rows = PAIR * span
    width = group * HD
    chip, core = pos_ref[0], pos_ref[1]
    heads = q_own.shape[1] // (PAIR * width)
    col = pl.multiple_of((core * heads + head) * width, width)
    own = pl.multiple_of(core * tok, tok)
    oth = pl.multiple_of((1 - core) * tok, tok)
    copies = [
        (q_own.at[:, pl.ds(col, width)], qs.at[pl.ds(own, tok)]),
        (q_rx, qs.at[pl.ds(oth, tok)]),
        (g_own.at[:, pl.ds(col, width)], gs.at[pl.ds(own, tok)]),
        (g_rx, gs.at[pl.ds(oth, tok)]),
    ] + [
        (kv_in[s], kv.at[pl.ds(pl.multiple_of((chip ^ s) * span, span), span)])
        for s in range(chips)
    ]
    started = [pltpu.make_async_copy(a, b, sems.at[i]) for i, (a, b) in enumerate(copies)]
    for c in started:
        c.start()
    acc[...] = jnp.zeros_like(acc)
    for c in started:
        c.wait()
    scale = 1.0 / math.sqrt(HD)
    log_scale = scale * math.log2(math.e)

    def two_heads(ref, u):
        both = ref[:, pl.ds(pl.multiple_of(u * PAIR * HD, PAIR * HD), PAIR * HD)]
        return jnp.concatenate([both[:, i * HD : (i + 1) * HD] for i in range(PAIR)], 0)

    def unit(u, _):
        q = two_heads(qs, u)
        g = two_heads(gs, u)

        def scores(j, carry, masked):
            top, total, weighted = carry
            at = pl.ds(pl.multiple_of(j * span, span), span)
            s = lax.dot_general(kv[at, :HD], q, NT, preferred_element_type=F32) * log_scale
            if masked:
                key_ids = lax.broadcasted_iota(jnp.int32, (span, span), 0)
                row_ids = lax.broadcasted_iota(jnp.int32, (span, span), 1)
                keep = key_ids <= row_ids
                s = jnp.concatenate(
                    [jnp.where(keep, s[:, i * span : (i + 1) * span], -jnp.inf) for i in range(PAIR)], 1
                )
            dp = lax.dot_general(kv[at, HD:], g, NT, preferred_element_type=F32)
            new = jnp.maximum(top, jnp.max(s, axis=0, keepdims=True))
            e = jnp.exp2(s - new)
            fade = jnp.exp2(top - new)
            es[j] = e
            ds[j] = dp
            ms[j] = new
            return (
                new,
                total * fade + jnp.sum(e, axis=0, keepdims=True),
                weighted * fade + jnp.sum(e * dp, axis=0, keepdims=True),
            )

        zero = jnp.zeros((1, rows), F32)
        carry = scores(chip, (jnp.full((1, rows), -jnp.inf, F32), zero, zero), True)
        top, total, weighted = lax.fori_loop(
            0, chip, lambda j, c: scores(j, c, False), carry
        )
        inv = 1.0 / total
        delta = weighted * inv
        dqa[...] = jnp.zeros_like(dqa)

        def grads(j, _):
            at = pl.ds(pl.multiple_of(j * span, span), span)
            p = es[j] * (jnp.exp2(ms[j] - top) * inv)
            sg = (p * (ds[j] - delta)).astype(BF16)
            acc[at, HD:] += jnp.dot(p.astype(BF16), g, preferred_element_type=F32)
            acc[at, :HD] += jnp.dot(sg, q, preferred_element_type=F32)
            dqa[...] += lax.dot_general(sg, kv[at, :HD], TN, preferred_element_type=F32)
            return 0

        lax.fori_loop(0, chip + 1, grads, 0)
        out = (dqa[...] * scale).astype(BF16)
        dqs[:, pl.ds(pl.multiple_of(u * PAIR * HD, PAIR * HD), PAIR * HD)] = jnp.concatenate(
            [out[i * span : (i + 1) * span] for i in range(PAIR)], 1
        )
        return 0

    lax.fori_loop(0, group // PAIR, unit, 0)
    dq_own[...] = dqs[pl.ds(own, tok), :]
    dq_oth[...] = dqs[pl.ds(oth, tok), :]
    for s in range(chips):
        j = chip ^ s
        at = pl.ds(pl.multiple_of(j * span, span), span)
        out = dkv_out[s]

        @pl.when(j <= chip)
        def _():
            out[:, :HD] = (acc[at, :HD] * scale).astype(out.dtype)
            out[:, HD:] = acc[at, HD:].astype(out.dtype)

        @pl.when(j > chip)
        def _():
            out[...] = jnp.zeros_like(out)


def attention(pos, q_own, q_rx, g_own, g_rx, kv_slots, head):
    chips = len(kv_slots)
    span = kv_slots[0].shape[0]
    tok = span // PAIR
    width = q_rx.shape[1]
    group = width // HD
    rows = PAIR * span
    anywhere = pl.BlockSpec(memory_space=pl.ANY)
    vmem = pl.BlockSpec(memory_space=pltpu.VMEM)
    out_shape = [jax.ShapeDtypeStruct((tok, width), BF16)] * 2 + [
        jax.ShapeDtypeStruct((span, 2 * HD), BF16 if s else F32) for s in range(chips)
    ]
    cells = width // HD * span * (chips + 1) * span // 2
    outs = pl.pallas_call(
        functools.partial(attention_kernel, chips, tok, group, head),
        out_shape=out_shape,
        in_specs=[pl.BlockSpec(memory_space=pltpu.SMEM)] + [anywhere] * (4 + chips),
        out_specs=[vmem] * (2 + chips),
        scratch_shapes=[
            pltpu.VMEM((span, width), BF16),
            pltpu.VMEM((span, width), BF16),
            pltpu.VMEM((chips * span, 2 * HD), BF16),
            pltpu.VMEM((chips * span, 2 * HD), F32),
            pltpu.VMEM((chips, span, rows), F32),
            pltpu.VMEM((chips, span, rows), F32),
            pltpu.VMEM((chips, 1, rows), F32),
            pltpu.VMEM((rows, HD), F32),
            pltpu.VMEM((span, width), BF16),
            pltpu.SemaphoreType.DMA((4 + chips,)),
        ],
        compiler_params=pltpu.CompilerParams(vmem_limit_bytes=44 * 1024 * 1024),
        cost_estimate=pl.CostEstimate(
            flops=10 * cells * HD, bytes_accessed=6 * span * width, transcendentals=cells
        ),
        name="attention_grads",
    )(pos, q_own, q_rx, g_own, g_rx, *kv_slots)
    return outs[0], outs[1], outs[2:]


def on_device(queries, keys, values, out_grad, hidden):
    tok = queries.shape[0]
    n_dp, n_ctx = lax.axis_size("dp"), lax.axis_size("ctx")
    chips = n_ctx // PAIR
    kv_heads = keys.shape[1] // HD
    own_heads = kv_heads // PAIR
    width = queries.shape[1] // kv_heads
    dp, ctx = lax.axis_index("dp"), lax.axis_index("ctx")
    chip, core = ctx // PAIR, ctx % PAIR
    pos = jnp.stack([chip, core]).astype(jnp.int32)
    first = core == 0

    def swap(x):
        return xor_permute(x, "ctx", n_ctx, 1)

    def across(x, mask):
        return xor_permute(x, "ctx", n_ctx, mask * PAIR)

    def in_order(mine, theirs, axis):
        return jnp.where(
            first,
            jnp.concatenate([mine, theirs], axis),
            jnp.concatenate([theirs, mine], axis),
        )

    def columns(x, head, size):
        return lax.dynamic_slice_in_dim(x, head * size, size, 1)

    def gather_kv(a):
        mine = core * own_heads + a
        theirs = (1 - core) * own_heads + a
        kept = jnp.concatenate([columns(keys, mine, HD), columns(values, mine, HD)], 1)
        sent = jnp.concatenate([columns(keys, theirs, HD), columns(values, theirs, HD)], 1)
        slots = {0: in_order(kept, swap(sent), 0)}
        bit = chips // 2
        while bit:
            slots.update({s ^ bit: across(x, bit) for s, x in slots.items()})
            bit //= 2
        return [slots[s] for s in range(chips)]

    def reduce_blocks(blocks):
        cur = dict(enumerate(blocks))
        bit = 1
        while bit < chips:
            for s in [s for s in cur if s & bit]:
                got = across(cur.pop(s).astype(BF16), bit)
                cur[s ^ bit] = cur[s ^ bit].astype(F32) + got.astype(F32)
            bit *= 2
        return cur[0]

    share = hidden.shape[1] // n_dp
    parts = [columns(hidden, dp, share)] + [
        xor_permute(columns(hidden, dp ^ s, share), "dp", n_dp, s) for s in range(1, n_dp)
    ]
    hidden_own = jnp.concatenate(parts, 0)
    hidden_oth = swap(hidden_own)

    query_own, query_oth, key_value, weights = [], [], [], []
    for a in range(own_heads):
        theirs = (1 - core) * own_heads + a
        q_rx = swap(columns(queries, theirs, width))
        g_rx = swap(columns(out_grad, theirs, width))
        kv_slots = gather_kv(a)
        dq_own, dq_oth, blocks = attention(pos, queries, q_rx, out_grad, g_rx, kv_slots, a)
        query_own.append(dq_own)
        query_oth.append(swap(dq_oth))
        total = reduce_blocks(blocks).astype(BF16)
        total = jnp.where(first, total, jnp.concatenate([total[tok:], total[:tok]], 0))
        key_value.append((total[:tok], swap(total[tok:])))
        every = [total] + [xor_permute(total, "dp", n_dp, s) for s in range(1, n_dp)]
        kv_own = jnp.concatenate([x[:tok] for x in every], 0)
        kv_oth = jnp.concatenate([x[tok:] for x in every], 0)
        product = lax.dot_general(
            hidden_own, kv_own, TN, preferred_element_type=F32
        ) + lax.dot_general(hidden_oth, kv_oth, TN, preferred_element_type=F32)
        product = product.astype(BF16).reshape(chips, share // chips, 2 * HD)
        summed = reduce_blocks(
            [lax.dynamic_index_in_dim(product, chip ^ s, 0, False) for s in range(chips)]
        ).astype(F32)
        rows = share // n_ctx
        mine = lax.dynamic_slice_in_dim(summed, core * rows, rows, 0)
        theirs = lax.dynamic_slice_in_dim(summed, (1 - core) * rows, rows, 0)
        weights.append((mine, swap(theirs)))

    def spread(pairs, lo):
        mine = jnp.concatenate([m[:, lo : lo + HD] for m, _ in pairs], 1)
        theirs = jnp.concatenate([t[:, lo : lo + HD] for _, t in pairs], 1)
        return in_order(mine, theirs, 1)

    query_grad = in_order(
        jnp.concatenate(query_own, 1), jnp.concatenate(query_oth, 1), 1
    )
    return (
        query_grad,
        spread(key_value, 0),
        spread(key_value, HD),
        spread(weights, 0),
        spread(weights, HD),
    )


def solution(mesh):
    spec = P(("dp", "ctx"), None)
    return jax.shard_map(
        on_device, mesh=mesh, in_specs=(spec,) * 5, out_specs=(spec,) * 5, check_vma=False
    )
```

time: 389 us -> 174 us (0.45); the launches traced: 384 us -> 173 us
  waiting for transfers between devices: 153 us -> 71.7 us
  matrix products: 70.9 us -> 4.19 us
  blocking collectives: 64.5 us -> 0 us
  starting transfers between devices: 22.2 us -> 68.1 us
  other arithmetic: 35.2 us -> 5.67 us
  local copies, waits for them, and re-layouts: 24.2 us -> 8.19 us
  Pallas kernels: 0 us -> 14.5 us
  between operations: 14.2 us -> 1.1 us
    all_to_all x5 -> x0, waiting for transfers between devices: 150 us -> none  [the longest x1 48.4 us: on_device(): lax.all_to_all(queries, 'ctx', split_axis=1, concat_axis=0, tiled=True)]
    ppermute x0 -> x40, waiting for transfers between devices: none -> 71.7 us  [xor_permute(): return lax.ppermute(array, axis, [(i, i ^ mask) for i in range(size)])]
    ppermute x0 -> x40, starting transfers between devices: none -> 68.1 us  [xor_permute(): return lax.ppermute(array, axis, [(i, i ^ mask) for i in range(size)])]
    all_to_all x1 -> x0, blocking collectives: 64.5 us -> none  [on_device(): lax.all_to_all(query_local, 'ctx', split_axis=0, concat_axis=1, tiled=True)]
    dot_general x18 -> x4, matrix products: 63.5 us -> 4.19 us  [the longest x2 2.16 us: on_device(): lax.dot_general(hidden_own, kv_own, TN, preferred_element_type=F32)]
    all_to_all x5 -> x0, starting transfers between devices: 22.1 us -> none  [the longest x1 6.33 us: on_device(): lax.all_to_all(queries, 'ctx', split_axis=1, concat_axis=0, tiled=True)]
    sub x2 -> x0, other arithmetic: 16.1 us -> none  [on_device(): exponent = jnp.exp(scores - row_max)]
    pallas_call x0 -> x2, Pallas kernels: none -> 14.5 us  [attention(): pl.pallas_call(functools.partial(attention_kernel, chips, tok, group, hea...]
  transfers between devices with their start and end apart: 9 -> 40, of which waited for: 5 -> 15; matrix products, arithmetic and copies ran while one was open for 16% -> 7% of each run, Pallas kernels for 0% -> 8%
where the time goes in v1:
time: 174 us; the launch traced here: 173 us
  waiting for transfers between devices  71.7 us (41%)
  starting transfers between devices  68.1 us (39%)
  Pallas kernels  14.5 us (8%)
  local copies, waits for them, and re-layouts  8.19 us (5%)
  other arithmetic  5.67 us (3%)
  matrix products  4.19 us (2%)
    ppermute x40, waiting for transfers between devices, xor_permute(): return lax.ppermute(array, axis, [(i, i ^ mask) for i in range(size)])  71.7 us
    ppermute x40, starting transfers between devices, xor_permute(): return lax.ppermute(array, axis, [(i, i ^ mask) for i in range(size)])  68.1 us
    pallas_call x2, Pallas kernels, attention(): pl.pallas_call(functools.partial(attention_kernel, chips, tok, group, hea...  14.5 us
    dynamic_slice x4, local copies, waits for them, and re-layouts, columns(): return lax.dynamic_slice_in_dim(x, head * size, size, 1)  7.76 us
    select_n x7, other arithmetic, in_order(): jnp.where(first, jnp.concatenate([mine, theirs], axis), jnp.concatenate([...  4.62 us
  transfers between devices with their start and end apart: 40, of which 15 were waited for; matrix products, arithmetic and copies ran while one was open for 7% of the time, Pallas kernels for 8%

profile of v1, /device:TPU:0, one launch (start us, length us, event | category | flops | bytes accessed | tf_op | source)
XLA Modules:
  0.0 173.5 jit_solution(16253057237016446980)
XLA Ops:
  0.7 2.2 %constant_dynamic-slice_fusion.19 = (bf16[192,1024]{1,0:T(8,128)(2,1)}, bf16[192,1024]{1,0:T(8,128)(2,1)}) fusion(bf16[192,4096]{1,0:T(8,128)(2,1)} %q_own.3, s32[]{:T(128)S(6)} %select_n.123, s32[]{:T(128)S(6)} %select_n.128), kind=kLoop, calls=%fused_computation.81 | loop fusion | bytes 1572872 | tf_op jit(solution)/shard_map/dynamic_slice | solution.py:195
  5.8 3.8 %collective-permute-start.10 = (bf16[384,256]{1,0:T(8,128)(2,1)S(1)}, bf16[384,256]{1,0:T(8,128)(2,1)}, u32[]{:S(2)}, u32[]{:S(2)}) collective-permute-start(bf16[384,256]{1,0:T(8,128)(2,1)S(1)} %maximum_select_fusion.4.refs_0_), channel_id=1, source_target_pairs={{0,4},{1,5},{2,6},{3,7},{4,0},{5,1},{6,2},{7,3},{8,12},{9,13},{10,... | collective-permute-start | bytes 589832 | tf_op jit(solution)/shard_map/ppermute | solution.py:19
  10.6 1.6 collective-permute-start.9
  12.7 7.1 %collective-permute-done.10.refs_2_ = bf16[384,256]{1,0:T(8,128)(2,1)} collective-permute-done((bf16[384,256]{1,0:T(8,128)(2,1)S(1)}, bf16[384,256]{1,0:T(8,128)(2,1)}, u32[]{:S(2)}, u32[]{:S(2)}) %collective-permute-start.10) | collective-permute-done | bytes 196640 | tf_op jit(solution)/shard_map/ppermute | solution.py:19
  20.4 3.6 %constant_dynamic-slice_fusion.7 = (bf16[192,2048]{1,0:T(8,128)(2,1)}, bf16[192,2048]{1,0:T(8,128)(2,1)}, bf16[192,2048]{1,0:T(8,128)(2,1)}, bf16[192,2048]{1,0:T(8,128)(2,1)}) fusion(bf16[192,8192]{1,0:T(8,128)(2,1)} %param.9, s32[]{:T(128)S(6)} %select_n.139, s32[]{:T(128)S(6)} %select_n.140, s32[]{:T(128)S(6)} %select_n.142, s32[]{:T(128)S(6)} %select_n.141), kind=kLoop, calls=%fused_computation.69 | loop fusion | bytes 6291472 | tf_op jit(solution)/shard_map/dynamic_slice | solution.py:195
  24.0 3.9 %collective-permute-done.4.refs_2_ = bf16[384,256]{1,0:T(8,128)(2,1)} collective-permute-done((bf16[384,256]{1,0:T(8,128)(2,1)S(1)}, bf16[384,256]{1,0:T(8,128)(2,1)}, u32[]{:S(2)}, u32[]{:S(2)}) %collective-permute-start.4) | collective-permute-done | bytes 196640 | tf_op jit(solution)/shard_map/ppermute | solution.py:19
  28.0 2.6 %collective-permute-start.24 = (bf16[192,2048]{1,0:T(8,128)(2,1)}, bf16[192,2048]{1,0:T(8,128)(2,1)S(1)}, u32[]{:S(2)}, u32[]{:S(2)}) collective-permute-start(bf16[192,2048]{1,0:T(8,128)(2,1)} %get-tuple-element.31), channel_id=1, source_target_pairs={{0,24},{8,16},{16,8},{24,0},{1,25},{9,17},{17,9},{25,1},{2,26},{10... | collective-permute-start | bytes 2359304 | tf_op jit(solution)/shard_map/ppermute | solution.py:19
  31.1 1.5 collective-permute-start.5
  32.5 7.1 %attention_grads.3 = (bf16[192,1024]{1,0:T(8,128)(2,1)S(1)}, bf16[192,1024]{1,0:T(8,128)(2,1)S(1)}, f32[384,256]{1,0:T(8,128)S(1)}, bf16[384,256]{1,0:T(8,128)(2...) custom-call(s32[2]{0:T(128)S(1)} %pad_add_fusion.pos_ref, bf16[192,4096]{1,0:T(8,128)(2,1)S(1)} %copy-done, ...), custom_call_target="tpu_custom_call" | custom-call | flops 3774873600 | bytes 2359296 | tf_op jit(solution)/shard_map/attention_grads/pallas_call | solution.py:143
  41.8 4.9 %collective-permute-start.18 = (bf16[384,256]{1,0:T(8,128)(2,1)S(1)}, bf16[384,256]{1,0:T(8,128)(2,1)S(1)}, u32[]{:S(2)}, u32[]{:S(2)}) collective-permute-start(bf16[384,256]{1,0:T(8,128)(2,1)S(1)} %get-tuple-element.28), channel_id=1, source_target_pairs={{0,2},{1,3},{2,0},{3,1},{4,6},{5,7},{6,4},{7,5},{8,10},{9,11},{10,... | collective-permute-start | bytes 589832 | tf_op jit(solution)/shard_map/ppermute | solution.py:19
  46.6 7.4 %attention_grads.2 = (bf16[192,1024]{1,0:T(8,128)(2,1)S(1)}, bf16[192,1024]{1,0:T(8,128)(2,1)S(1)}, f32[384,256]{1,0:T(8,128)S(1)}, bf16[384,256]{1,0:T(8,128)(2...) custom-call(s32[2]{0:T(128)S(1)} %pad_add_fusion.pos_ref, bf16[192,4096]{1,0:T(8,128)(2,1)S(1)} %copy-done, ...), custom_call_target="tpu_custom_call" | custom-call | flops 3774873600 | bytes 2359296 | tf_op jit(solution)/shard_map/attention_grads/pallas_call | solution.py:143
  54.1 4.9 %collective-permute-start.15 = (bf16[384,256]{1,0:T(8,128)(2,1)S(1)}, bf16[384,256]{1,0:T(8,128)(2,1)S(1)}, u32[]{:S(2)}, u32[]{:S(2)}) collective-permute-start(bf16[384,256]{1,0:T(8,128)(2,1)S(1)} %get-tuple-element.24), channel_id=1, source_target_pairs={{0,2},{1,3},{2,0},{3,1},{4,6},{5,7},{6,4},{7,5},{8,10},{9,11},{10,... | collective-permute-start | bytes 589832 | tf_op jit(solution)/shard_map/ppermute | solution.py:19
  59.0 5.4 %collective-permute-done.15 = bf16[384,256]{1,0:T(8,128)(2,1)S(1)} collective-permute-done((bf16[384,256]{1,0:T(8,128)(2,1)S(1)}, bf16[384,256]{1,0:T(8,128)(2,1)S(1)}, u32[]{:S(2)}, u32[]{:S(2)}) %collective-permute-start.15) | collective-permute-done | bytes 196640 | tf_op jit(solution)/shard_map/ppermute | solution.py:19
  64.5 1.8 %collective-permute-start.17 = (bf16[384,256]{1,0:T(8,128)(2,1)S(1)}, bf16[384,256]{1,0:T(8,128)(2,1)S(1)}, u32[]{:S(2)}, u32[]{:S(2)}) collective-permute-start(bf16[384,256]{1,0:T(8,128)(2,1)S(1)} %get-tuple-element.26), channel_id=1, source_target_pairs={{0,2},{1,3},{2,0},{3,1},{4,6},{5,7},{6,4},{7,5},{8,10},{9,11},{10,... | collective-permute-start | bytes 589832 | tf_op jit(solution)/shard_map/ppermute | solution.py:19
  66.6 23.1 %collective-permute-start.19 = (bf16[384,256]{1,0:T(8,128)(2,1)S(1)}, bf16[384,256]{1,0:T(8,128)(2,1)S(1)}, u32[]{:S(2)}, u32[]{:S(2)}) collective-permute-start(bf16[384,256]{1,0:T(8,128)(2,1)S(1)} %add_convert_fusion.1), channel_id=1, source_target_pairs={{0,4},{1,5},{2,6},{3,7},{4,0},{5,1},{6,2},{7,3},{8,12},{9,13},{10,... | collective-permute-start | bytes 589832 | tf_op jit(solution)/shard_map/ppermute | solution.py:19
  90.0 5.4 %collective-permute-start.16 = (bf16[384,256]{1,0:T(8,128)(2,1)S(1)}, bf16[384,256]{1,0:T(8,128)(2,1)S(1)}, u32[]{:S(2)}, u32[]{:S(2)}) collective-permute-start(bf16[384,256]{1,0:T(8,128)(2,1)S(1)} %add_convert_fusion.3), channel_id=1, source_target_pairs={{0,4},{1,5},{2,6},{3,7},{4,0},{5,1},{6,2},{7,3},{8,12},{9,13},{10,... | collective-permute-start | bytes 589832 | tf_op jit(solution)/shard_map/ppermute | solution.py:19
  95.6 2.0 %collective-permute-start.34 = (bf16[384,256]{1,0:T(8,128)(2,1)S(1)}, bf16[384,256]{1,0:T(8,128)(2,1)S(1)}, u32[]{:S(2)}, u32[]{:S(2)}) collective-permute-start(bf16[384,256]{1,0:T(8,128)(2,1)S(1)} %maximum_select_fusion.6), channel_id=1, source_target_pairs={{0,24},{8,16},{16,8},{24,0},{1,25},{9,17},{17,9},{25,1},{2,26},{10... | collective-permute-start | bytes 589832 | tf_op jit(solution)/shard_map/ppermute | solution.py:19
  97.5 10.7 %collective-permute-done.16 = bf16[384,256]{1,0:T(8,128)(2,1)S(1)} collective-permute-done((bf16[384,256]{1,0:T(8,128)(2,1)S(1)}, bf16[384,256]{1,0:T(8,128)(2,1)S(1)}, u32[]{:S(2)}, u32[]{:S(2)}) %collective-permute-start.16) | collective-permute-done | bytes 196640 | tf_op jit(solution)/shard_map/ppermute | solution.py:19
  109.4 1.4 maximum_select_fusion
  110.8 1.6 collective-permute-start.33
  112.6 1.1 collective-permute-done.20
  116.4 6.3 %collective-permute-done.33 = bf16[384,256]{1,0:T(8,128)(2,1)S(1)} collective-permute-done((bf16[384,256]{1,0:T(8,128)(2,1)S(1)}, bf16[384,256]{1,0:T(8,128)(2,1)S(1)}, u32[]{:S(2)}, u32[]{:S(2)}) %collective-permute-start.33) | collective-permute-done | bytes 196640 | tf_op jit(solution)/shard_map/ppermute | solution.py:19
  122.8 1.2 collective-permute-start.25
  124.0 2.5 %collective-permute-done.26 = bf16[384,256]{1,0:T(8,128)(2,1)S(1)} collective-permute-done((bf16[384,256]{1,0:T(8,128)(2,1)S(1)}, bf16[384,256]{1,0:T(8,128)(2,1)S(1)}, u32[]{:S(2)}, u32[]{:S(2)}) %collective-permute-start.26) | collective-permute-done | bytes 196640 | tf_op jit(solution)/shard_map/ppermute | solution.py:19
  126.6 2.3 %collective-permute-done.25 = bf16[384,256]{1,0:T(8,128)(2,1)S(1)} collective-permute-done((bf16[384,256]{1,0:T(8,128)(2,1)S(1)}, bf16[384,256]{1,0:T(8,128)(2,1)S(1)}, u32[]{:S(2)}, u32[]{:S(2)}) %collective-permute-start.25) | collective-permute-done | bytes 196640 | tf_op jit(solution)/shard_map/ppermute | solution.py:19
  131.1 2.0 %collective-permute-start.35 = (bf16[512,256]{1,0:T(8,128)(2,1)S(1)}, bf16[512,256]{1,0:T(8,128)(2,1)S(1)}, u32[]{:S(2)}, u32[]{:S(2)}) collective-permute-start(bf16[512,256]{1,0:T(8,128)(2,1)S(1)} %get-tuple-element.39), channel_id=1, source_target_pairs={{0,2},{1,3},{2,0},{3,1},{4,6},{5,7},{6,4},{7,5},{8,10},{9,11},{10,... | collective-permute-start | bytes 786440 | tf_op jit(solution)/shard_map/ppermute | solution.py:19
  135.4 7.7 %collective-permute-done.36 = bf16[512,256]{1,0:T(8,128)(2,1)S(1)} collective-permute-done((bf16[512,256]{1,0:T(8,128)(2,1)S(1)}, bf16[512,256]{1,0:T(8,128)(2,1)S(1)}, u32[]{:S(2)}, u32[]{:S(2)}) %collective-permute-start.36) | collective-permute-done | bytes 262176 | tf_op jit(solution)/shard_map/ppermute | solution.py:19
  144.8 2.5 %collective-permute-start.29 = (bf16[512,256]{1,0:T(8,128)(2,1)S(1)}, bf16[512,256]{1,0:T(8,128)(2,1)S(1)}, u32[]{:S(2)}, u32[]{:S(2)}) collective-permute-start(bf16[512,256]{1,0:T(8,128)(2,1)S(1)} %get-tuple-element.37), channel_id=1, source_target_pairs={{0,2},{1,3},{2,0},{3,1},{4,6},{5,7},{6,4},{7,5},{8,10},{9,11},{10,... | collective-permute-start | bytes 786440 | tf_op jit(solution)/shard_map/ppermute | solution.py:19
  147.3 12.7 %collective-permute-done.30 = bf16[512,256]{1,0:T(8,128)(2,1)S(1)} collective-permute-done((bf16[512,256]{1,0:T(8,128)(2,1)S(1)}, bf16[512,256]{1,0:T(8,128)(2,1)S(1)}, u32[]{:S(2)}, u32[]{:S(2)}) %collective-permute-start.30) | collective-permute-done | bytes 262176 | tf_op jit(solution)/shard_map/ppermute | solution.py:19
  161.2 1.7 collective-permute-done.29
  162.9 7.2 %collective-permute-done.31 = bf16[512,256]{1,0:T(8,128)(2,1)S(1)} collective-permute-done((bf16[512,256]{1,0:T(8,128)(2,1)S(1)}, bf16[512,256]{1,0:T(8,128)(2,1)S(1)}, u32[]{:S(2)}, u32[]{:S(2)}) %collective-permute-start.31) | collective-permute-done | bytes 262176 | tf_op jit(solution)/shard_map/ppermute | solution.py:19
  170.4 1.4 collective-permute-done.38
  (111 shorter events, 22.1 us)
Async XLA Ops:
  2.8 25.1 %collective-permute-start.6 = (bf16[192,1024]{1,0:T(8,128)(2,1)}, bf16[192,1024]{1,0:T(8,128)(2,1)}, u32[]{:S(2)}, u32[]{:S(2)}) collective-permute-start(bf16[192,1024]{1,0:T(8,128)(2,1)} %get-tuple-element.36), channel_id=1, source_target_pairs={{0,1},{1,0},{2,3},{3,2},{4,5},{5,4},{6,7},{7,6},{8,9},{9,8},{10,11... | collective-permute-start | bytes 1179656 | tf_op jit(solution)/shard_map/ppermute | solution.py:19
  5.8 14.0 %collective-permute-start.10 = (bf16[384,256]{1,0:T(8,128)(2,1)S(1)}, bf16[384,256]{1,0:T(8,128)(2,1)}, u32[]{:S(2)}, u32[]{:S(2)}) collective-permute-start(bf16[384,256]{1,0:T(8,128)(2,1)S(1)} %maximum_select_fusion.4.refs_0_), channel_id=1, source_target_pairs={{0,4},{1,5},{2,6},{3,7},{4,0},{5,1},{6,2},{7,3},{8,12},{9,13},{10,... | collective-permute-start | bytes 589832 | tf_op jit(solution)/shard_map/ppermute | solution.py:19
  10.5 20.0 %collective-permute-start.7 = (bf16[192,1024]{1,0:T(8,128)(2,1)}, bf16[192,1024]{1,0:T(8,128)(2,1)}, u32[]{:S(2)}, u32[]{:S(2)}) collective-permute-start(bf16[192,1024]{1,0:T(8,128)(2,1)} %get-tuple-element.34), channel_id=1, source_target_pairs={{0,1},{1,0},{2,3},{3,2},{4,5},{5,4},{6,7},{7,6},{8,9},{9,8},{10,11... | collective-permute-start | bytes 1179656 | tf_op jit(solution)/shard_map/ppermute | solution.py:19
  10.6 13.4 %collective-permute-start.9 = (bf16[384,256]{1,0:T(8,128)(2,1)S(1)}, bf16[384,256]{1,0:T(8,128)(2,1)}, u32[]{:S(2)}, u32[]{:S(2)}) collective-permute-start(bf16[384,256]{1,0:T(8,128)(2,1)S(1)} %maximum_select_fusion.4.refs_0_), channel_id=1, source_target_pairs={{0,2},{1,3},{2,0},{3,1},{4,6},{5,7},{6,4},{7,5},{8,10},{9,11},{10,... | collective-permute-start | bytes 589832 | tf_op jit(solution)/shard_map/ppermute | solution.py:19
  12.3 15.6 %collective-permute-start.4 = (bf16[384,256]{1,0:T(8,128)(2,1)S(1)}, bf16[384,256]{1,0:T(8,128)(2,1)}, u32[]{:S(2)}, u32[]{:S(2)}) collective-permute-start(bf16[384,256]{1,0:T(8,128)(2,1)S(1)} %maximum_select_fusion.3.refs_0_), channel_id=1, source_target_pairs={{0,4},{1,5},{2,6},{3,7},{4,0},{5,1},{6,2},{7,3},{8,12},{9,13},{10,... | collective-permute-start | bytes 589832 | tf_op jit(solution)/shard_map/ppermute | solution.py:19
  19.7 11.3 %collective-permute-start.11 = (bf16[384,256]{1,0:T(8,128)(2,1)}, bf16[384,256]{1,0:T(8,128)(2,1)}, u32[]{:S(2)}, u32[]{:S(2)}) collective-permute-start(bf16[384,256]{1,0:T(8,128)(2,1)} %collective-permute-done.10.refs_2_), channel_id=1, source_target_pairs={{0,2},{1,3},{2,0},{3,1},{4,6},{5,7},{6,4},{7,5},{8,10},{9,11},{10,... | collective-permute-start | bytes 589832 | tf_op jit(solution)/shard_map/ppermute | solution.py:19
  24.0 16.2 %collective-permute-start = (bf16[192,1024]{1,0:T(8,128)(2,1)}, bf16[192,1024]{1,0:T(8,128)(2,1)}, u32[]{:S(2)}, u32[]{:S(2)}) collective-permute-start(bf16[192,1024]{1,0:T(8,128)(2,1)} %get-tuple-element.35), channel_id=1, source_target_pairs={{0,1},{1,0},{2,3},{3,2},{4,5},{5,4},{6,7},{7,6},{8,9},{9,8},{10,11... | collective-permute-start | bytes 1179656 | tf_op jit(solution)/shard_map/ppermute | solution.py:19
  27.9 12.9 %collective-permute-start.1 = (bf16[192,1024]{1,0:T(8,128)(2,1)}, bf16[192,1024]{1,0:T(8,128)(2,1)}, u32[]{:S(2)}, u32[]{:S(2)}) collective-permute-start(bf16[192,1024]{1,0:T(8,128)(2,1)} %get-tuple-element.33), channel_id=1, source_target_pairs={{0,1},{1,0},{2,3},{3,2},{4,5},{5,4},{6,7},{7,6},{8,9},{9,8},{10,11... | collective-permute-start | bytes 1179656 | tf_op jit(solution)/shard_map/ppermute | solution.py:19
  28.0 36.6 %collective-permute-start.24 = (bf16[192,2048]{1,0:T(8,128)(2,1)}, bf16[192,2048]{1,0:T(8,128)(2,1)S(1)}, u32[]{:S(2)}, u32[]{:S(2)}) collective-permute-start(bf16[192,2048]{1,0:T(8,128)(2,1)} %get-tuple-element.31), channel_id=1, source_target_pairs={{0,24},{8,16},{16,8},{24,0},{1,25},{9,17},{17,9},{25,1},{2,26},{10... | collective-permute-start | bytes 2359304 | tf_op jit(solution)/shard_map/ppermute | solution.py:19
  31.1 10.7 %collective-permute-start.5 = (bf16[384,256]{1,0:T(8,128)(2,1)}, bf16[384,256]{1,0:T(8,128)(2,1)S(1)}, u32[]{:S(2)}, u32[]{:S(2)}) collective-permute-start(bf16[384,256]{1,0:T(8,128)(2,1)} %collective-permute-done.4.refs_2_), channel_id=1, source_target_pairs={{0,2},{1,3},{2,0},{3,1},{4,6},{5,7},{6,4},{7,5},{8,10},{9,11},{10,... | collective-permute-start | bytes 589832 | tf_op jit(solution)/shard_map/ppermute | solution.py:19
  39.7 26.7 %collective-permute-start.23 = (bf16[192,2048]{1,0:T(8,128)(2,1)S(1)}, bf16[192,2048]{1,0:T(8,128)(2,1)S(1)}, u32[]{:S(2)}, u32[]{:S(2)}) collective-permute-start(bf16[192,2048]{1,0:T(8,128)(2,1)S(1)} %copy-done.4), channel_id=1, source_target_pairs={{0,16},{8,24},{16,0},{24,8},{1,17},{9,25},{17,1},{25,9},{2,18},{10... | collective-permute-start | bytes 2359304 | tf_op jit(solution)/shard_map/ppermute | solution.py:19
  40.2 26.4 %collective-permute-start.22 = (bf16[192,2048]{1,0:T(8,128)(2,1)S(1)}, bf16[192,2048]{1,0:T(8,128)(2,1)S(1)}, u32[]{:S(2)}, u32[]{:S(2)}) collective-permute-start(bf16[192,2048]{1,0:T(8,128)(2,1)S(1)} %copy-done.3), channel_id=1, source_target_pairs={{0,8},{8,0},{16,24},{24,16},{1,9},{9,1},{17,25},{25,17},{2,10},{10... | collective-permute-start | bytes 2359304 | tf_op jit(solution)/shard_map/ppermute | solution.py:19
  40.7 68.6 %collective-permute-start.13 = (bf16[192,1024]{1,0:T(8,128)(2,1)S(1)}, bf16[192,1024]{1,0:T(8,128)(2,1)S(1)}, u32[]{:S(2)}, u32[]{:S(2)}) collective-permute-start(bf16[192,1024]{1,0:T(8,128)(2,1)S(1)} %get-tuple-element.20), channel_id=1, source_target_pairs={{0,1},{1,0},{2,3},{3,2},{4,5},{5,4},{6,7},{7,6},{8,9},{9,8},{10,11... | collective-permute-start | bytes 1179656 | tf_op jit(solution)/shard_map/ppermute | solution.py:19
  41.8 12.3 %collective-permute-start.18 = (bf16[384,256]{1,0:T(8,128)(2,1)S(1)}, bf16[384,256]{1,0:T(8,128)(2,1)S(1)}, u32[]{:S(2)}, u32[]{:S(2)}) collective-permute-start(bf16[384,256]{1,0:T(8,128)(2,1)S(1)} %get-tuple-element.28), channel_id=1, source_target_pairs={{0,2},{1,3},{2,0},{3,1},{4,6},{5,7},{6,4},{7,5},{8,10},{9,11},{10,... | collective-permute-start | bytes 589832 | tf_op jit(solution)/shard_map/ppermute | solution.py:19
  54.1 10.4 %collective-permute-start.15 = (bf16[384,256]{1,0:T(8,128)(2,1)S(1)}, bf16[384,256]{1,0:T(8,128)(2,1)S(1)}, u32[]{:S(2)}, u32[]{:S(2)}) collective-permute-start(bf16[384,256]{1,0:T(8,128)(2,1)S(1)} %get-tuple-element.24), channel_id=1, source_target_pairs={{0,2},{1,3},{2,0},{3,1},{4,6},{5,7},{6,4},{7,5},{8,10},{9,11},{10,... | collective-permute-start | bytes 589832 | tf_op jit(solution)/shard_map/ppermute | solution.py:19
  64.5 44.9 %collective-permute-start.12 = (bf16[192,1024]{1,0:T(8,128)(2,1)S(1)}, bf16[192,1024]{1,0:T(8,128)(2,1)S(1)}, u32[]{:S(2)}, u32[]{:S(2)}) collective-permute-start(bf16[192,1024]{1,0:T(8,128)(2,1)S(1)} %get-tuple-element.19), channel_id=1, source_target_pairs={{0,1},{1,0},{2,3},{3,2},{4,5},{5,4},{6,7},{7,6},{8,9},{9,8},{10,11... | collective-permute-start | bytes 1179656 | tf_op jit(solution)/shard_map/ppermute | solution.py:19
  64.5 25.5 %collective-permute-start.17 = (bf16[384,256]{1,0:T(8,128)(2,1)S(1)}, bf16[384,256]{1,0:T(8,128)(2,1)S(1)}, u32[]{:S(2)}, u32[]{:S(2)}) collective-permute-start(bf16[384,256]{1,0:T(8,128)(2,1)S(1)} %get-tuple-element.26), channel_id=1, source_target_pairs={{0,2},{1,3},{2,0},{3,1},{4,6},{5,7},{6,4},{7,5},{8,10},{9,11},{10,... | collective-permute-start | bytes 589832 | tf_op jit(solution)/shard_map/ppermute | solution.py:19
  66.4 29.2 %collective-permute-start.14 = (bf16[384,256]{1,0:T(8,128)(2,1)S(1)}, bf16[384,256]{1,0:T(8,128)(2,1)S(1)}, u32[]{:S(2)}, u32[]{:S(2)}) collective-permute-start(bf16[384,256]{1,0:T(8,128)(2,1)S(1)} %get-tuple-element.22), channel_id=1, source_target_pairs={{0,2},{1,3},{2,0},{3,1},{4,6},{5,7},{6,4},{7,5},{8,10},{9,11},{10,... | collective-permute-start | bytes 589832 | tf_op jit(solution)/shard_map/ppermute | solution.py:19
  66.6 28.8 %collective-permute-start.19 = (bf16[384,256]{1,0:T(8,128)(2,1)S(1)}, bf16[384,256]{1,0:T(8,128)(2,1)S(1)}, u32[]{:S(2)}, u32[]{:S(2)}) collective-permute-start(bf16[384,256]{1,0:T(8,128)(2,1)S(1)} %add_convert_fusion.1), channel_id=1, source_target_pairs={{0,4},{1,5},{2,6},{3,7},{4,0},{5,1},{6,2},{7,3},{8,12},{9,13},{10,... | collective-permute-start | bytes 589832 | tf_op jit(solution)/shard_map/ppermute | solution.py:19
  90.0 18.2 %collective-permute-start.16 = (bf16[384,256]{1,0:T(8,128)(2,1)S(1)}, bf16[384,256]{1,0:T(8,128)(2,1)S(1)}, u32[]{:S(2)}, u32[]{:S(2)}) collective-permute-start(bf16[384,256]{1,0:T(8,128)(2,1)S(1)} %add_convert_fusion.3), channel_id=1, source_target_pairs={{0,4},{1,5},{2,6},{3,7},{4,0},{5,1},{6,2},{7,3},{8,12},{9,13},{10,... | collective-permute-start | bytes 589832 | tf_op jit(solution)/shard_map/ppermute | solution.py:19
  95.4 33.4 %collective-permute-start.28 = (bf16[768,2048]{1,0:T(8,128)(2,1)S(1)}, bf16[768,2048]{1,0:T(8,128)(2,1)S(1)}, u32[]{:S(2)}, u32[]{:S(2)}) collective-permute-start(bf16[768,2048]{1,0:T(8,128)(2,1)S(1)} %pad_maximum_fusion), channel_id=1, source_target_pairs={{0,1},{1,0},{2,3},{3,2},{4,5},{5,4},{6,7},{7,6},{8,9},{9,8},{10,11... | collective-permute-start | bytes 9437192 | tf_op jit(solution)/shard_map/ppermute | solution.py:19
  95.6 19.9 %collective-permute-start.34 = (bf16[384,256]{1,0:T(8,128)(2,1)S(1)}, bf16[384,256]{1,0:T(8,128)(2,1)S(1)}, u32[]{:S(2)}, u32[]{:S(2)}) collective-permute-start(bf16[384,256]{1,0:T(8,128)(2,1)S(1)} %maximum_select_fusion.6), channel_id=1, source_target_pairs={{0,24},{8,16},{16,8},{24,0},{1,25},{9,17},{17,9},{25,1},{2,26},{10... | collective-permute-start | bytes 589832 | tf_op jit(solution)/shard_map/ppermute | solution.py:19
  108.2 15.7 %collective-permute-start.32 = (bf16[384,256]{1,0:T(8,128)(2,1)S(1)}, bf16[384,256]{1,0:T(8,128)(2,1)S(1)}, u32[]{:S(2)}, u32[]{:S(2)}) collective-permute-start(bf16[384,256]{1,0:T(8,128)(2,1)S(1)} %maximum_select_fusion.6), channel_id=1, source_target_pairs={{0,8},{8,0},{16,24},{24,16},{1,9},{9,1},{17,25},{25,17},{2,10},{10... | collective-permute-start | bytes 589832 | tf_op jit(solution)/shard_map/ppermute | solution.py:19
  110.8 12.0 %collective-permute-start.33 = (bf16[384,256]{1,0:T(8,128)(2,1)S(1)}, bf16[384,256]{1,0:T(8,128)(2,1)S(1)}, u32[]{:S(2)}, u32[]{:S(2)}) collective-permute-start(bf16[384,256]{1,0:T(8,128)(2,1)S(1)} %maximum_select_fusion.6), channel_id=1, source_target_pairs={{0,16},{8,24},{16,0},{24,8},{1,17},{9,25},{17,1},{25,9},{2,18},{10... | collective-permute-start | bytes 589832 | tf_op jit(solution)/shard_map/ppermute | solution.py:19
  113.7 10.2 %collective-permute-start.27 = (bf16[384,256]{1,0:T(8,128)(2,1)S(1)}, bf16[384,256]{1,0:T(8,128)(2,1)S(1)}, u32[]{:S(2)}, u32[]{:S(2)}) collective-permute-start(bf16[384,256]{1,0:T(8,128)(2,1)S(1)} %maximum_select_fusion.5), channel_id=1, source_target_pairs={{0,24},{8,16},{16,8},{24,0},{1,25},{9,17},{17,9},{25,1},{2,26},{10... | collective-permute-start | bytes 589832 | tf_op jit(solution)/shard_map/ppermute | solution.py:19
  115.5 11.0 %collective-permute-start.26 = (bf16[384,256]{1,0:T(8,128)(2,1)S(1)}, bf16[384,256]{1,0:T(8,128)(2,1)S(1)}, u32[]{:S(2)}, u32[]{:S(2)}) collective-permute-start(bf16[384,256]{1,0:T(8,128)(2,1)S(1)} %maximum_select_fusion.5), channel_id=1, source_target_pairs={{0,16},{8,24},{16,0},{24,8},{1,17},{9,25},{17,1},{25,9},{2,18},{10... | collective-permute-start | bytes 589832 | tf_op jit(solution)/shard_map/ppermute | solution.py:19
  131.0 12.1 %collective-permute-start.36 = (bf16[512,256]{1,0:T(8,128)(2,1)S(1)}, bf16[512,256]{1,0:T(8,128)(2,1)S(1)}, u32[]{:S(2)}, u32[]{:S(2)}) collective-permute-start(bf16[512,256]{1,0:T(8,128)(2,1)S(1)} %get-tuple-element.40), channel_id=1, source_target_pairs={{0,2},{1,3},{2,0},{3,1},{4,6},{5,7},{6,4},{7,5},{8,10},{9,11},{10,... | collective-permute-start | bytes 786440 | tf_op jit(solution)/shard_map/ppermute | solution.py:19
  131.1 29.9 %collective-permute-start.35 = (bf16[512,256]{1,0:T(8,128)(2,1)S(1)}, bf16[512,256]{1,0:T(8,128)(2,1)S(1)}, u32[]{:S(2)}, u32[]{:S(2)}) collective-permute-start(bf16[512,256]{1,0:T(8,128)(2,1)S(1)} %get-tuple-element.39), channel_id=1, source_target_pairs={{0,2},{1,3},{2,0},{3,1},{4,6},{5,7},{6,4},{7,5},{8,10},{9,11},{10,... | collective-permute-start | bytes 786440 | tf_op jit(solution)/shard_map/ppermute | solution.py:19
  135.2 24.7 %collective-permute-start.30 = (bf16[512,256]{1,0:T(8,128)(2,1)S(1)}, bf16[512,256]{1,0:T(8,128)(2,1)S(1)}, u32[]{:S(2)}, u32[]{:S(2)}) collective-permute-start(bf16[512,256]{1,0:T(8,128)(2,1)S(1)} %get-tuple-element.38), channel_id=1, source_target_pairs={{0,2},{1,3},{2,0},{3,1},{4,6},{5,7},{6,4},{7,5},{8,10},{9,11},{10,... | collective-permute-start | bytes 786440 | tf_op jit(solution)/shard_map/ppermute | solution.py:19
  143.2 17.8 %collective-permute-start.37 = (bf16[512,256]{1,0:T(8,128)(2,1)S(1)}, bf16[512,256]{1,0:T(8,128)(2,1)S(1)}, u32[]{:S(2)}, u32[]{:S(2)}) collective-permute-start(bf16[512,256]{1,0:T(8,128)(2,1)S(1)} %fusion.2), channel_id=1, source_target_pairs={{0,4},{1,5},{2,6},{3,7},{4,0},{5,1},{6,2},{7,3},{8,12},{9,13},{10,... | collective-permute-start | bytes 786440 | tf_op jit(solution)/shard_map/ppermute | solution.py:19
  144.8 18.1 %collective-permute-start.29 = (bf16[512,256]{1,0:T(8,128)(2,1)S(1)}, bf16[512,256]{1,0:T(8,128)(2,1)S(1)}, u32[]{:S(2)}, u32[]{:S(2)}) collective-permute-start(bf16[512,256]{1,0:T(8,128)(2,1)S(1)} %get-tuple-element.37), channel_id=1, source_target_pairs={{0,2},{1,3},{2,0},{3,1},{4,6},{5,7},{6,4},{7,5},{8,10},{9,11},{10,... | collective-permute-start | bytes 786440 | tf_op jit(solution)/shard_map/ppermute | solution.py:19
  160.0 10.0 %collective-permute-start.31 = (bf16[512,256]{1,0:T(8,128)(2,1)S(1)}, bf16[512,256]{1,0:T(8,128)(2,1)S(1)}, u32[]{:S(2)}, u32[]{:S(2)}) collective-permute-start(bf16[512,256]{1,0:T(8,128)(2,1)S(1)} %fusion.4), channel_id=1, source_target_pairs={{0,4},{1,5},{2,6},{3,7},{4,0},{5,1},{6,2},{7,3},{8,12},{9,13},{10,... | collective-permute-start | bytes 786440 | tf_op jit(solution)/shard_map/ppermute | solution.py:19
  (13 other events, 140.7 us)

commit v2 on v1

v2 whole, which is shorter than its diff:
```python
import functools
import math

import jax
import jax.numpy as jnp
from jax import lax
from jax.experimental import pallas as pl
from jax.experimental.pallas import tpu as pltpu
from jax.sharding import PartitionSpec as P

HD = 128
PAIR = 2
VMEM_BYTES = 60 << 20
UNIT, LANES, KEYS, WIDE = 4, 256, 128, 768
F32, BF16 = jnp.float32, jnp.bfloat16
NT = (((1,), (1,)), ((), ()))
TN = (((0,), (0,)), ((), ()))


def xor_permute(array, axis, size, mask):
    return lax.ppermute(array, axis, [(i, i ^ mask) for i in range(size)])


def attention_kernel(
    chips, tok, group, head, units, packing, layout, pos_ref, q_own, g_own, qg_rx, *refs
):
    n_in = len(packing)
    kv_in = refs[:n_in]
    dq_own, dq_oth = refs[n_in : n_in + 2]
    dkv_out = refs[n_in + 2 : n_in + 2 + len(layout)]
    qs, gs, kv, kt, acc, es, ds, ms, dqa, dqs, own_block, sent_blocks, sems, out_sems = refs[n_in + 2 + len(layout) :]
    span = PAIR * tok
    rows = UNIT * span
    width = group * HD
    chip, core = pos_ref[0], pos_ref[1]
    heads = q_own.shape[1] // (PAIR * width)
    col = pl.multiple_of((core * heads + head) * width, width)
    own = pl.multiple_of(core * tok, tok)
    oth = pl.multiple_of((1 - core) * tok, tok)
    copies = [
        (q_own.at[:, pl.ds(col, width)], qs.at[pl.ds(own, tok)]),
        (qg_rx.at[:, pl.ds(0, width)], qs.at[pl.ds(oth, tok)]),
        (g_own.at[:, pl.ds(col, width)], gs.at[pl.ds(own, tok)]),
        (qg_rx.at[:, pl.ds(width, width)], gs.at[pl.ds(oth, tok)]),
    ]
    for ref, (slots, lo) in zip(kv_in, packing):
        for i, s in enumerate(slots):
            copies.append((ref.at[pl.ds(i * span, span), pl.ds(lo, 2 * HD)], kv.at[chip ^ s]))
    started = [pltpu.make_async_copy(a, b, sems.at[i]) for i, (a, b) in enumerate(copies)]
    for c in started:
        c.start()
    acc[...] = jnp.zeros_like(acc)
    for c in started:
        c.wait()
    scale = 1.0 / math.sqrt(HD)
    log_scale = scale * math.log2(math.e)

    def turn(j, _):
        kt[j] = kv[j, :, :HD].T
        return 0

    lax.fori_loop(0, chip + 1, turn, 0)

    def columns_of(u):
        return pl.ds(pl.multiple_of(u * UNIT * HD, UNIT * HD), UNIT * HD)

    def stacked(ref, u):
        wide = ref[:, columns_of(u)]
        return jnp.concatenate([wide[:, i * HD : (i + 1) * HD] for i in range(UNIT)], 0)

    def unit(u, _):
        q = stacked(qs, u)
        g = stacked(gs, u)
        qt, gt = q.T, g.T

        def scores(j, carry, masked):
            out = []
            for t, lane in enumerate(range(0, rows, LANES)):
                top, total, weighted = carry[t]
                for i, key in enumerate(range(0, span, KEYS)):
                    s = lax.dot_general(
                        kv[j, key : key + KEYS, :HD],
                        q[lane : lane + LANES],
                        NT,
                        preferred_element_type=F32,
                    ) * log_scale
                    if masked:
                        key_ids = lax.broadcasted_iota(jnp.int32, s.shape, 0) + key
                        row_ids = lax.broadcasted_iota(jnp.int32, s.shape, 1) + lane % span
                        row_ids = jnp.where(row_ids >= span, row_ids - span, row_ids)
                        s = jnp.where(key_ids <= row_ids, s, -jnp.inf)
                    dp = lax.dot_general(
                        kv[j, key : key + KEYS, HD:],
                        g[lane : lane + LANES],
                        NT,
                        preferred_element_type=F32,
                    )
                    new = jnp.maximum(top, jnp.max(s, axis=0, keepdims=True))
                    e = jnp.exp2(s - new)
                    fade = jnp.exp2(top - new)
                    es[j, key : key + KEYS, lane : lane + LANES] = e
                    ds[j, key : key + KEYS, lane : lane + LANES] = dp
                    ms[j, i : i + 1, lane : lane + LANES] = new
                    total = total * fade + jnp.sum(e, axis=0, keepdims=True)
                    weighted = weighted * fade + jnp.sum(e * dp, axis=0, keepdims=True)
                    top = new
                out.append((top, total, weighted))
            return tuple(out)

        zero = jnp.zeros((1, LANES), F32)
        start = (jnp.full((1, LANES), -jnp.inf, F32), zero, zero)
        carry = scores(chip, (start,) * (rows // LANES), True)
        carry = lax.fori_loop(0, chip, lambda j, c: scores(j, c, False), carry)
        top, total, weighted = (jnp.concatenate(x, 1) for x in zip(*carry))
        inv = 1.0 / total
        delta = weighted * inv
        dqa[...] = jnp.zeros_like(dqa)

        def grads(j, _):
            for lane in range(0, rows, WIDE):
                at = slice(lane, lane + WIDE)
                ps, sgs = [], []
                for i, key in enumerate(range(0, span, KEYS)):
                    keys = slice(key, key + KEYS)
                    part = jnp.exp2(ms[j, i : i + 1, at] - top[:, at]) * inv[:, at]
                    p = es[j, keys, at] * part
                    ps.append(p.astype(BF16))
                    sgs.append((p * (ds[j, keys, at] - delta[:, at])).astype(BF16))
                p, sg = jnp.concatenate(ps, 0), jnp.concatenate(sgs, 0)
                acc[j, HD:] += lax.dot_general(gt[:, at], p, NT, preferred_element_type=F32)
                acc[j, :HD] += lax.dot_general(qt[:, at], sg, NT, preferred_element_type=F32)
                dqa[:, at] += jnp.dot(kt[j], sg, preferred_element_type=F32)
            return 0

        lax.fori_loop(0, chip + 1, grads, 0)
        out = (dqa[...] * scale).T.astype(BF16)
        dqs[:, columns_of(u)] = jnp.concatenate(
            [out[i * span : (i + 1) * span] for i in range(UNIT)], 1
        )
        for copy in query_copies(u):
            copy.start()
        return 0

    def query_copies(u):
        return [
            pltpu.make_async_copy(
                dqs.at[pl.ds(row, tok), columns_of(u)], ref.at[:, columns_of(u)], out_sems.at[i, u]
            )
            for i, (ref, row) in enumerate(((dq_own, own), (dq_oth, oth)))
        ]

    lax.fori_loop(0, units, unit, 0)
    leaving = [copy for u in range(units) for copy in query_copies(u)]
    starts, place = {(0,): 0}, 0
    for group_slots, _, _ in layout:
        if group_slots not in starts:
            starts[group_slots] = place
            place += len(group_slots) * span
    for n, (out, (group_slots, lo, hi)) in enumerate(zip(dkv_out, layout)):
        held = (own_block if group_slots == (0,) else sent_blocks).at[:, pl.ds(lo, hi - lo)]
        first_row = starts[group_slots]
        for i, s in enumerate(group_slots):
            j = chip ^ s
            part = pl.ds(first_row + i * span, span)

            @pl.when(j <= chip)
            def _():
                for half in range(lo, hi, HD):
                    cell = acc[j, half : half + HD]
                    cell = cell * scale if half == 0 else cell
                    held[part, half - lo : half - lo + HD] = cell.T.astype(held.dtype)

            @pl.when(j > chip)
            def _():
                held[part, :] = jnp.zeros((span, hi - lo), held.dtype)

        copy = pltpu.make_async_copy(
            held.at[pl.ds(first_row, len(group_slots) * span)], out, out_sems.at[2, n]
        )
        copy.start()
        leaving.append(copy)
    for copy in leaving:
        copy.wait()


def attention(pos, q_own, g_own, qg_rx, kv_parts, packing, head, direct):
    chips = sum(len(slots) for slots, _ in packing)
    width = qg_rx.shape[1] // 2
    tok = qg_rx.shape[0]
    span = PAIR * tok
    group = width // HD
    rows = UNIT * span
    if direct:
        layout = tuple(((s,), 0, 2 * HD) for s in range(chips))
    else:
        groups = [(0,)] + by_lowest_bit(chips)
        layout = tuple((slots, lo, lo + HD) for lo in (HD, 0) for slots in groups)
    hbm = pl.BlockSpec(memory_space=pltpu.HBM)
    out_shape = [jax.ShapeDtypeStruct((tok, width), BF16)] * 2 + [
        jax.ShapeDtypeStruct((len(slots) * span, hi - lo), F32 if slots == (0,) else BF16)
        for slots, lo, hi in layout
    ]
    inputs = [q_own, g_own, qg_rx, *kv_parts]
    outs = pl.pallas_call(
        functools.partial(
            attention_kernel, chips, tok, group, head, group // UNIT, packing, layout
        ),
        out_shape=out_shape,
        in_specs=[pl.BlockSpec(memory_space=pltpu.SMEM)] + [hbm] * len(inputs),
        out_specs=[hbm] * len(out_shape),
        scratch_shapes=[
            pltpu.VMEM((span, width), BF16),
            pltpu.VMEM((span, width), BF16),
            pltpu.VMEM((chips, span, 2 * HD), BF16),
            pltpu.VMEM((chips, HD, span), BF16),
            pltpu.VMEM((chips, 2 * HD, span), F32),
            pltpu.VMEM((chips, span, rows), F32),
            pltpu.VMEM((chips, span, rows), F32),
            pltpu.VMEM((chips, span // KEYS, rows), F32),
            pltpu.VMEM((HD, rows), F32),
            pltpu.VMEM((span, width), BF16),
            pltpu.VMEM((span, 2 * HD), F32),
            pltpu.VMEM(((chips - 1) * span, 2 * HD), BF16),
            pltpu.SemaphoreType.DMA((4 + chips,)),
            pltpu.SemaphoreType.DMA((3, max(len(layout), group // UNIT))),
        ],
        compiler_params=pltpu.CompilerParams(vmem_limit_bytes=VMEM_BYTES),
        cost_estimate=pl.CostEstimate(
            flops=400 * group * span * chips * span * HD, bytes_accessed=6 * span * width, transcendentals=0
        ),
        name="attention_grads",
    )(pos, *inputs)
    return outs


def product_kernel(chips, n_dp, tok, order, pos_ref, *refs):
    slots, halves, outs = refs[:n_dp], refs[n_dp : n_dp + PAIR], refs[n_dp + PAIR : -4]
    kvs, turned, held, sems = refs[-4:]
    depth = n_dp * tok
    block = held.shape[2]
    flat = [s for group in order for s in group]
    copies = []
    for i, s in enumerate(flat):
        columns = pl.ds(pl.multiple_of((pos_ref[0] ^ s) * block, block), block)
        for at, half in enumerate(halves):
            copy = pltpu.make_async_copy(
                half.at[:, columns], held.at[i, pl.ds(at * depth, depth)], sems.at[i, at]
            )
            copy.start()
            copies.append(copy)
    for s in range(n_dp):
        kvs[pos_ref[1] ^ s] = slots[s][...]
    for at in range(PAIR):
        rows = kvs[:, at * tok : (at + 1) * tok]
        turned[:, at * depth : (at + 1) * depth] = rows.reshape(depth, rows.shape[2]).T
    i = 0
    for out, group in zip(outs, order):
        for at in range(len(group)):
            for copy in copies[i * PAIR : (i + 1) * PAIR]:
                copy.wait()
            both = jnp.dot(turned[...], held[i], preferred_element_type=F32)
            out[at * block : (at + 1) * block] = both.T.astype(out.dtype)
            i += 1


def weight_products(pos, slots, hidden_own, hidden_oth, chips):
    n_dp = len(slots)
    span, wide = slots[0].shape
    depth, share = hidden_own.shape
    block = share // chips
    order = by_lowest_bit(chips) + [(0,)]
    vmem = pl.BlockSpec(memory_space=pltpu.VMEM)
    outs = pl.pallas_call(
        functools.partial(product_kernel, chips, n_dp, span // PAIR, order),
        in_specs=[pl.BlockSpec(memory_space=pltpu.SMEM)]
        + [vmem] * n_dp
        + [pl.BlockSpec(memory_space=pltpu.HBM)] * PAIR,
        out_specs=[pl.BlockSpec()] * len(order),
        out_shape=[
            jax.ShapeDtypeStruct((len(group) * block, wide), F32 if group == (0,) else BF16)
            for group in order
        ],
        scratch_shapes=[
            pltpu.VMEM((n_dp, span, wide), BF16),
            pltpu.VMEM((wide, PAIR * depth), BF16),
            pltpu.VMEM((chips, PAIR * depth, block), BF16),
            pltpu.SemaphoreType.DMA((chips, PAIR)),
        ],
        compiler_params=pltpu.CompilerParams(
            vmem_limit_bytes=VMEM_BYTES
        ),
        cost_estimate=pl.CostEstimate(flops=1, bytes_accessed=1, transcendentals=0),
        name="weight_products",
    )(pos, *slots, hidden_own, hidden_oth)
    return outs[-1], list(outs[:-1])


def by_lowest_bit(chips):
    bits = chips.bit_length() - 1
    return [tuple(s for s in range(1, chips) if s & -s == 1 << i) for i in range(bits)]


def on_device(queries, keys, values, out_grad, hidden):
    tok = queries.shape[0]
    n_dp, n_ctx = lax.axis_size("dp"), lax.axis_size("ctx")
    chips = n_ctx // PAIR
    kv_heads = keys.shape[1] // HD
    own_heads = kv_heads // PAIR
    width = queries.shape[1] // kv_heads
    dp, ctx = lax.axis_index("dp"), lax.axis_index("ctx")
    chip, core = ctx // PAIR, ctx % PAIR
    pos = jnp.stack([chip, core]).astype(jnp.int32)
    place = jnp.stack([chip, dp]).astype(jnp.int32)
    first = core == 0

    def swap(x):
        return xor_permute(x, "ctx", n_ctx, 1)

    def across(x, mask):
        return xor_permute(x, "ctx", n_ctx, mask * PAIR)

    def in_order(mine, theirs, axis):
        return jnp.where(
            first,
            jnp.concatenate([mine, theirs], axis),
            jnp.concatenate([theirs, mine], axis),
        )

    def columns(x, head, size):
        return lax.dynamic_slice_in_dim(x, head * size, size, 1)

    def after(x, *others):
        return lax.optimization_barrier((x, others))[0]

    def both_kv(owner):
        return jnp.concatenate(
            [columns(x, owner * own_heads + a, HD) for a in range(own_heads) for x in (keys, values)], 1
        )

    def rows_for_pair(a, queries, out_grad):
        theirs = (1 - core) * own_heads + a
        return jnp.concatenate([columns(queries, theirs, width), columns(out_grad, theirs, width)], 1)

    lowest = by_lowest_bit(chips)

    def own_first(total):
        return jnp.where(first, total, jnp.concatenate([total[tok:], total[:tok]], 0))

    def over_sequences(total):
        return [total] + [xor_permute(total, "dp", n_dp, s) for s in range(1, n_dp)]

    def product_blocks(slots, *gate):
        return weight_products(place, after(slots, *gate), hidden_own, hidden_oth, chips)

    def core_rows(summed):
        rows = share // n_ctx
        mine = lax.dynamic_slice_in_dim(summed, core * rows, rows, 0)
        theirs = lax.dynamic_slice_in_dim(summed, (1 - core) * rows, rows, 0)
        return mine, swap(theirs)

    def step(kept, groups, i, *gate):
        groups = list(groups)
        got = after(across(groups[i].astype(BF16), 1 << i), *gate)
        size = got.shape[0] // len(lowest[i])
        for at, s in enumerate(lowest[i]):
            piece = got[at * size : (at + 1) * size].astype(F32)
            to = s ^ (1 << i)
            if to == 0:
                kept = kept + piece
            else:
                g = next(g for g in range(len(lowest)) if to in lowest[g])
                at_to = lowest[g].index(to) * size
                pieces = [groups[g][:at_to], groups[g][at_to : at_to + size].astype(F32) + piece, groups[g][at_to + size :]]
                groups[g] = jnp.concatenate([x.astype(BF16) for x in pieces if x.shape[0]], 0)
        return kept, groups

    share = hidden.shape[1] // n_dp
    bits = len(lowest)

    kept, got = both_kv(core), swap(both_kv(1 - core))
    wide = 2 * HD
    kv_local = [in_order(kept[:, i * wide : (i + 1) * wide], got[:, i * wide : (i + 1) * wide], 0) for i in range(own_heads)]

    def doubling(slots, bits, *gate):
        for bit in bits:
            slots = slots | {s ^ bit: across(after(x, *gate), bit) for s, x in slots.items()}
        return slots

    far_first = [1 << i for i in reversed(range(bits))]
    queries_, out_grad_, hidden_ = after((queries, out_grad, hidden), kv_local)
    rx, rx1 = rows_for_pair(0, queries_, out_grad_), rows_for_pair(1, queries_, out_grad_)
    shares = hidden_.reshape(tok, n_dp, share).transpose(1, 0, 2)
    slots = doubling({0: kv_local[0]}, far_first[:-1])
    near = across(kv_local[0], 1)
    forward = {s: after(slots[s], rx, rx1, shares) for s in range(2, chips, 2)}
    slots |= {1: near} | {s ^ 1: across(x, 1) for s, x in forward.items()}
    rx, rx1 = swap(rx), swap(rx1)
    hidden_own = lax.all_to_all(shares, "dp", split_axis=0, concat_axis=0, tiled=True)
    hidden_own = hidden_own.reshape(n_dp * tok, share)
    parts = [slots[s] for s in range(chips)]
    packing = tuple(((s,), 0) for s in range(chips))
    local1 = after(kv_local[1], parts)
    parts1 = [local1] + [across(local1, s) for s in range(1, chips)]
    dq_own, dq_oth, *blocks = attention(
        pos, queries, out_grad, rx, parts, packing, 0, True
    )

    moved = [blocks[0]] + [across(blocks[s], s) for s in range(1, chips)]
    rx1, parts1 = after((rx1, parts1), blocks)
    dq_own1, dq_oth1, *blocks1 = attention(
        pos, queries, out_grad, rx1, parts1, packing, 1, False
    )
    one = sum(x.astype(F32) for x in after(moved, blocks1))
    hidden_own, dq_oth = after((hidden_own, dq_oth), one)
    hidden_oth = swap(hidden_own)

    total = own_first(one.astype(BF16))
    slots = over_sequences(total)
    size = 1 + len(lowest)
    value, key = ((blocks1[i], blocks1[i + 1 : i + size]) for i in (0, size))
    for i in range(bits - 1):
        value = step(*value, i)
        key = step(*key, i, value)
    product = product_blocks(slots, key)
    value = step(*value, bits - 1, product)
    total_v = own_first(value[0].astype(BF16))
    slots_v = over_sequences(total_v)
    key = step(*key, bits - 1, total_v)
    total_k = own_first(key[0].astype(BF16))
    slots_k = over_sequences(total_k)
    product_v = product_blocks(slots_v, total_k)
    for i in range(bits - 1):
        product = step(*product, i, product_v)
    product_k = product_blocks(slots_k, product)
    total, total_v, total_k, dq_oth, dq_oth1 = after(
        (total, total_v, total_k, dq_oth, dq_oth1), product_k[0]
    )
    for i in range(bits - 1):
        product_v = step(*product_v, i, product_k)
    product = step(*product, bits - 1, product_v)
    for i in range(bits - 1):
        product_k = step(*product_k, i, product)
    product_v = step(*product_v, bits - 1, product_k)
    product_k = step(*product_k, bits - 1, product_v)
    w_first, w_value, w_key = (core_rows(x[0]) for x in (product, product_v, product_k))
    both = swap(jnp.concatenate([total[tok:], total_k[tok:], total_v[tok:]], 1))
    wide = 2 * HD
    kv_first = total[:tok], both[:, :wide]
    kv_key = total_k[:tok], both[:, wide : wide + HD]
    kv_value = total_v[:tok], both[:, wide + HD :]

    def spread(one, two, lo):
        return in_order(*(jnp.concatenate([x[:, lo : lo + HD], y], 1) for x, y in zip(one, two)), 1)

    return (
        in_order(
            jnp.concatenate([dq_own, dq_own1], 1),
            swap(jnp.concatenate([dq_oth, dq_oth1], 1)),
            1,
        ),
        spread(kv_first, kv_key, 0),
        spread(kv_first, kv_value, HD),
        spread(w_first, w_key, 0),
        spread(w_first, w_value, HD),
    )


def solution(mesh):
    spec = P(("dp", "ctx"), None)
    return jax.shard_map(
        on_device, mesh=mesh, in_specs=(spec,) * 5, out_specs=(spec,) * 5, check_vma=False
    )
```

time: 174 us -> 156 us (0.90)
  waiting for transfers between devices: 71.7 us -> 24.7 us
  Pallas kernels: 14.5 us -> 33.7 us
  other arithmetic: 5.67 us -> 13.1 us
  starting transfers between devices: 68.1 us -> 72.8 us
  matrix products: 4.19 us -> 0 us
    ppermute x40 -> x37, waiting for transfers between devices: 71.7 us -> 24.7 us  [xor_permute(): return lax.ppermute(array, axis, [(i, i ^ mask) for i in range(size)])]
    pallas_call x0 -> x3, Pallas kernels: none -> 16.6 us  [weight_products(): pl.pallas_call(functools.partial(product_kernel, chips, n_dp, span // PAI...]
    dynamic_slice x4 -> x3, local copies, waits for them, and re-layouts: 7.76 us -> 1.25 us  [columns(): return lax.dynamic_slice_in_dim(x, head * size, size, 1)]
    unnamed x10 -> x74, local copies, waits for them, and re-layouts: 0.02 us -> 5.42 us
    all_to_all x0 -> x1, starting transfers between devices: none -> 4.66 us  [on_device(): lax.all_to_all(shares, 'dp', split_axis=0, concat_axis=0, tiled=True)]
    dot_general x4 -> x0, matrix products: 4.19 us -> none  [the longest x2 2.16 us: on_device(): lax.dot_general(hidden_own, kv_own, TN, preferred_element_type=F32)]
    convert_element_type x6 -> x7, other arithmetic: 0.36 us -> 3.77 us  [the longest x5 1.94 us: step(): x.astype(BF16)]
    pallas_call x2, Pallas kernels: 14.5 us -> 17.1 us  [attention(): pl.pallas_call(functools.partial(attention_kernel, chips, tok, group, hea...]
  transfers between devices with their start and end apart: 40 -> 38, of which waited for: 15 -> 10; matrix products, arithmetic and copies ran while one was open for 7% -> 8% of each run, Pallas kernels for 8% -> 22%
where the time goes in v2:
time: 156 us
  starting transfers between devices  72.8 us (47%)
  Pallas kernels  33.7 us (22%)
  waiting for transfers between devices  24.7 us (16%)
  other arithmetic  13.1 us (8%)
  local copies, waits for them, and re-layouts  9.9 us (6%)
    ppermute x37, starting transfers between devices, xor_permute(): return lax.ppermute(array, axis, [(i, i ^ mask) for i in range(size)])  68.1 us
    ppermute x37, waiting for transfers between devices, xor_permute(): return lax.ppermute(array, axis, [(i, i ^ mask) for i in range(size)])  24.7 us
    pallas_call x2, Pallas kernels, attention(): pl.pallas_call(functools.partial(attention_kernel, chips, tok, group, hea...  17.1 us
    pallas_call x3, Pallas kernels, weight_products(): pl.pallas_call(functools.partial(product_kernel, chips, n_dp, span // PAI...  16.6 us
    select_n x7, other arithmetic, in_order(): jnp.where(first, jnp.concatenate([mine, theirs], axis), jnp.concatenate([...  5.66 us
    unnamed x74, local copies, waits for them, and re-layouts  5.42 us
    all_to_all x1, starting transfers between devices, on_device(): lax.all_to_all(shares, 'dp', split_axis=0, concat_axis=0, tiled=True)  4.66 us
  transfers between devices with their start and end apart: 38, of which 10 were waited for; matrix products, arithmetic and copies ran while one was open for 8% of the time, Pallas kernels for 22%

profile of v2, /device:TPU:0, one launch (start us, length us, event | category | flops | bytes accessed | tf_op | source)
XLA Modules:
  0.0 155.6 jit_solution(2225447384183670618)
XLA Ops:
  6.0 2.7 %collective-permute-start.2 = (bf16[384,256]{1,0:T(8,128)(2,1)S(1)}, bf16[384,256]{1,0:T(8,128)(2,1)S(1)}, u32[]{:S(2)}, u32[]{:S(2)}) collective-permute-start(bf16[384,256]{1,0:T(8,128)(2,1)S(1)} %maximum_select_fusion.3.refs_0_), channel_id=1, source_target_pairs={{0,2},{1,3},{2,0},{3,1},{4,6},{5,7},{6,4},{7,5},{8,10},{9,11},{10,... | collective-permute-start | bytes 589832 | tf_op jit(solution)/shard_map/ppermute | solution.py:21
  8.8 2.1 %copy.13 = bf16[24,4,8,2048]{3,2,0,1:T(8,128)(2,1)} copy(bf16[24,4,8,2048]{3,2,1,0:T(8,128)(2,1)S(1)} %bitcast.11) | data formatting | bytes 6291456 | tf_op jit(solution)/shard_map/reshape | solution.py:392
  10.9 2.6 %collective-permute-start.3 = (bf16[384,256]{1,0:T(8,128)(2,1)S(1)}, bf16[384,256]{1,0:T(8,128)(2,1)S(1)}, u32[]{:S(2)}, u32[]{:S(2)}) collective-permute-start(bf16[384,256]{1,0:T(8,128)(2,1)S(1)} %maximum_select_fusion.3.refs_0_), channel_id=1, source_target_pairs={{0,4},{1,5},{2,6},{3,7},{4,0},{5,1},{6,2},{7,3},{8,12},{9,13},{10,... | collective-permute-start | bytes 589832 | tf_op jit(solution)/shard_map/ppermute | solution.py:21
  14.4 8.5 %collective-permute-done.3.refs_2_ = bf16[384,256]{1,0:T(8,128)(2,1)S(1)} collective-permute-done((bf16[384,256]{1,0:T(8,128)(2,1)S(1)}, bf16[384,256]{1,0:T(8,128)(2,1)S(1)}, u32[]{:S(2)}, u32[]{:S(2)}) %collective-permute-start.3) | collective-permute-done | bytes 196640 | tf_op jit(solution)/shard_map/ppermute | solution.py:21
  24.1 4.7 %all-to-all-start = ((bf16[4,192,2048]{2,1,0:T(8,128)(2,1)}), bf16[4,192,2048]{2,1,0:T(8,128)(2,1)}, u32[]{:S(2)}, u32[]{:S(2)}) async-start(bf16[4,192,2048]{2,1,0:T(8,128)(2,1)} %bitcast.10), calls=%async_computation | async-start | bytes 6291456 | tf_op jit(solution)/shard_map/all_to_all | solution.py:398
  28.9 1.5 collective-permute-start.6
  30.4 3.4 %collective-permute-start.7 = (bf16[384,256]{1,0:T(8,128)(2,1)}, bf16[384,256]{1,0:T(8,128)(2,1)}, u32[]{:S(2)}, u32[]{:S(2)}) collective-permute-start(bf16[384,256]{1,0:T(8,128)(2,1)} %maximum_select_fusion.4.refs_0_), channel_id=1, source_target_pairs={{0,4},{1,5},{2,6},{3,7},{4,0},{5,1},{6,2},{7,3},{8,12},{9,13},{10,... | collective-permute-start | bytes 589832 | tf_op jit(solution)/shard_map/ppermute | solution.py:21
  34.7 8.4 %attention_grads.2 = (bf16[192,1024]{1,0:T(8,128)(2,1)}, bf16[192,1024]{1,0:T(8,128)(2,1)}, f32[384,256]{1,0:T(8,128)}, bf16[384,256]{1,0:T(8,128)(2,1)}, bf16[3...) custom-call(s32[2]{0:T(128)} %pad_add_fusion.pos_ref, bf16[192,4096]{1,0:T(8,128)(2,1)} %q_own.3, bf16[192,4096]{1,0:T(8,128)(2,1)} %g_own.3, ...), custom_call_target="tpu_custom_call" | custom-call | flops 241591910400 | bytes 2359296 | tf_op jit(solution)/shard_map/attention_grads/pallas_call | solution.py:204
  43.2 10.3 %collective-permute-start.10 = (bf16[384,256]{1,0:T(8,128)(2,1)}, bf16[384,256]{1,0:T(8,128)(2,1)}, u32[]{:S(2)}, u32[]{:S(2)}) collective-permute-start(bf16[384,256]{1,0:T(8,128)(2,1)} %get-tuple-element.78), channel_id=1, source_target_pairs={{0,4},{1,5},{2,6},{3,7},{4,0},{5,1},{6,2},{7,3},{8,12},{9,13},{10,... | collective-permute-start | bytes 589832 | tf_op jit(solution)/shard_map/ppermute | solution.py:21
  53.5 6.1 %collective-permute-start.11 = (bf16[384,256]{1,0:T(8,128)(2,1)}, bf16[384,256]{1,0:T(8,128)(2,1)}, u32[]{:S(2)}, u32[]{:S(2)}) collective-permute-start(bf16[384,256]{1,0:T(8,128)(2,1)} %get-tuple-element.79), channel_id=1, source_target_pairs={{0,6},{1,7},{2,4},{3,5},{4,2},{5,3},{6,0},{7,1},{8,14},{9,15},{10,... | collective-permute-start | bytes 589832 | tf_op jit(solution)/shard_map/ppermute | solution.py:21
  60.1 8.7 %attention_grads.3 = (bf16[192,1024]{1,0:T(8,128)(2,1)}, bf16[192,1024]{1,0:T(8,128)(2,1)}, f32[384,128]{1,0:T(8,128)}, bf16[768,128]{1,0:T(8,128)(2,1)}, bf16[3...) custom-call(s32[2]{0:T(128)} %pad_add_fusion.pos_ref, ...), custom_call_target="tpu_custom_call" | custom-call | flops 241591910400 | bytes 2359296 | tf_op jit(solution)/shard_map/attention_grads/pallas_call | solution.py:204
  71.7 4.8 %collective-permute-start.12 = (bf16[768,128]{1,0:T(8,128)(2,1)}, bf16[768,128]{1,0:T(8,128)(2,1)S(1)}, u32[]{:S(2)}, u32[]{:S(2)}) collective-permute-start(bf16[768,128]{1,0:T(8,128)(2,1)} %get-tuple-element.87), channel_id=1, source_target_pairs={{0,2},{1,3},{2,0},{3,1},{4,6},{5,7},{6,4},{7,5},{8,10},{9,11},{10,... | collective-permute-start | bytes 589832 | tf_op jit(solution)/shard_map/ppermute | solution.py:21
  76.6 1.6 %collective-permute-start.14 = (bf16[384,256]{1,0:T(8,128)(2,1)S(1)}, bf16[384,256]{1,0:T(8,128)(2,1)S(1)}, u32[]{:S(2)}, u32[]{:S(2)}) collective-permute-start(bf16[384,256]{1,0:T(8,128)(2,1)S(1)} %maximum_select_fusion.5.refs_0_), channel_id=1, source_target_pairs={{0,8},{8,0},{16,24},{24,16},{1,9},{9,1},{17,25},{25,17},{2,10},{10... | collective-permute-start | bytes 589832 | tf_op jit(solution)/shard_map/ppermute | solution.py:21
  78.2 1.5 collective-permute-start.15
  79.7 2.8 %collective-permute-done.12 = bf16[768,128]{1,0:T(8,128)(2,1)S(1)} collective-permute-done((bf16[768,128]{1,0:T(8,128)(2,1)}, bf16[768,128]{1,0:T(8,128)(2,1)S(1)}, u32[]{:S(2)}, u32[]{:S(2)}) %collective-permute-start.12) | collective-permute-done | bytes 196640 | tf_op jit(solution)/shard_map/ppermute | solution.py:21
  82.4 2.5 %collective-permute-start.16 = (bf16[384,256]{1,0:T(8,128)(2,1)S(1)}, bf16[384,256]{1,0:T(8,128)(2,1)S(1)}, u32[]{:S(2)}, u32[]{:S(2)}) collective-permute-start(bf16[384,256]{1,0:T(8,128)(2,1)S(1)} %maximum_select_fusion.5.refs_0_), channel_id=1, source_target_pairs={{0,24},{8,16},{16,8},{24,0},{1,25},{9,17},{17,9},{25,1},{2,26},{10... | collective-permute-start | bytes 589832 | tf_op jit(solution)/shard_map/ppermute | solution.py:21
  84.9 1.7 %add_convert_fusion.6 = (bf16[384,128]{1,0:T(8,128)(2,1)}, f32[384,128]{1,0:T(8,128)S(1)}) fusion(bf16[384,128]{1,0:T(8,128)(2,1)} %get-tuple-element.88, bf16[768,128]{1,0:T(8,128)(2,1)S(1)} %collective-permute-done.12, f32[384,128]{1,0:T(8,128)} %get-tuple-element.86), kind=kLoop, calls=%fused_computation.28 | loop fusion | flops 294912 | bytes 786432 | tf_op jit(solution)/shard_map/convert_element_type | solution.py:374
  86.6 10.5 %collective-permute-start.13 = (bf16[384,128]{1,0:T(8,128)(2,1)}, bf16[384,128]{1,0:T(8,128)(2,1)}, u32[]{:S(2)}, u32[]{:S(2)}) collective-permute-start(bf16[384,128]{1,0:T(8,128)(2,1)} %get-tuple-element.161), channel_id=1, source_target_pairs={{0,4},{1,5},{2,6},{3,7},{4,0},{5,1},{6,2},{7,3},{8,12},{9,13},{10,... | collective-permute-start | bytes 294920 | tf_op jit(solution)/shard_map/ppermute | solution.py:21
  98.6 1.6 %copy-done = bf16[768,2048]{1,0:T(8,128)(2,1)} copy-done((bf16[768,2048]{1,0:T(8,128)(2,1)}, bf16[768,2048]{1,0:T(8,128)(2,1)S(1)}, u32[]{:S(2)}) %copy-start) | copy-done | bytes 3145752
  100.3 6.2 %weight_products.3 = (bf16[1024,256]{1,0:T(8,128)(2,1)}, bf16[512,256]{1,0:T(8,128)(2,1)}, f32[512,256]{1,0:T(8,128)}) custom-call(s32[2]{0:T(128)} %pad_add_fusion.1.pos_ref, bf16[384,256]{1,0:T(8,128)(2,1)} %copy-done.2, bf16[384,256]{1,0:T(8,128)(2,1)} %copy-done.19, bf16[384,256]{1,0:T(8,128)(2,1)} %copy-done.20, bf16[384,256]{1,0:T(8,128)(2,1)} %copy-done.21, ...), custom_call_target="tpu_custom_call" | custom-call | flops 1 | bytes 1 | tf_op jit(solution)/shard_map/weight_products/pallas_call | solution.py:273
  108.8 1.5 collective-permute-start.25
  111.0 2.0 %collective-permute-start.23 = (bf16[1024,256]{1,0:T(8,128)(2,1)}, bf16[1024,256]{1,0:T(8,128)(2,1)S(1)}, u32[]{:S(2)}, u32[]{:S(2)}) collective-permute-start(bf16[1024,256]{1,0:T(8,128)(2,1)} %get-tuple-element.104), channel_id=1, source_target_pairs={{0,2},{1,3},{2,0},{3,1},{4,6},{5,7},{6,4},{7,5},{8,10},{9,11},{10,... | collective-permute-start | bytes 1572872 | tf_op jit(solution)/shard_map/ppermute | solution.py:21
  115.2 1.5 collective-permute-start.21
  118.2 5.2 %weight_products.4 = (bf16[1024,128]{1,0:T(8,128)(2,1)}, bf16[512,128]{1,0:T(8,128)(2,1)}, f32[512,128]{1,0:T(8,128)}) custom-call(s32[2]{0:T(128)} %pad_add_fusion.1.pos_ref, bf16[384,128]{1,0:T(8,128)(2,1)} %copy-done.4, bf16[384,128]{1,0:T(8,128)(2,1)} %copy-done.29, bf16[384,128]{1,0:T(8,128)(2,1)} %copy-done.30, bf16[384,128]{1,0:T(8,128)(2,1)} %copy-done.32, ...), custom_call_target="tpu_custom_call" | custom-call | flops 1 | bytes 1 | tf_op jit(solution)/shard_map/weight_products/pallas_call | solution.py:273
  124.2 2.8 %collective-permute-start.29 = (bf16[512,256]{1,0:T(8,128)(2,1)S(1)}, bf16[512,256]{1,0:T(8,128)(2,1)S(1)}, u32[]{:S(2)}, u32[]{:S(2)}) collective-permute-start(bf16[512,256]{1,0:T(8,128)(2,1)S(1)} %get-tuple-element.141), channel_id=1, source_target_pairs={{0,4},{1,5},{2,6},{3,7},{4,0},{5,1},{6,2},{7,3},{8,12},{9,13},{10,... | collective-permute-start | bytes 786440 | tf_op jit(solution)/shard_map/ppermute | solution.py:21
  127.7 5.2 %weight_products.5 = (bf16[1024,128]{1,0:T(8,128)(2,1)}, bf16[512,128]{1,0:T(8,128)(2,1)}, f32[512,128]{1,0:T(8,128)}) custom-call(s32[2]{0:T(128)} %pad_add_fusion.1.pos_ref, bf16[384,128]{1,0:T(8,128)(2,1)} %copy-done.6, bf16[384,128]{1,0:T(8,128)(2,1)} %copy-done.27, bf16[384,128]{1,0:T(8,128)(2,1)} %copy-done.28, bf16[384,128]{1,0:T(8,128)(2,1)} %copy-done.31, ...), custom_call_target="tpu_custom_call" | custom-call | flops 1 | bytes 1 | tf_op jit(solution)/shard_map/weight_products/pallas_call | solution.py:273
  132.9 1.7 %collective-permute-start.31 = (bf16[1024,128]{1,0:T(8,128)(2,1)}, bf16[1024,128]{1,0:T(8,128)(2,1)S(1)}, u32[]{:S(2)}, u32[]{:S(2)}) collective-permute-start(bf16[1024,128]{1,0:T(8,128)(2,1)} %get-tuple-element.128), channel_id=1, source_target_pairs={{0,2},{1,3},{2,0},{3,1},{4,6},{5,7},{6,4},{7,5},{8,10},{9,11},{10,... | collective-permute-start | bytes 786440 | tf_op jit(solution)/shard_map/ppermute | solution.py:21
  134.6 1.8 %collective-permute-done.30 = bf16[1024,128]{1,0:T(8,128)(2,1)S(1)} collective-permute-done((bf16[1024,128]{1,0:T(8,128)(2,1)}, bf16[1024,128]{1,0:T(8,128)(2,1)S(1)}, u32[]{:S(2)}, u32[]{:S(2)}) %collective-permute-start.30) | collective-permute-done | bytes 262176 | tf_op jit(solution)/shard_map/ppermute | solution.py:21
  136.4 1.6 %collective-permute-start.33 = (bf16[512,128]{1,0:T(8,128)(2,1)S(1)}, bf16[512,128]{1,0:T(8,128)(2,1)S(1)}, u32[]{:S(2)}, u32[]{:S(2)}) collective-permute-start(bf16[512,128]{1,0:T(8,128)(2,1)S(1)} %get-tuple-element.151), channel_id=1, source_target_pairs={{0,4},{1,5},{2,6},{3,7},{4,0},{5,1},{6,2},{7,3},{8,12},{9,13},{10,... | collective-permute-start | bytes 393224 | tf_op jit(solution)/shard_map/ppermute | solution.py:21
  141.2 2.2 %collective-permute-done.31 = bf16[1024,128]{1,0:T(8,128)(2,1)S(1)} collective-permute-done((bf16[1024,128]{1,0:T(8,128)(2,1)}, bf16[1024,128]{1,0:T(8,128)(2,1)S(1)}, u32[]{:S(2)}, u32[]{:S(2)}) %collective-permute-start.31) | collective-permute-done | bytes 262176 | tf_op jit(solution)/shard_map/ppermute | solution.py:21
  145.5 6.1 %collective-permute-done.32 = bf16[512,128]{1,0:T(8,128)(2,1)S(1)} collective-permute-done((bf16[512,128]{1,0:T(8,128)(2,1)S(1)}, bf16[512,128]{1,0:T(8,128)(2,1)S(1)}, u32[]{:S(2)}, u32[]{:S(2)}) %collective-permute-start.32) | collective-permute-done | bytes 131104 | tf_op jit(solution)/shard_map/ppermute | solution.py:21
  153.9 1.7 %maximum_select_fusion = bf16[192,4096]{1,0:T(8,128)(2,1)} fusion(bf16[192,2048]{1,0:T(8,128)(2,1)S(1)} %collective-permute-done.27, bf16[192,1024]{1,0:T(8,128)(2,1)S(1)} %copy-done.15, bf16[192,1024]{1,0:T(8,128)(2,1)S(1)} %copy-done.14, pred[]{:T(512)S(6)} %eq.5), kind=kLoop, calls=%fused_computation.1 | loop fusion | flops 10223616 | bytes 3145729 | tf_op jit(solution)/shard_map/jit(_where)/select_n | solution.py:323
  (169 shorter events, 29.1 us)
Async XLA Ops:
  5.6 28.1 %collective-permute-start.1 = (bf16[192,2048]{1,0:T(8,128)(2,1)S(1)}, bf16[192,2048]{1,0:T(8,128)(2,1)S(1)}, u32[]{:S(2)}, u32[]{:S(2)}) collective-permute-start(bf16[192,2048]{1,0:T(8,128)(2,1)S(1)} %pad_maximum_fusion), channel_id=1, source_target_pairs={{0,1},{1,0},{2,3},{3,2},{4,5},{5,4},{6,7},{7,6},{8,9},{9,8},{10,11... | collective-permute-start | bytes 2359304 | tf_op jit(solution)/shard_map/ppermute | solution.py:21
  6.0 22.7 %collective-permute-start.2 = (bf16[384,256]{1,0:T(8,128)(2,1)S(1)}, bf16[384,256]{1,0:T(8,128)(2,1)S(1)}, u32[]{:S(2)}, u32[]{:S(2)}) collective-permute-start(bf16[384,256]{1,0:T(8,128)(2,1)S(1)} %maximum_select_fusion.3.refs_0_), channel_id=1, source_target_pairs={{0,2},{1,3},{2,0},{3,1},{4,6},{5,7},{6,4},{7,5},{8,10},{9,11},{10,... | collective-permute-start | bytes 589832 | tf_op jit(solution)/shard_map/ppermute | solution.py:21
  10.9 12.0 %collective-permute-start.3 = (bf16[384,256]{1,0:T(8,128)(2,1)S(1)}, bf16[384,256]{1,0:T(8,128)(2,1)S(1)}, u32[]{:S(2)}, u32[]{:S(2)}) collective-permute-start(bf16[384,256]{1,0:T(8,128)(2,1)S(1)} %maximum_select_fusion.3.refs_0_), channel_id=1, source_target_pairs={{0,4},{1,5},{2,6},{3,7},{4,0},{5,1},{6,2},{7,3},{8,12},{9,13},{10,... | collective-permute-start | bytes 589832 | tf_op jit(solution)/shard_map/ppermute | solution.py:21
  24.1 36.0 %collective-permute-start.5 = (bf16[192,2048]{1,0:T(8,128)(2,1)}, bf16[192,2048]{1,0:T(8,128)(2,1)}, u32[]{:S(2)}, u32[]{:S(2)}) collective-permute-start(bf16[192,2048]{1,0:T(8,128)(2,1)} %pad_maximum_fusion.1), channel_id=1, source_target_pairs={{0,1},{1,0},{2,3},{3,2},{4,5},{5,4},{6,7},{7,6},{8,9},{9,8},{10,11... | collective-permute-start | bytes 2359304 | tf_op jit(solution)/shard_map/ppermute | solution.py:21
  24.1 46.9 %all-to-all-start = ((bf16[4,192,2048]{2,1,0:T(8,128)(2,1)}), bf16[4,192,2048]{2,1,0:T(8,128)(2,1)}, u32[]{:S(2)}, u32[]{:S(2)}) async-start(bf16[4,192,2048]{2,1,0:T(8,128)(2,1)} %bitcast.10), calls=%async_computation | async-start | bytes 6291456 | tf_op jit(solution)/shard_map/all_to_all | solution.py:398
  28.9 24.6 %collective-permute-start.6 = (bf16[384,256]{1,0:T(8,128)(2,1)}, bf16[384,256]{1,0:T(8,128)(2,1)}, u32[]{:S(2)}, u32[]{:S(2)}) collective-permute-start(bf16[384,256]{1,0:T(8,128)(2,1)} %maximum_select_fusion.4.refs_0_), channel_id=1, source_target_pairs={{0,2},{1,3},{2,0},{3,1},{4,6},{5,7},{6,4},{7,5},{8,10},{9,11},{10,... | collective-permute-start | bytes 589832 | tf_op jit(solution)/shard_map/ppermute | solution.py:21
  30.4 29.2 %collective-permute-start.7 = (bf16[384,256]{1,0:T(8,128)(2,1)}, bf16[384,256]{1,0:T(8,128)(2,1)}, u32[]{:S(2)}, u32[]{:S(2)}) collective-permute-start(bf16[384,256]{1,0:T(8,128)(2,1)} %maximum_select_fusion.4.refs_0_), channel_id=1, source_target_pairs={{0,4},{1,5},{2,6},{3,7},{4,0},{5,1},{6,2},{7,3},{8,12},{9,13},{10,... | collective-permute-start | bytes 589832 | tf_op jit(solution)/shard_map/ppermute | solution.py:21
  33.8 26.4 %collective-permute-start.8 = (bf16[384,256]{1,0:T(8,128)(2,1)}, bf16[384,256]{1,0:T(8,128)(2,1)}, u32[]{:S(2)}, u32[]{:S(2)}) collective-permute-start(bf16[384,256]{1,0:T(8,128)(2,1)} %maximum_select_fusion.4.refs_0_), channel_id=1, source_target_pairs={{0,6},{1,7},{2,4},{3,5},{4,2},{5,3},{6,0},{7,1},{8,14},{9,15},{10,... | collective-permute-start | bytes 589832 | tf_op jit(solution)/shard_map/ppermute | solution.py:21
  43.2 25.6 %collective-permute-start.10 = (bf16[384,256]{1,0:T(8,128)(2,1)}, bf16[384,256]{1,0:T(8,128)(2,1)}, u32[]{:S(2)}, u32[]{:S(2)}) collective-permute-start(bf16[384,256]{1,0:T(8,128)(2,1)} %get-tuple-element.78), channel_id=1, source_target_pairs={{0,4},{1,5},{2,6},{3,7},{4,0},{5,1},{6,2},{7,3},{8,12},{9,13},{10,... | collective-permute-start | bytes 589832 | tf_op jit(solution)/shard_map/ppermute | solution.py:21
  53.5 16.3 %collective-permute-start.11 = (bf16[384,256]{1,0:T(8,128)(2,1)}, bf16[384,256]{1,0:T(8,128)(2,1)}, u32[]{:S(2)}, u32[]{:S(2)}) collective-permute-start(bf16[384,256]{1,0:T(8,128)(2,1)} %get-tuple-element.79), channel_id=1, source_target_pairs={{0,6},{1,7},{2,4},{3,5},{4,2},{5,3},{6,0},{7,1},{8,14},{9,15},{10,... | collective-permute-start | bytes 589832 | tf_op jit(solution)/shard_map/ppermute | solution.py:21
  59.6 10.2 %collective-permute-start.9 = (bf16[384,256]{1,0:T(8,128)(2,1)}, bf16[384,256]{1,0:T(8,128)(2,1)}, u32[]{:S(2)}, u32[]{:S(2)}) collective-permute-start(bf16[384,256]{1,0:T(8,128)(2,1)} %get-tuple-element.77), channel_id=1, source_target_pairs={{0,2},{1,3},{2,0},{3,1},{4,6},{5,7},{6,4},{7,5},{8,10},{9,11},{10,... | collective-permute-start | bytes 589832 | tf_op jit(solution)/shard_map/ppermute | solution.py:21
  71.0 27.6 %collective-permute-start.18 = (bf16[768,2048]{1,0:T(8,128)(2,1)}, bf16[768,2048]{1,0:T(8,128)(2,1)S(1)}, u32[]{:S(2)}, u32[]{:S(2)}) collective-permute-start(bf16[768,2048]{1,0:T(8,128)(2,1)} %bitcast.4.refs_4_), channel_id=1, source_target_pairs={{0,1},{1,0},{2,3},{3,2},{4,5},{5,4},{6,7},{7,6},{8,9},{9,8},{10,11... | collective-permute-start | bytes 9437192 | tf_op jit(solution)/shard_map/ppermute | solution.py:21
  71.7 10.8 %collective-permute-start.12 = (bf16[768,128]{1,0:T(8,128)(2,1)}, bf16[768,128]{1,0:T(8,128)(2,1)S(1)}, u32[]{:S(2)}, u32[]{:S(2)}) collective-permute-start(bf16[768,128]{1,0:T(8,128)(2,1)} %get-tuple-element.87), channel_id=1, source_target_pairs={{0,2},{1,3},{2,0},{3,1},{4,6},{5,7},{6,4},{7,5},{8,10},{9,11},{10,... | collective-permute-start | bytes 589832 | tf_op jit(solution)/shard_map/ppermute | solution.py:21
  76.5 10.1 %collective-permute-start.17 = (bf16[768,128]{1,0:T(8,128)(2,1)}, bf16[768,128]{1,0:T(8,128)(2,1)S(1)}, u32[]{:S(2)}, u32[]{:S(2)}) collective-permute-start(bf16[768,128]{1,0:T(8,128)(2,1)} %get-tuple-element.90), channel_id=1, source_target_pairs={{0,2},{1,3},{2,0},{3,1},{4,6},{5,7},{6,4},{7,5},{8,10},{9,11},{10,... | collective-permute-start | bytes 589832 | tf_op jit(solution)/shard_map/ppermute | solution.py:21
  76.6 20.5 %collective-permute-start.14 = (bf16[384,256]{1,0:T(8,128)(2,1)S(1)}, bf16[384,256]{1,0:T(8,128)(2,1)S(1)}, u32[]{:S(2)}, u32[]{:S(2)}) collective-permute-start(bf16[384,256]{1,0:T(8,128)(2,1)S(1)} %maximum_select_fusion.5.refs_0_), channel_id=1, source_target_pairs={{0,8},{8,0},{16,24},{24,16},{1,9},{9,1},{17,25},{25,17},{2,10},{10... | collective-permute-start | bytes 589832 | tf_op jit(solution)/shard_map/ppermute | solution.py:21
  78.2 19.0 %collective-permute-start.15 = (bf16[384,256]{1,0:T(8,128)(2,1)S(1)}, bf16[384,256]{1,0:T(8,128)(2,1)S(1)}, u32[]{:S(2)}, u32[]{:S(2)}) collective-permute-start(bf16[384,256]{1,0:T(8,128)(2,1)S(1)} %maximum_select_fusion.5.refs_0_), channel_id=1, source_target_pairs={{0,16},{8,24},{16,0},{24,8},{1,17},{9,25},{17,1},{25,9},{2,18},{10... | collective-permute-start | bytes 589832 | tf_op jit(solution)/shard_map/ppermute | solution.py:21
  82.4 14.8 %collective-permute-start.16 = (bf16[384,256]{1,0:T(8,128)(2,1)S(1)}, bf16[384,256]{1,0:T(8,128)(2,1)S(1)}, u32[]{:S(2)}, u32[]{:S(2)}) collective-permute-start(bf16[384,256]{1,0:T(8,128)(2,1)S(1)} %maximum_select_fusion.5.refs_0_), channel_id=1, source_target_pairs={{0,24},{8,16},{16,8},{24,0},{1,25},{9,17},{17,9},{25,1},{2,26},{10... | collective-permute-start | bytes 589832 | tf_op jit(solution)/shard_map/ppermute | solution.py:21
  86.6 19.9 %collective-permute-start.13 = (bf16[384,128]{1,0:T(8,128)(2,1)}, bf16[384,128]{1,0:T(8,128)(2,1)}, u32[]{:S(2)}, u32[]{:S(2)}) collective-permute-start(bf16[384,128]{1,0:T(8,128)(2,1)} %get-tuple-element.161), channel_id=1, source_target_pairs={{0,4},{1,5},{2,6},{3,7},{4,0},{5,1},{6,2},{7,3},{8,12},{9,13},{10,... | collective-permute-start | bytes 294920 | tf_op jit(solution)/shard_map/ppermute | solution.py:21
  97.1 15.8 %collective-permute-start.19 = (bf16[384,128]{1,0:T(8,128)(2,1)S(1)}, bf16[384,128]{1,0:T(8,128)(2,1)}, u32[]{:S(2)}, u32[]{:S(2)}) collective-permute-start(bf16[384,128]{1,0:T(8,128)(2,1)S(1)} %get-tuple-element.159), channel_id=1, source_target_pairs={{0,4},{1,5},{2,6},{3,7},{4,0},{5,1},{6,2},{7,3},{8,12},{9,13},{10,... | collective-permute-start | bytes 294920 | tf_op jit(solution)/shard_map/ppermute | solution.py:21
  107.4 7.7 %collective-permute-start.24 = (bf16[384,128]{1,0:T(8,128)(2,1)S(1)}, bf16[384,128]{1,0:T(8,128)(2,1)S(1)}, u32[]{:S(2)}, u32[]{:S(2)}) collective-permute-start(bf16[384,128]{1,0:T(8,128)(2,1)S(1)} %maximum_select_fusion.8.refs_0_), channel_id=1, source_target_pairs={{0,8},{8,0},{16,24},{24,16},{1,9},{9,1},{17,25},{25,17},{2,10},{10... | collective-permute-start | bytes 294920 | tf_op jit(solution)/shard_map/ppermute | solution.py:21
  108.8 7.8 %collective-permute-start.25 = (bf16[384,128]{1,0:T(8,128)(2,1)S(1)}, bf16[384,128]{1,0:T(8,128)(2,1)S(1)}, u32[]{:S(2)}, u32[]{:S(2)}) collective-permute-start(bf16[384,128]{1,0:T(8,128)(2,1)S(1)} %maximum_select_fusion.8.refs_0_), channel_id=1, source_target_pairs={{0,16},{8,24},{16,0},{24,8},{1,17},{9,25},{17,1},{25,9},{2,18},{10... | collective-permute-start | bytes 294920 | tf_op jit(solution)/shard_map/ppermute | solution.py:21
  110.4 7.1 %collective-permute-start.26 = (bf16[384,128]{1,0:T(8,128)(2,1)S(1)}, bf16[384,128]{1,0:T(8,128)(2,1)S(1)}, u32[]{:S(2)}, u32[]{:S(2)}) collective-permute-start(bf16[384,128]{1,0:T(8,128)(2,1)S(1)} %maximum_select_fusion.8.refs_0_), channel_id=1, source_target_pairs={{0,24},{8,16},{16,8},{24,0},{1,25},{9,17},{17,9},{25,1},{2,26},{10... | collective-permute-start | bytes 294920 | tf_op jit(solution)/shard_map/ppermute | solution.py:21
  111.0 13.1 %collective-permute-start.23 = (bf16[1024,256]{1,0:T(8,128)(2,1)}, bf16[1024,256]{1,0:T(8,128)(2,1)S(1)}, u32[]{:S(2)}, u32[]{:S(2)}) collective-permute-start(bf16[1024,256]{1,0:T(8,128)(2,1)} %get-tuple-element.104), channel_id=1, source_target_pairs={{0,2},{1,3},{2,0},{3,1},{4,6},{5,7},{6,4},{7,5},{8,10},{9,11},{10,... | collective-permute-start | bytes 1572872 | tf_op jit(solution)/shard_map/ppermute | solution.py:21
  113.9 13.0 %collective-permute-start.20 = (bf16[384,128]{1,0:T(8,128)(2,1)S(1)}, bf16[384,128]{1,0:T(8,128)(2,1)S(1)}, u32[]{:S(2)}, u32[]{:S(2)}) collective-permute-start(bf16[384,128]{1,0:T(8,128)(2,1)S(1)} %maximum_select_fusion.9.refs_0_), channel_id=1, source_target_pairs={{0,8},{8,0},{16,24},{24,16},{1,9},{9,1},{17,25},{25,17},{2,10},{10... | collective-permute-start | bytes 294920 | tf_op jit(solution)/shard_map/ppermute | solution.py:21
  115.2 11.8 %collective-permute-start.21 = (bf16[384,128]{1,0:T(8,128)(2,1)S(1)}, bf16[384,128]{1,0:T(8,128)(2,1)S(1)}, u32[]{:S(2)}, u32[]{:S(2)}) collective-permute-start(bf16[384,128]{1,0:T(8,128)(2,1)S(1)} %maximum_select_fusion.9.refs_0_), channel_id=1, source_target_pairs={{0,16},{8,24},{16,0},{24,8},{1,17},{9,25},{17,1},{25,9},{2,18},{10... | collective-permute-start | bytes 294920 | tf_op jit(solution)/shard_map/ppermute | solution.py:21
  116.7 10.3 %collective-permute-start.22 = (bf16[384,128]{1,0:T(8,128)(2,1)S(1)}, bf16[384,128]{1,0:T(8,128)(2,1)S(1)}, u32[]{:S(2)}, u32[]{:S(2)}) collective-permute-start(bf16[384,128]{1,0:T(8,128)(2,1)S(1)} %maximum_select_fusion.9.refs_0_), channel_id=1, source_target_pairs={{0,24},{8,16},{16,8},{24,0},{1,25},{9,17},{17,9},{25,1},{2,26},{10... | collective-permute-start | bytes 294920 | tf_op jit(solution)/shard_map/ppermute | solution.py:21
  123.4 13.0 %collective-permute-start.30 = (bf16[1024,128]{1,0:T(8,128)(2,1)}, bf16[1024,128]{1,0:T(8,128)(2,1)S(1)}, u32[]{:S(2)}, u32[]{:S(2)}) collective-permute-start(bf16[1024,128]{1,0:T(8,128)(2,1)} %get-tuple-element.115), channel_id=1, source_target_pairs={{0,2},{1,3},{2,0},{3,1},{4,6},{5,7},{6,4},{7,5},{8,10},{9,11},{10,... | collective-permute-start | bytes 786440 | tf_op jit(solution)/shard_map/ppermute | solution.py:21
  124.2 17.0 %collective-permute-start.29 = (bf16[512,256]{1,0:T(8,128)(2,1)S(1)}, bf16[512,256]{1,0:T(8,128)(2,1)S(1)}, u32[]{:S(2)}, u32[]{:S(2)}) collective-permute-start(bf16[512,256]{1,0:T(8,128)(2,1)S(1)} %get-tuple-element.141), channel_id=1, source_target_pairs={{0,4},{1,5},{2,6},{3,7},{4,0},{5,1},{6,2},{7,3},{8,12},{9,13},{10,... | collective-permute-start | bytes 786440 | tf_op jit(solution)/shard_map/ppermute | solution.py:21
  132.9 10.5 %collective-permute-start.31 = (bf16[1024,128]{1,0:T(8,128)(2,1)}, bf16[1024,128]{1,0:T(8,128)(2,1)S(1)}, u32[]{:S(2)}, u32[]{:S(2)}) collective-permute-start(bf16[1024,128]{1,0:T(8,128)(2,1)} %get-tuple-element.128), channel_id=1, source_target_pairs={{0,2},{1,3},{2,0},{3,1},{4,6},{5,7},{6,4},{7,5},{8,10},{9,11},{10,... | collective-permute-start | bytes 786440 | tf_op jit(solution)/shard_map/ppermute | solution.py:21
  136.4 8.4 %collective-permute-start.33 = (bf16[512,128]{1,0:T(8,128)(2,1)S(1)}, bf16[512,128]{1,0:T(8,128)(2,1)S(1)}, u32[]{:S(2)}, u32[]{:S(2)}) collective-permute-start(bf16[512,128]{1,0:T(8,128)(2,1)S(1)} %get-tuple-element.151), channel_id=1, source_target_pairs={{0,4},{1,5},{2,6},{3,7},{4,0},{5,1},{6,2},{7,3},{8,12},{9,13},{10,... | collective-permute-start | bytes 393224 | tf_op jit(solution)/shard_map/ppermute | solution.py:21
  138.4 15.5 %collective-permute-start.27 = (bf16[192,2048]{1,0:T(8,128)(2,1)S(1)}, bf16[192,2048]{1,0:T(8,128)(2,1)S(1)}, u32[]{:S(2)}, u32[]{:S(2)}) collective-permute-start(bf16[192,2048]{1,0:T(8,128)(2,1)S(1)} %pad_maximum_fusion.2), channel_id=1, source_target_pairs={{0,1},{1,0},{2,3},{3,2},{4,5},{5,4},{6,7},{7,6},{8,9},{9,8},{10,11... | collective-permute-start | bytes 2359304 | tf_op jit(solution)/shard_map/ppermute | solution.py:21
  143.5 8.1 %collective-permute-start.32 = (bf16[512,128]{1,0:T(8,128)(2,1)S(1)}, bf16[512,128]{1,0:T(8,128)(2,1)S(1)}, u32[]{:S(2)}, u32[]{:S(2)}) collective-permute-start(bf16[512,128]{1,0:T(8,128)(2,1)S(1)} %get-tuple-element.149), channel_id=1, source_target_pairs={{0,4},{1,5},{2,6},{3,7},{4,0},{5,1},{6,2},{7,3},{8,12},{9,13},{10,... | collective-permute-start | bytes 393224 | tf_op jit(solution)/shard_map/ppermute | solution.py:21
  (43 other events, 261.5 us)

commit v3 on v2

--- a/solution.py
+++ b/solution.py
@@ -195,7 +195,7 @@
     else:
         groups = [(0,)] + by_lowest_bit(chips)
         layout = tuple((slots, lo, lo + HD) for lo in (HD, 0) for slots in groups)
-    hbm = pl.BlockSpec(memory_space=pltpu.HBM)
+    hbm = pl.BlockSpec(memory_space=pl.ANY)
     out_shape = [jax.ShapeDtypeStruct((tok, width), BF16)] * 2 + [
         jax.ShapeDtypeStruct((len(slots) * span, hi - lo), F32 if slots == (0,) else BF16)
         for slots, lo, hi in layout
@@ -234,33 +234,36 @@
 
 
 def product_kernel(chips, n_dp, tok, order, pos_ref, *refs):
-    slots, halves, outs = refs[:n_dp], refs[n_dp : n_dp + PAIR], refs[n_dp + PAIR : -4]
-    kvs, turned, held, sems = refs[-4:]
+    slots, halves, outs = refs[:n_dp], refs[n_dp : n_dp + PAIR], refs[n_dp + PAIR : -5]
+    kvs, turned, *staged, out_sems = refs[-5:]
     depth = n_dp * tok
-    block = held.shape[2]
+    block = staged[1].shape[0]
     flat = [s for group in order for s in group]
-    copies = []
+    for s in range(n_dp):
+        kvs[pos_ref[2] ^ s] = slots[s][...]
+    for at in range(PAIR):
+        rows = kvs[:, at * tok : (at + 1) * tok]
+        turned[at] = rows.reshape(depth, rows.shape[2]).T
+    leaving = []
     for i, s in enumerate(flat):
         columns = pl.ds(pl.multiple_of((pos_ref[0] ^ s) * block, block), block)
-        for at, half in enumerate(halves):
-            copy = pltpu.make_async_copy(
-                half.at[:, columns], held.at[i, pl.ds(at * depth, depth)], sems.at[i, at]
-            )
-            copy.start()
-            copies.append(copy)
-    for s in range(n_dp):
-        kvs[pos_ref[1] ^ s] = slots[s][...]
-    for at in range(PAIR):
-        rows = kvs[:, at * tok : (at + 1) * tok]
-        turned[:, at * depth : (at + 1) * depth] = rows.reshape(depth, rows.shape[2]).T
-    i = 0
-    for out, group in zip(outs, order):
-        for at in range(len(group)):
-            for copy in copies[i * PAIR : (i + 1) * PAIR]:
-                copy.wait()
-            both = jnp.dot(turned[...], held[i], preferred_element_type=F32)
-            out[at * block : (at + 1) * block] = both.T.astype(out.dtype)
-            i += 1
+        both = sum(
+            jnp.dot(turned[at], halves[at][:, columns], preferred_element_type=F32)
+            for at in range(PAIR)
+        ).T
+        n = next(n for n, group in enumerate(order) if s in group)
+        target = outs[n].at[pl.ds(order[n].index(s) * block, block)]
+        if s == 0:
+            staged[1][...] = both
+            source = staged[1]
+        else:
+            staged[0][i] = both.astype(BF16)
+            source = staged[0].at[i]
+        copy = pltpu.make_async_copy(source, target, out_sems.at[i])
+        copy.start()
+        leaving.append(copy)
+    for copy in leaving:
+        copy.wait()
 
 
 def weight_products(pos, slots, hidden_own, hidden_oth, chips):
@@ -269,26 +272,23 @@
     depth, share = hidden_own.shape
     block = share // chips
     order = by_lowest_bit(chips) + [(0,)]
-    vmem = pl.BlockSpec(memory_space=pltpu.VMEM)
+    anywhere = pl.BlockSpec(memory_space=pl.ANY)
     outs = pl.pallas_call(
         functools.partial(product_kernel, chips, n_dp, span // PAIR, order),
-        in_specs=[pl.BlockSpec(memory_space=pltpu.SMEM)]
-        + [vmem] * n_dp
-        + [pl.BlockSpec(memory_space=pltpu.HBM)] * PAIR,
-        out_specs=[pl.BlockSpec()] * len(order),
+        in_specs=[pl.BlockSpec(memory_space=pltpu.SMEM)] + [pl.BlockSpec(memory_space=pltpu.VMEM)] * (n_dp + PAIR),
+        out_specs=[anywhere] * len(order),
         out_shape=[
             jax.ShapeDtypeStruct((len(group) * block, wide), F32 if group == (0,) else BF16)
             for group in order
         ],
         scratch_shapes=[
             pltpu.VMEM((n_dp, span, wide), BF16),
-            pltpu.VMEM((wide, PAIR * depth), BF16),
-            pltpu.VMEM((chips, PAIR * depth, block), BF16),
-            pltpu.SemaphoreType.DMA((chips, PAIR)),
+            pltpu.VMEM((PAIR, wide, depth), BF16),
+            pltpu.VMEM((chips - 1, block, wide), BF16),
+            pltpu.VMEM((block, wide), F32),
+            pltpu.SemaphoreType.DMA((chips,)),
         ],
-        compiler_params=pltpu.CompilerParams(
-            vmem_limit_bytes=VMEM_BYTES
-        ),
+        compiler_params=pltpu.CompilerParams(vmem_limit_bytes=16 << 20),
         cost_estimate=pl.CostEstimate(flops=1, bytes_accessed=1, transcendentals=0),
         name="weight_products",
     )(pos, *slots, hidden_own, hidden_oth)
@@ -309,8 +309,7 @@
     width = queries.shape[1] // kv_heads
     dp, ctx = lax.axis_index("dp"), lax.axis_index("ctx")
     chip, core = ctx // PAIR, ctx % PAIR
-    pos = jnp.stack([chip, core]).astype(jnp.int32)
-    place = jnp.stack([chip, dp]).astype(jnp.int32)
+    pos = jnp.stack([chip, core, dp]).astype(jnp.int32)
     first = core == 0
 
     def swap(x):
@@ -350,7 +349,7 @@
         return [total] + [xor_permute(total, "dp", n_dp, s) for s in range(1, n_dp)]
 
     def product_blocks(slots, *gate):
-        return weight_products(place, after(slots, *gate), hidden_own, hidden_oth, chips)
+        return weight_products(pos, after(slots, *gate), hidden_own, hidden_oth, chips)
 
     def core_rows(summed):
         rows = share // n_ctx
@@ -441,28 +440,26 @@
     for i in range(bits - 1):
         product_k = step(*product_k, i, product)
     product_v = step(*product_v, bits - 1, product_k)
-    product_k = step(*product_k, bits - 1, product_v)
-    w_first, w_value, w_key = (core_rows(x[0]) for x in (product, product_v, product_k))
+
+    def spread(one, two, lo):
+        return in_order(*(jnp.concatenate([x[:, lo : lo + HD], y], 1) for x, y in zip(one, two)), 1)
+
     both = swap(jnp.concatenate([total[tok:], total_k[tok:], total_v[tok:]], 1))
     wide = 2 * HD
     kv_first = total[:tok], both[:, :wide]
-    kv_key = total_k[:tok], both[:, wide : wide + HD]
-    kv_value = total_v[:tok], both[:, wide + HD :]
-
-    def spread(one, two, lo):
-        return in_order(*(jnp.concatenate([x[:, lo : lo + HD], y], 1) for x, y in zip(one, two)), 1)
-
-    return (
+    w_first, w_value = core_rows(product[0]), core_rows(product_v[0])
+    done = (
         in_order(
             jnp.concatenate([dq_own, dq_own1], 1),
             swap(jnp.concatenate([dq_oth, dq_oth1], 1)),
             1,
         ),
-        spread(kv_first, kv_key, 0),
-        spread(kv_first, kv_value, HD),
-        spread(w_first, w_key, 0),
-        spread(w_first, w_value, HD),
+        spread(kv_first, (total_k[:tok], both[:, wide : wide + HD]), 0),
+        spread(kv_first, (total_v[:tok], both[:, wide + HD :]), HD),
     )
+    value_weights = spread(w_first, w_value, HD)
+    product_k = step(*product_k, bits - 1, done, value_weights)
+    return *done, spread(w_first, core_rows(product_k[0]), 0), value_weights
 
 
 def solution(mesh):

time: 156 us -> 151 us (0.968)
  waiting for transfers between devices: 24.7 us -> 29.3 us
  local copies, waits for them, and re-layouts: 9.9 us -> 5.51 us
  Pallas kernels: 33.7 us -> 30.8 us
  other arithmetic: 13.1 us -> 10.2 us
    ppermute x37, waiting for transfers between devices: 24.7 us -> 29.3 us  [xor_permute(): return lax.ppermute(array, axis, [(i, i ^ mask) for i in range(size)])]
    unnamed x74 -> x32, local copies, waits for them, and re-layouts: 5.42 us -> 1.01 us
    pallas_call x3, Pallas kernels: 16.6 us -> 13.6 us  [weight_products(): pl.pallas_call(functools.partial(product_kernel, chips, n_dp, span // PAI...]
  transfers between devices with their start and end apart: 38 -> 38, of which waited for: 10 -> 14; matrix products, arithmetic and copies ran while one was open for 8% -> 7% of each run, Pallas kernels for 22% -> 20%
where the time goes in v3:
time: 151 us; the launch traced here: 150 us
  starting transfers between devices  73.4 us (49%)
  Pallas kernels  30.8 us (20%)
  waiting for transfers between devices  29.3 us (19%)
  other arithmetic  10.2 us (7%)
  local copies, waits for them, and re-layouts  5.51 us (4%)
    ppermute x37, starting transfers between devices, xor_permute(): return lax.ppermute(array, axis, [(i, i ^ mask) for i in range(size)])  68.7 us
    ppermute x37, waiting for transfers between devices, xor_permute(): return lax.ppermute(array, axis, [(i, i ^ mask) for i in range(size)])  29.3 us
    pallas_call x2, Pallas kernels, attention(): pl.pallas_call(functools.partial(attention_kernel, chips, tok, group, hea...  17.2 us
    pallas_call x3, Pallas kernels, weight_products(): pl.pallas_call(functools.partial(product_kernel, chips, n_dp, span // PAI...  13.6 us
    select_n x7, other arithmetic, in_order(): jnp.where(first, jnp.concatenate([mine, theirs], axis), jnp.concatenate([...  5.68 us
    all_to_all x1, starting transfers between devices, on_device(): lax.all_to_all(shares, 'dp', split_axis=0, concat_axis=0, tiled=True)  4.7 us
  transfers between devices with their start and end apart: 38, of which 14 were waited for; matrix products, arithmetic and copies ran while one was open for 7% of the time, Pallas kernels for 20%

profile of v3, /device:TPU:0, one launch (start us, length us, event | category | flops | bytes accessed | tf_op | source)
XLA Modules:
  0.0 150.4 jit_solution(1003155422245664435)
XLA Ops:
  6.0 2.7 %collective-permute-start.2 = (bf16[384,256]{1,0:T(8,128)(2,1)S(1)}, bf16[384,256]{1,0:T(8,128)(2,1)S(1)}, u32[]{:S(2)}, u32[]{:S(2)}) collective-permute-start(bf16[384,256]{1,0:T(8,128)(2,1)S(1)} %maximum_select_fusion.3.refs_0_), channel_id=1, source_target_pairs={{0,2},{1,3},{2,0},{3,1},{4,6},{5,7},{6,4},{7,5},{8,10},{9,11},{10,... | collective-permute-start | bytes 589832 | tf_op jit(solution)/shard_map/ppermute | solution.py:21
  8.8 2.1 %copy.13 = bf16[24,4,8,2048]{3,2,0,1:T(8,128)(2,1)} copy(bf16[24,4,8,2048]{3,2,1,0:T(8,128)(2,1)S(1)} %bitcast.11) | data formatting | bytes 6291456 | tf_op jit(solution)/shard_map/reshape | solution.py:391
  10.9 2.6 %collective-permute-start.3 = (bf16[384,256]{1,0:T(8,128)(2,1)S(1)}, bf16[384,256]{1,0:T(8,128)(2,1)S(1)}, u32[]{:S(2)}, u32[]{:S(2)}) collective-permute-start(bf16[384,256]{1,0:T(8,128)(2,1)S(1)} %maximum_select_fusion.3.refs_0_), channel_id=1, source_target_pairs={{0,4},{1,5},{2,6},{3,7},{4,0},{5,1},{6,2},{7,3},{8,12},{9,13},{10,... | collective-permute-start | bytes 589832 | tf_op jit(solution)/shard_map/ppermute | solution.py:21
  14.4 8.5 %collective-permute-done.3.refs_2_ = bf16[384,256]{1,0:T(8,128)(2,1)S(1)} collective-permute-done((bf16[384,256]{1,0:T(8,128)(2,1)S(1)}, bf16[384,256]{1,0:T(8,128)(2,1)S(1)}, u32[]{:S(2)}, u32[]{:S(2)}) %collective-permute-start.3) | collective-permute-done | bytes 196640 | tf_op jit(solution)/shard_map/ppermute | solution.py:21
  24.2 4.7 %all-to-all-start = ((bf16[4,192,2048]{2,1,0:T(8,128)(2,1)}), bf16[4,192,2048]{2,1,0:T(8,128)(2,1)}, u32[]{:S(2)}, u32[]{:S(2)}) async-start(bf16[4,192,2048]{2,1,0:T(8,128)(2,1)} %bitcast.10), calls=%async_computation | async-start | bytes 6291456 | tf_op jit(solution)/shard_map/all_to_all | solution.py:397
  30.4 3.4 %collective-permute-start.7 = (bf16[384,256]{1,0:T(8,128)(2,1)}, bf16[384,256]{1,0:T(8,128)(2,1)}, u32[]{:S(2)}, u32[]{:S(2)}) collective-permute-start(bf16[384,256]{1,0:T(8,128)(2,1)} %maximum_select_fusion.4.refs_0_), channel_id=1, source_target_pairs={{0,4},{1,5},{2,6},{3,7},{4,0},{5,1},{6,2},{7,3},{8,12},{9,13},{10,... | collective-permute-start | bytes 589832 | tf_op jit(solution)/shard_map/ppermute | solution.py:21
  34.8 8.5 %attention_grads.2 = (bf16[192,1024]{1,0:T(8,128)(2,1)}, bf16[192,1024]{1,0:T(8,128)(2,1)}, f32[384,256]{1,0:T(8,128)}, bf16[384,256]{1,0:T(8,128)(2,1)}, bf16[3...) custom-call(s32[3]{0:T(128)} %pad_add_fusion.pos_ref, bf16[192,4096]{1,0:T(8,128)(2,1)} %q_own.3, bf16[192,4096]{1,0:T(8,128)(2,1)} %g_own.3, ...), custom_call_target="tpu_custom_call" | custom-call | flops 241591910400 | bytes 2359296 | tf_op jit(solution)/shard_map/attention_grads/pallas_call | solution.py:204
  43.3 10.3 %collective-permute-start.10 = (bf16[384,256]{1,0:T(8,128)(2,1)}, bf16[384,256]{1,0:T(8,128)(2,1)}, u32[]{:S(2)}, u32[]{:S(2)}) collective-permute-start(bf16[384,256]{1,0:T(8,128)(2,1)} %get-tuple-element.78), channel_id=1, source_target_pairs={{0,4},{1,5},{2,6},{3,7},{4,0},{5,1},{6,2},{7,3},{8,12},{9,13},{10,... | collective-permute-start | bytes 589832 | tf_op jit(solution)/shard_map/ppermute | solution.py:21
  53.6 6.0 %collective-permute-start.11 = (bf16[384,256]{1,0:T(8,128)(2,1)}, bf16[384,256]{1,0:T(8,128)(2,1)}, u32[]{:S(2)}, u32[]{:S(2)}) collective-permute-start(bf16[384,256]{1,0:T(8,128)(2,1)} %get-tuple-element.79), channel_id=1, source_target_pairs={{0,6},{1,7},{2,4},{3,5},{4,2},{5,3},{6,0},{7,1},{8,14},{9,15},{10,... | collective-permute-start | bytes 589832 | tf_op jit(solution)/shard_map/ppermute | solution.py:21
  60.1 8.7 %attention_grads.3 = (bf16[192,1024]{1,0:T(8,128)(2,1)}, bf16[192,1024]{1,0:T(8,128)(2,1)}, f32[384,128]{1,0:T(8,128)}, bf16[768,128]{1,0:T(8,128)(2,1)}, bf16[3...) custom-call(s32[3]{0:T(128)} %pad_add_fusion.pos_ref, ...), custom_call_target="tpu_custom_call" | custom-call | flops 241591910400 | bytes 2359296 | tf_op jit(solution)/shard_map/attention_grads/pallas_call | solution.py:204
  71.2 4.8 %collective-permute-start.12 = (bf16[768,128]{1,0:T(8,128)(2,1)}, bf16[768,128]{1,0:T(8,128)(2,1)S(1)}, u32[]{:S(2)}, u32[]{:S(2)}) collective-permute-start(bf16[768,128]{1,0:T(8,128)(2,1)} %get-tuple-element.87), channel_id=1, source_target_pairs={{0,2},{1,3},{2,0},{3,1},{4,6},{5,7},{6,4},{7,5},{8,10},{9,11},{10,... | collective-permute-start | bytes 589832 | tf_op jit(solution)/shard_map/ppermute | solution.py:21
  76.2 1.5 %collective-permute-start.14 = (bf16[384,256]{1,0:T(8,128)(2,1)S(1)}, bf16[384,256]{1,0:T(8,128)(2,1)S(1)}, u32[]{:S(2)}, u32[]{:S(2)}) collective-permute-start(bf16[384,256]{1,0:T(8,128)(2,1)S(1)} %maximum_select_fusion.5.refs_0_), channel_id=1, source_target_pairs={{0,8},{8,0},{16,24},{24,16},{1,9},{9,1},{17,25},{25,17},{2,10},{10... | collective-permute-start | bytes 589832 | tf_op jit(solution)/shard_map/ppermute | solution.py:21
  77.8 1.5 %collective-permute-start.15 = (bf16[384,256]{1,0:T(8,128)(2,1)S(1)}, bf16[384,256]{1,0:T(8,128)(2,1)S(1)}, u32[]{:S(2)}, u32[]{:S(2)}) collective-permute-start(bf16[384,256]{1,0:T(8,128)(2,1)S(1)} %maximum_select_fusion.5.refs_0_), channel_id=1, source_target_pairs={{0,16},{8,24},{16,0},{24,8},{1,17},{9,25},{17,1},{25,9},{2,18},{10... | collective-permute-start | bytes 589832 | tf_op jit(solution)/shard_map/ppermute | solution.py:21
  79.3 2.7 %collective-permute-done.12 = bf16[768,128]{1,0:T(8,128)(2,1)S(1)} collective-permute-done((bf16[768,128]{1,0:T(8,128)(2,1)}, bf16[768,128]{1,0:T(8,128)(2,1)S(1)}, u32[]{:S(2)}, u32[]{:S(2)}) %collective-permute-start.12) | collective-permute-done | bytes 196640 | tf_op jit(solution)/shard_map/ppermute | solution.py:21
  82.0 2.4 %collective-permute-start.16 = (bf16[384,256]{1,0:T(8,128)(2,1)S(1)}, bf16[384,256]{1,0:T(8,128)(2,1)S(1)}, u32[]{:S(2)}, u32[]{:S(2)}) collective-permute-start(bf16[384,256]{1,0:T(8,128)(2,1)S(1)} %maximum_select_fusion.5.refs_0_), channel_id=1, source_target_pairs={{0,24},{8,16},{16,8},{24,0},{1,25},{9,17},{17,9},{25,1},{2,26},{10... | collective-permute-start | bytes 589832 | tf_op jit(solution)/shard_map/ppermute | solution.py:21
  86.0 10.5 %collective-permute-start.13 = (bf16[384,128]{1,0:T(8,128)(2,1)S(1)}, bf16[384,128]{1,0:T(8,128)(2,1)S(1)}, u32[]{:S(2)}, u32[]{:S(2)}) collective-permute-start(bf16[384,128]{1,0:T(8,128)(2,1)S(1)} %get-tuple-element.161), channel_id=1, source_target_pairs={{0,4},{1,5},{2,6},{3,7},{4,0},{5,1},{6,2},{7,3},{8,12},{9,13},{10,... | collective-permute-start | bytes 294920 | tf_op jit(solution)/shard_map/ppermute | solution.py:21
  96.6 4.8 %weight_products.3 = (bf16[1024,256]{1,0:T(8,128)(2,1)S(1)}, bf16[512,256]{1,0:T(8,128)(2,1)S(1)}, f32[512,256]{1,0:T(8,128)S(1)}) custom-call(s32[3]{0:T(128)S(1)} %copy-done, bf16[384,256]{1,0:T(8,128)(2,1)S(1)} %maximum_select_fusion.5.refs_0_, bf16[384,256]{1,0:T(8,128)(2,1)S(1)} %collective-permute-done.14.refs_1_, ...), custom_call_target="tpu_custom_call" | custom-call | flops 1 | bytes 1 | tf_op jit(solution)/shard_map/weight_products/pallas_call | solution.py:276
  101.4 2.8 %collective-permute-done.13 = bf16[384,128]{1,0:T(8,128)(2,1)S(1)} collective-permute-done((bf16[384,128]{1,0:T(8,128)(2,1)S(1)}, bf16[384,128]{1,0:T(8,128)(2,1)S(1)}, u32[]{:S(2)}, u32[]{:S(2)}) %collective-permute-start.13) | collective-permute-done | bytes 98336 | tf_op jit(solution)/shard_map/ppermute | solution.py:21
  104.3 1.5 %collective-permute-start.24 = (bf16[384,128]{1,0:T(8,128)(2,1)S(1)}, bf16[384,128]{1,0:T(8,128)(2,1)S(1)}, u32[]{:S(2)}, u32[]{:S(2)}) collective-permute-start(bf16[384,128]{1,0:T(8,128)(2,1)S(1)} %maximum_select_fusion.8.refs_0_), channel_id=1, source_target_pairs={{0,8},{8,0},{16,24},{24,16},{1,9},{9,1},{17,25},{25,17},{2,10},{10... | collective-permute-start | bytes 294920 | tf_op jit(solution)/shard_map/ppermute | solution.py:21
  105.9 1.5 %collective-permute-start.25 = (bf16[384,128]{1,0:T(8,128)(2,1)S(1)}, bf16[384,128]{1,0:T(8,128)(2,1)S(1)}, u32[]{:S(2)}, u32[]{:S(2)}) collective-permute-start(bf16[384,128]{1,0:T(8,128)(2,1)S(1)} %maximum_select_fusion.8.refs_0_), channel_id=1, source_target_pairs={{0,16},{8,24},{16,0},{24,8},{1,17},{9,25},{17,1},{25,9},{2,18},{10... | collective-permute-start | bytes 294920 | tf_op jit(solution)/shard_map/ppermute | solution.py:21
  108.0 1.5 %collective-permute-start.20 = (bf16[384,128]{1,0:T(8,128)(2,1)S(1)}, bf16[384,128]{1,0:T(8,128)(2,1)S(1)}, u32[]{:S(2)}, u32[]{:S(2)}) collective-permute-start(bf16[384,128]{1,0:T(8,128)(2,1)S(1)} %maximum_select_fusion.9.refs_0_), channel_id=1, source_target_pairs={{0,8},{8,0},{16,24},{24,16},{1,9},{9,1},{17,25},{25,17},{2,10},{10... | collective-permute-start | bytes 294920 | tf_op jit(solution)/shard_map/ppermute | solution.py:21
  109.5 1.5 %collective-permute-start.21 = (bf16[384,128]{1,0:T(8,128)(2,1)S(1)}, bf16[384,128]{1,0:T(8,128)(2,1)S(1)}, u32[]{:S(2)}, u32[]{:S(2)}) collective-permute-start(bf16[384,128]{1,0:T(8,128)(2,1)S(1)} %maximum_select_fusion.9.refs_0_), channel_id=1, source_target_pairs={{0,16},{8,24},{16,0},{24,8},{1,17},{9,25},{17,1},{25,9},{2,18},{10... | collective-permute-start | bytes 294920 | tf_op jit(solution)/shard_map/ppermute | solution.py:21
  113.1 4.4 %weight_products.4 = (bf16[1024,128]{1,0:T(8,128)(2,1)S(1)}, bf16[512,128]{1,0:T(8,128)(2,1)S(1)}, f32[512,128]{1,0:T(8,128)S(1)}) custom-call(s32[3]{0:T(128)S(1)} %copy-done, bf16[384,128]{1,0:T(8,128)(2,1)S(1)} %maximum_select_fusion.8.refs_0_, bf16[384,128]{1,0:T(8,128)(2,1)S(1)} %collective-permute-done.24.refs_1_, ...), custom_call_target="tpu_custom_call" | custom-call | flops 1 | bytes 1 | tf_op jit(solution)/shard_map/weight_products/pallas_call | solution.py:276
  118.4 3.1 %collective-permute-done.23 = bf16[1024,256]{1,0:T(8,128)(2,1)S(1)} collective-permute-done((bf16[1024,256]{1,0:T(8,128)(2,1)S(1)}, bf16[1024,256]{1,0:T(8,128)(2,1)S(1)}, u32[]{:S(2)}, u32[]{:S(2)}) %collective-permute-start.23) | collective-permute-done | bytes 524320 | tf_op jit(solution)/shard_map/ppermute | solution.py:21
  121.6 2.7 %collective-permute-start.29 = (bf16[512,256]{1,0:T(8,128)(2,1)S(1)}, bf16[512,256]{1,0:T(8,128)(2,1)S(1)}, u32[]{:S(2)}, u32[]{:S(2)}) collective-permute-start(bf16[512,256]{1,0:T(8,128)(2,1)S(1)} %get-tuple-element.141), channel_id=1, source_target_pairs={{0,4},{1,5},{2,6},{3,7},{4,0},{5,1},{6,2},{7,3},{8,12},{9,13},{10,... | collective-permute-start | bytes 786440 | tf_op jit(solution)/shard_map/ppermute | solution.py:21
  124.3 4.4 %weight_products.5 = (bf16[1024,128]{1,0:T(8,128)(2,1)S(1)}, bf16[512,128]{1,0:T(8,128)(2,1)S(1)}, f32[512,128]{1,0:T(8,128)S(1)}) custom-call(s32[3]{0:T(128)S(1)} %copy-done, bf16[384,128]{1,0:T(8,128)(2,1)S(1)} %maximum_select_fusion.9.refs_0_, bf16[384,128]{1,0:T(8,128)(2,1)S(1)} %collective-permute-done.20.refs_1_, ...), custom_call_target="tpu_custom_call" | custom-call | flops 1 | bytes 1 | tf_op jit(solution)/shard_map/weight_products/pallas_call | solution.py:276
  128.7 3.0 %collective-permute-start.31 = (bf16[1024,128]{1,0:T(8,128)(2,1)S(1)}, bf16[1024,128]{1,0:T(8,128)(2,1)S(1)}, u32[]{:S(2)}, u32[]{:S(2)}) collective-permute-start(bf16[1024,128]{1,0:T(8,128)(2,1)S(1)} %get-tuple-element.128), channel_id=1, source_target_pairs={{0,2},{1,3},{2,0},{3,1},{4,6},{5,7},{6,4},{7,5},{8,10},{9,11},{10,... | collective-permute-start | bytes 786440 | tf_op jit(solution)/shard_map/ppermute | solution.py:21
  131.8 2.0 %collective-permute-start.33 = (bf16[512,128]{1,0:T(8,128)(2,1)S(1)}, bf16[512,128]{1,0:T(8,128)(2,1)S(1)}, u32[]{:S(2)}, u32[]{:S(2)}) collective-permute-start(bf16[512,128]{1,0:T(8,128)(2,1)S(1)} %get-tuple-element.151), channel_id=1, source_target_pairs={{0,4},{1,5},{2,6},{3,7},{4,0},{5,1},{6,2},{7,3},{8,12},{9,13},{10,... | collective-permute-start | bytes 393224 | tf_op jit(solution)/shard_map/ppermute | solution.py:21
  136.9 2.4 %collective-permute-done.31 = bf16[1024,128]{1,0:T(8,128)(2,1)S(1)} collective-permute-done((bf16[1024,128]{1,0:T(8,128)(2,1)S(1)}, bf16[1024,128]{1,0:T(8,128)(2,1)S(1)}, u32[]{:S(2)}, u32[]{:S(2)}) %collective-permute-start.31) | collective-permute-done | bytes 262176 | tf_op jit(solution)/shard_map/ppermute | solution.py:21
  139.3 1.6 %collective-permute-start.32 = (bf16[512,128]{1,0:T(8,128)(2,1)S(1)}, bf16[512,128]{1,0:T(8,128)(2,1)S(1)}, u32[]{:S(2)}, u32[]{:S(2)}) collective-permute-start(bf16[512,128]{1,0:T(8,128)(2,1)S(1)} %get-tuple-element.149), channel_id=1, source_target_pairs={{0,4},{1,5},{2,6},{3,7},{4,0},{5,1},{6,2},{7,3},{8,12},{9,13},{10,... | collective-permute-start | bytes 393224 | tf_op jit(solution)/shard_map/ppermute | solution.py:21
  143.6 1.7 %maximum_select_fusion = bf16[192,4096]{1,0:T(8,128)(2,1)} fusion(bf16[192,2048]{1,0:T(8,128)(2,1)S(1)} %collective-permute-done.27, bf16[192,1024]{1,0:T(8,128)(2,1)S(1)} %copy-done.8, bf16[192,1024]{1,0:T(8,128)(2,1)S(1)} %copy-done.7, pred[]{:T(512)S(6)} %eq.5), kind=kLoop, calls=%fused_computation.1 | loop fusion | flops 10223616 | bytes 3145729 | tf_op jit(solution)/shard_map/jit(_where)/select_n | solution.py:322
  145.3 2.8 %collective-permute-done.32 = bf16[512,128]{1,0:T(8,128)(2,1)S(1)} collective-permute-done((bf16[512,128]{1,0:T(8,128)(2,1)S(1)}, bf16[512,128]{1,0:T(8,128)(2,1)S(1)}, u32[]{:S(2)}, u32[]{:S(2)}) %collective-permute-start.32) | collective-permute-done | bytes 131104 | tf_op jit(solution)/shard_map/ppermute | solution.py:21
  (126 shorter events, 26.5 us)
Async XLA Ops:
  5.6 28.3 %collective-permute-start.1 = (bf16[192,2048]{1,0:T(8,128)(2,1)S(1)}, bf16[192,2048]{1,0:T(8,128)(2,1)S(1)}, u32[]{:S(2)}, u32[]{:S(2)}) collective-permute-start(bf16[192,2048]{1,0:T(8,128)(2,1)S(1)} %pad_maximum_fusion), channel_id=1, source_target_pairs={{0,1},{1,0},{2,3},{3,2},{4,5},{5,4},{6,7},{7,6},{8,9},{9,8},{10,11... | collective-permute-start | bytes 2359304 | tf_op jit(solution)/shard_map/ppermute | solution.py:21
  6.0 22.9 %collective-permute-start.2 = (bf16[384,256]{1,0:T(8,128)(2,1)S(1)}, bf16[384,256]{1,0:T(8,128)(2,1)S(1)}, u32[]{:S(2)}, u32[]{:S(2)}) collective-permute-start(bf16[384,256]{1,0:T(8,128)(2,1)S(1)} %maximum_select_fusion.3.refs_0_), channel_id=1, source_target_pairs={{0,2},{1,3},{2,0},{3,1},{4,6},{5,7},{6,4},{7,5},{8,10},{9,11},{10,... | collective-permute-start | bytes 589832 | tf_op jit(solution)/shard_map/ppermute | solution.py:21
  10.9 12.0 %collective-permute-start.3 = (bf16[384,256]{1,0:T(8,128)(2,1)S(1)}, bf16[384,256]{1,0:T(8,128)(2,1)S(1)}, u32[]{:S(2)}, u32[]{:S(2)}) collective-permute-start(bf16[384,256]{1,0:T(8,128)(2,1)S(1)} %maximum_select_fusion.3.refs_0_), channel_id=1, source_target_pairs={{0,4},{1,5},{2,6},{3,7},{4,0},{5,1},{6,2},{7,3},{8,12},{9,13},{10,... | collective-permute-start | bytes 589832 | tf_op jit(solution)/shard_map/ppermute | solution.py:21
  22.9 6.1 %collective-permute-start.4 = (bf16[384,256]{1,0:T(8,128)(2,1)S(1)}, bf16[384,256]{1,0:T(8,128)(2,1)S(1)}, u32[]{:S(2)}, u32[]{:S(2)}) collective-permute-start(bf16[384,256]{1,0:T(8,128)(2,1)S(1)} %collective-permute-done.3.refs_2_), channel_id=1, source_target_pairs={{0,2},{1,3},{2,0},{3,1},{4,6},{5,7},{6,4},{7,5},{8,10},{9,11},{10,... | collective-permute-start | bytes 589832 | tf_op jit(solution)/shard_map/ppermute | solution.py:21
  24.2 35.9 %collective-permute-start.5 = (bf16[192,2048]{1,0:T(8,128)(2,1)}, bf16[192,2048]{1,0:T(8,128)(2,1)}, u32[]{:S(2)}, u32[]{:S(2)}) collective-permute-start(bf16[192,2048]{1,0:T(8,128)(2,1)} %pad_maximum_fusion.1), channel_id=1, source_target_pairs={{0,1},{1,0},{2,3},{3,2},{4,5},{5,4},{6,7},{7,6},{8,9},{9,8},{10,11... | collective-permute-start | bytes 2359304 | tf_op jit(solution)/shard_map/ppermute | solution.py:21
  24.2 46.9 %all-to-all-start = ((bf16[4,192,2048]{2,1,0:T(8,128)(2,1)}), bf16[4,192,2048]{2,1,0:T(8,128)(2,1)}, u32[]{:S(2)}, u32[]{:S(2)}) async-start(bf16[4,192,2048]{2,1,0:T(8,128)(2,1)} %bitcast.10), calls=%async_computation | async-start | bytes 6291456 | tf_op jit(solution)/shard_map/all_to_all | solution.py:397
  29.0 24.6 %collective-permute-start.6 = (bf16[384,256]{1,0:T(8,128)(2,1)}, bf16[384,256]{1,0:T(8,128)(2,1)}, u32[]{:S(2)}, u32[]{:S(2)}) collective-permute-start(bf16[384,256]{1,0:T(8,128)(2,1)} %maximum_select_fusion.4.refs_0_), channel_id=1, source_target_pairs={{0,2},{1,3},{2,0},{3,1},{4,6},{5,7},{6,4},{7,5},{8,10},{9,11},{10,... | collective-permute-start | bytes 589832 | tf_op jit(solution)/shard_map/ppermute | solution.py:21
  30.4 29.2 %collective-permute-start.7 = (bf16[384,256]{1,0:T(8,128)(2,1)}, bf16[384,256]{1,0:T(8,128)(2,1)}, u32[]{:S(2)}, u32[]{:S(2)}) collective-permute-start(bf16[384,256]{1,0:T(8,128)(2,1)} %maximum_select_fusion.4.refs_0_), channel_id=1, source_target_pairs={{0,4},{1,5},{2,6},{3,7},{4,0},{5,1},{6,2},{7,3},{8,12},{9,13},{10,... | collective-permute-start | bytes 589832 | tf_op jit(solution)/shard_map/ppermute | solution.py:21
  33.8 26.4 %collective-permute-start.8 = (bf16[384,256]{1,0:T(8,128)(2,1)}, bf16[384,256]{1,0:T(8,128)(2,1)}, u32[]{:S(2)}, u32[]{:S(2)}) collective-permute-start(bf16[384,256]{1,0:T(8,128)(2,1)} %maximum_select_fusion.4.refs_0_), channel_id=1, source_target_pairs={{0,6},{1,7},{2,4},{3,5},{4,2},{5,3},{6,0},{7,1},{8,14},{9,15},{10,... | collective-permute-start | bytes 589832 | tf_op jit(solution)/shard_map/ppermute | solution.py:21
  43.3 25.6 %collective-permute-start.10 = (bf16[384,256]{1,0:T(8,128)(2,1)}, bf16[384,256]{1,0:T(8,128)(2,1)}, u32[]{:S(2)}, u32[]{:S(2)}) collective-permute-start(bf16[384,256]{1,0:T(8,128)(2,1)} %get-tuple-element.78), channel_id=1, source_target_pairs={{0,4},{1,5},{2,6},{3,7},{4,0},{5,1},{6,2},{7,3},{8,12},{9,13},{10,... | collective-permute-start | bytes 589832 | tf_op jit(solution)/shard_map/ppermute | solution.py:21
  53.6 16.3 %collective-permute-start.11 = (bf16[384,256]{1,0:T(8,128)(2,1)}, bf16[384,256]{1,0:T(8,128)(2,1)}, u32[]{:S(2)}, u32[]{:S(2)}) collective-permute-start(bf16[384,256]{1,0:T(8,128)(2,1)} %get-tuple-element.79), channel_id=1, source_target_pairs={{0,6},{1,7},{2,4},{3,5},{4,2},{5,3},{6,0},{7,1},{8,14},{9,15},{10,... | collective-permute-start | bytes 589832 | tf_op jit(solution)/shard_map/ppermute | solution.py:21
  59.6 10.3 %collective-permute-start.9 = (bf16[384,256]{1,0:T(8,128)(2,1)}, bf16[384,256]{1,0:T(8,128)(2,1)}, u32[]{:S(2)}, u32[]{:S(2)}) collective-permute-start(bf16[384,256]{1,0:T(8,128)(2,1)} %get-tuple-element.77), channel_id=1, source_target_pairs={{0,2},{1,3},{2,0},{3,1},{4,6},{5,7},{6,4},{7,5},{8,10},{9,11},{10,... | collective-permute-start | bytes 589832 | tf_op jit(solution)/shard_map/ppermute | solution.py:21
  71.1 25.5 %collective-permute-start.18 = (bf16[768,2048]{1,0:T(8,128)(2,1)}, bf16[768,2048]{1,0:T(8,128)(2,1)S(1)}, u32[]{:S(2)}, u32[]{:S(2)}) collective-permute-start(bf16[768,2048]{1,0:T(8,128)(2,1)} %bitcast.4.refs_4_), channel_id=1, source_target_pairs={{0,1},{1,0},{2,3},{3,2},{4,5},{5,4},{6,7},{7,6},{8,9},{9,8},{10,11... | collective-permute-start | bytes 9437192 | tf_op jit(solution)/shard_map/ppermute | solution.py:21
  71.2 10.8 %collective-permute-start.12 = (bf16[768,128]{1,0:T(8,128)(2,1)}, bf16[768,128]{1,0:T(8,128)(2,1)S(1)}, u32[]{:S(2)}, u32[]{:S(2)}) collective-permute-start(bf16[768,128]{1,0:T(8,128)(2,1)} %get-tuple-element.87), channel_id=1, source_target_pairs={{0,2},{1,3},{2,0},{3,1},{4,6},{5,7},{6,4},{7,5},{8,10},{9,11},{10,... | collective-permute-start | bytes 589832 | tf_op jit(solution)/shard_map/ppermute | solution.py:21
  76.0 9.9 %collective-permute-start.17 = (bf16[768,128]{1,0:T(8,128)(2,1)}, bf16[768,128]{1,0:T(8,128)(2,1)S(1)}, u32[]{:S(2)}, u32[]{:S(2)}) collective-permute-start(bf16[768,128]{1,0:T(8,128)(2,1)} %get-tuple-element.90), channel_id=1, source_target_pairs={{0,2},{1,3},{2,0},{3,1},{4,6},{5,7},{6,4},{7,5},{8,10},{9,11},{10,... | collective-permute-start | bytes 589832 | tf_op jit(solution)/shard_map/ppermute | solution.py:21
  76.2 20.3 %collective-permute-start.14 = (bf16[384,256]{1,0:T(8,128)(2,1)S(1)}, bf16[384,256]{1,0:T(8,128)(2,1)S(1)}, u32[]{:S(2)}, u32[]{:S(2)}) collective-permute-start(bf16[384,256]{1,0:T(8,128)(2,1)S(1)} %maximum_select_fusion.5.refs_0_), channel_id=1, source_target_pairs={{0,8},{8,0},{16,24},{24,16},{1,9},{9,1},{17,25},{25,17},{2,10},{10... | collective-permute-start | bytes 589832 | tf_op jit(solution)/shard_map/ppermute | solution.py:21
  77.8 18.8 %collective-permute-start.15 = (bf16[384,256]{1,0:T(8,128)(2,1)S(1)}, bf16[384,256]{1,0:T(8,128)(2,1)S(1)}, u32[]{:S(2)}, u32[]{:S(2)}) collective-permute-start(bf16[384,256]{1,0:T(8,128)(2,1)S(1)} %maximum_select_fusion.5.refs_0_), channel_id=1, source_target_pairs={{0,16},{8,24},{16,0},{24,8},{1,17},{9,25},{17,1},{25,9},{2,18},{10... | collective-permute-start | bytes 589832 | tf_op jit(solution)/shard_map/ppermute | solution.py:21
  82.0 14.6 %collective-permute-start.16 = (bf16[384,256]{1,0:T(8,128)(2,1)S(1)}, bf16[384,256]{1,0:T(8,128)(2,1)S(1)}, u32[]{:S(2)}, u32[]{:S(2)}) collective-permute-start(bf16[384,256]{1,0:T(8,128)(2,1)S(1)} %maximum_select_fusion.5.refs_0_), channel_id=1, source_target_pairs={{0,24},{8,16},{16,8},{24,0},{1,25},{9,17},{17,9},{25,1},{2,26},{10... | collective-permute-start | bytes 589832 | tf_op jit(solution)/shard_map/ppermute | solution.py:21
  86.0 18.3 %collective-permute-start.13 = (bf16[384,128]{1,0:T(8,128)(2,1)S(1)}, bf16[384,128]{1,0:T(8,128)(2,1)S(1)}, u32[]{:S(2)}, u32[]{:S(2)}) collective-permute-start(bf16[384,128]{1,0:T(8,128)(2,1)S(1)} %get-tuple-element.161), channel_id=1, source_target_pairs={{0,4},{1,5},{2,6},{3,7},{4,0},{5,1},{6,2},{7,3},{8,12},{9,13},{10,... | collective-permute-start | bytes 294920 | tf_op jit(solution)/shard_map/ppermute | solution.py:21
  96.5 11.4 %collective-permute-start.19 = (bf16[384,128]{1,0:T(8,128)(2,1)S(1)}, bf16[384,128]{1,0:T(8,128)(2,1)S(1)}, u32[]{:S(2)}, u32[]{:S(2)}) collective-permute-start(bf16[384,128]{1,0:T(8,128)(2,1)S(1)} %get-tuple-element.159), channel_id=1, source_target_pairs={{0,4},{1,5},{2,6},{3,7},{4,0},{5,1},{6,2},{7,3},{8,12},{9,13},{10,... | collective-permute-start | bytes 294920 | tf_op jit(solution)/shard_map/ppermute | solution.py:21
  104.3 5.2 %collective-permute-start.24 = (bf16[384,128]{1,0:T(8,128)(2,1)S(1)}, bf16[384,128]{1,0:T(8,128)(2,1)S(1)}, u32[]{:S(2)}, u32[]{:S(2)}) collective-permute-start(bf16[384,128]{1,0:T(8,128)(2,1)S(1)} %maximum_select_fusion.8.refs_0_), channel_id=1, source_target_pairs={{0,8},{8,0},{16,24},{24,16},{1,9},{9,1},{17,25},{25,17},{2,10},{10... | collective-permute-start | bytes 294920 | tf_op jit(solution)/shard_map/ppermute | solution.py:21
  107.4 5.7 %collective-permute-start.26 = (bf16[384,128]{1,0:T(8,128)(2,1)S(1)}, bf16[384,128]{1,0:T(8,128)(2,1)S(1)}, u32[]{:S(2)}, u32[]{:S(2)}) collective-permute-start(bf16[384,128]{1,0:T(8,128)(2,1)S(1)} %maximum_select_fusion.8.refs_0_), channel_id=1, source_target_pairs={{0,24},{8,16},{16,8},{24,0},{1,25},{9,17},{17,9},{25,1},{2,26},{10... | collective-permute-start | bytes 294920 | tf_op jit(solution)/shard_map/ppermute | solution.py:21
  107.9 13.6 %collective-permute-start.23 = (bf16[1024,256]{1,0:T(8,128)(2,1)S(1)}, bf16[1024,256]{1,0:T(8,128)(2,1)S(1)}, u32[]{:S(2)}, u32[]{:S(2)}) collective-permute-start(bf16[1024,256]{1,0:T(8,128)(2,1)S(1)} %get-tuple-element.104), channel_id=1, source_target_pairs={{0,2},{1,3},{2,0},{3,1},{4,6},{5,7},{6,4},{7,5},{8,10},{9,11},{10,... | collective-permute-start | bytes 1572872 | tf_op jit(solution)/shard_map/ppermute | solution.py:21
  108.0 16.3 %collective-permute-start.20 = (bf16[384,128]{1,0:T(8,128)(2,1)S(1)}, bf16[384,128]{1,0:T(8,128)(2,1)S(1)}, u32[]{:S(2)}, u32[]{:S(2)}) collective-permute-start(bf16[384,128]{1,0:T(8,128)(2,1)S(1)} %maximum_select_fusion.9.refs_0_), channel_id=1, source_target_pairs={{0,8},{8,0},{16,24},{24,16},{1,9},{9,1},{17,25},{25,17},{2,10},{10... | collective-permute-start | bytes 294920 | tf_op jit(solution)/shard_map/ppermute | solution.py:21
  109.5 14.8 %collective-permute-start.21 = (bf16[384,128]{1,0:T(8,128)(2,1)S(1)}, bf16[384,128]{1,0:T(8,128)(2,1)S(1)}, u32[]{:S(2)}, u32[]{:S(2)}) collective-permute-start(bf16[384,128]{1,0:T(8,128)(2,1)S(1)} %maximum_select_fusion.9.refs_0_), channel_id=1, source_target_pairs={{0,16},{8,24},{16,0},{24,8},{1,17},{9,25},{17,1},{25,9},{2,18},{10... | collective-permute-start | bytes 294920 | tf_op jit(solution)/shard_map/ppermute | solution.py:21
  111.1 13.2 %collective-permute-start.22 = (bf16[384,128]{1,0:T(8,128)(2,1)S(1)}, bf16[384,128]{1,0:T(8,128)(2,1)S(1)}, u32[]{:S(2)}, u32[]{:S(2)}) collective-permute-start(bf16[384,128]{1,0:T(8,128)(2,1)S(1)} %maximum_select_fusion.9.refs_0_), channel_id=1, source_target_pairs={{0,24},{8,16},{16,8},{24,0},{1,25},{9,17},{17,9},{25,1},{2,26},{10... | collective-permute-start | bytes 294920 | tf_op jit(solution)/shard_map/ppermute | solution.py:21
  117.4 14.3 %collective-permute-start.30 = (bf16[1024,128]{1,0:T(8,128)(2,1)S(1)}, bf16[1024,128]{1,0:T(8,128)(2,1)S(1)}, u32[]{:S(2)}, u32[]{:S(2)}) collective-permute-start(bf16[1024,128]{1,0:T(8,128)(2,1)S(1)} %get-tuple-element.115), channel_id=1, source_target_pairs={{0,2},{1,3},{2,0},{3,1},{4,6},{5,7},{6,4},{7,5},{8,10},{9,11},{10,... | collective-permute-start | bytes 786440 | tf_op jit(solution)/shard_map/ppermute | solution.py:21
  121.6 15.2 %collective-permute-start.29 = (bf16[512,256]{1,0:T(8,128)(2,1)S(1)}, bf16[512,256]{1,0:T(8,128)(2,1)S(1)}, u32[]{:S(2)}, u32[]{:S(2)}) collective-permute-start(bf16[512,256]{1,0:T(8,128)(2,1)S(1)} %get-tuple-element.141), channel_id=1, source_target_pairs={{0,4},{1,5},{2,6},{3,7},{4,0},{5,1},{6,2},{7,3},{8,12},{9,13},{10,... | collective-permute-start | bytes 786440 | tf_op jit(solution)/shard_map/ppermute | solution.py:21
  128.7 10.6 %collective-permute-start.31 = (bf16[1024,128]{1,0:T(8,128)(2,1)S(1)}, bf16[1024,128]{1,0:T(8,128)(2,1)S(1)}, u32[]{:S(2)}, u32[]{:S(2)}) collective-permute-start(bf16[1024,128]{1,0:T(8,128)(2,1)S(1)} %get-tuple-element.128), channel_id=1, source_target_pairs={{0,2},{1,3},{2,0},{3,1},{4,6},{5,7},{6,4},{7,5},{8,10},{9,11},{10,... | collective-permute-start | bytes 786440 | tf_op jit(solution)/shard_map/ppermute | solution.py:21
  131.8 9.1 %collective-permute-start.33 = (bf16[512,128]{1,0:T(8,128)(2,1)S(1)}, bf16[512,128]{1,0:T(8,128)(2,1)S(1)}, u32[]{:S(2)}, u32[]{:S(2)}) collective-permute-start(bf16[512,128]{1,0:T(8,128)(2,1)S(1)} %get-tuple-element.151), channel_id=1, source_target_pairs={{0,4},{1,5},{2,6},{3,7},{4,0},{5,1},{6,2},{7,3},{8,12},{9,13},{10,... | collective-permute-start | bytes 393224 | tf_op jit(solution)/shard_map/ppermute | solution.py:21
  134.0 9.6 %collective-permute-start.27 = (bf16[192,2048]{1,0:T(8,128)(2,1)S(1)}, bf16[192,2048]{1,0:T(8,128)(2,1)S(1)}, u32[]{:S(2)}, u32[]{:S(2)}) collective-permute-start(bf16[192,2048]{1,0:T(8,128)(2,1)S(1)} %pad_maximum_fusion.2), channel_id=1, source_target_pairs={{0,1},{1,0},{2,3},{3,2},{4,5},{5,4},{6,7},{7,6},{8,9},{9,8},{10,11... | collective-permute-start | bytes 2359304 | tf_op jit(solution)/shard_map/ppermute | solution.py:21
  139.3 8.7 %collective-permute-start.32 = (bf16[512,128]{1,0:T(8,128)(2,1)S(1)}, bf16[512,128]{1,0:T(8,128)(2,1)S(1)}, u32[]{:S(2)}, u32[]{:S(2)}) collective-permute-start(bf16[512,128]{1,0:T(8,128)(2,1)S(1)} %get-tuple-element.149), channel_id=1, source_target_pairs={{0,4},{1,5},{2,6},{3,7},{4,0},{5,1},{6,2},{7,3},{8,12},{9,13},{10,... | collective-permute-start | bytes 393224 | tf_op jit(solution)/shard_map/ppermute | solution.py:21
  (22 other events, 146.2 us)

commit v4 on v3

--- a/solution.py
+++ b/solution.py
@@ -391,7 +391,7 @@
     shares = hidden_.reshape(tok, n_dp, share).transpose(1, 0, 2)
     slots = doubling({0: kv_local[0]}, far_first[:-1])
     near = across(kv_local[0], 1)
-    forward = {s: after(slots[s], rx, rx1, shares) for s in range(2, chips, 2)}
+    forward = {s: after(slots[s], rx, shares) for s in range(2, chips, 2)}
     slots |= {1: near} | {s ^ 1: across(x, 1) for s, x in forward.items()}
     rx, rx1 = swap(rx), swap(rx1)
     hidden_own = lax.all_to_all(shares, "dp", split_axis=0, concat_axis=0, tiled=True)
@@ -405,13 +405,13 @@
     )
 
     moved = [blocks[0]] + [across(blocks[s], s) for s in range(1, chips)]
-    rx1, parts1 = after((rx1, parts1), blocks)
+    rx1, parts1, hidden_own = after((rx1, parts1, hidden_own), blocks)
+    hidden_oth = swap(hidden_own)
     dq_own1, dq_oth1, *blocks1 = attention(
         pos, queries, out_grad, rx1, parts1, packing, 1, False
     )
     one = sum(x.astype(F32) for x in after(moved, blocks1))
-    hidden_own, dq_oth = after((hidden_own, dq_oth), one)
-    hidden_oth = swap(hidden_own)
+    hidden_oth, dq_oth = after((hidden_oth, dq_oth), one)
 
     total = own_first(one.astype(BF16))
     slots = over_sequences(total)
@@ -436,10 +436,10 @@
     )
     for i in range(bits - 1):
         product_v = step(*product_v, i, product_k)
-    product = step(*product, bits - 1, product_v)
     for i in range(bits - 1):
-        product_k = step(*product_k, i, product)
-    product_v = step(*product_v, bits - 1, product_k)
+        product_k = step(*product_k, i, product_v)
+    product = step(*product, bits - 1, product_k)
+    product_v = step(*product_v, bits - 1, product)
 
     def spread(one, two, lo):
         return in_order(*(jnp.concatenate([x[:, lo : lo + HD], y], 1) for x, y in zip(one, two)), 1)

time: 151 us -> 148 us (0.980)
  waiting for transfers between devices: 29.3 us -> 21.6 us
  Pallas kernels: 30.8 us -> 33.6 us
    ppermute x37, waiting for transfers between devices: 29.3 us -> 21.6 us  [xor_permute(): return lax.ppermute(array, axis, [(i, i ^ mask) for i in range(size)])]
    pallas_call x3, Pallas kernels: 13.6 us -> 16.5 us  [weight_products(): pl.pallas_call(functools.partial(product_kernel, chips, n_dp, span // PAI...]
    dynamic_slice x3, local copies, waits for them, and re-layouts: 1.25 us -> 3.24 us  [columns(): return lax.dynamic_slice_in_dim(x, head * size, size, 1)]
  transfers between devices with their start and end apart: 38 -> 38, of which waited for: 14 -> 14; matrix products, arithmetic and copies ran while one was open for 7% -> 6% of each run, Pallas kernels for 20% -> 23%
where the time goes in v4:
time: 148 us; the launch traced here: 147 us
  starting transfers between devices  74.7 us (50%)
  Pallas kernels  33.6 us (23%)
  waiting for transfers between devices  21.6 us (15%)
  other arithmetic  10.8 us (7%)
  local copies, waits for them, and re-layouts  5.44 us (4%)
    ppermute x37, starting transfers between devices, xor_permute(): return lax.ppermute(array, axis, [(i, i ^ mask) for i in range(size)])  69.8 us
    ppermute x37, waiting for transfers between devices, xor_permute(): return lax.ppermute(array, axis, [(i, i ^ mask) for i in range(size)])  21.6 us
    pallas_call x2, Pallas kernels, attention(): pl.pallas_call(functools.partial(attention_kernel, chips, tok, group, hea...  17.2 us
    pallas_call x3, Pallas kernels, weight_products(): pl.pallas_call(functools.partial(product_kernel, chips, n_dp, span // PAI...  16.5 us
    select_n x7, other arithmetic, in_order(): jnp.where(first, jnp.concatenate([mine, theirs], axis), jnp.concatenate([...  6.36 us
    all_to_all x1, starting transfers between devices, on_device(): lax.all_to_all(shares, 'dp', split_axis=0, concat_axis=0, tiled=True)  4.83 us
    dynamic_slice x3, local copies, waits for them, and re-layouts, columns(): return lax.dynamic_slice_in_dim(x, head * size, size, 1)  3.24 us
  transfers between devices with their start and end apart: 38, of which 14 were waited for; matrix products, arithmetic and copies ran while one was open for 6% of the time, Pallas kernels for 23%

profile of v4, /device:TPU:0, one launch (start us, length us, event | category | flops | bytes accessed | tf_op | source)
XLA Modules:
  0.0 147.2 jit_solution(2434774561345233217)
XLA Ops:
  5.0 2.1 %constant_dynamic-slice_fusion.6 = (bf16[192,1024]{1,0:T(8,128)(2,1)}, bf16[192,1024]{1,0:T(8,128)(2,1)S(1)}) fusion(bf16[192,4096]{1,0:T(8,128)(2,1)} %g_own.3, s32[]{:T(128)S(6)} %select_n.112, s32[]{:T(128)S(6)} %select_n.111), kind=kLoop, calls=%fused_computation.38 | loop fusion | bytes 1572872 | tf_op jit(solution)/shard_map/dynamic_slice | solution.py:329
  8.4 3.7 %collective-permute-start.3 = (bf16[384,256]{1,0:T(8,128)(2,1)}, bf16[384,256]{1,0:T(8,128)(2,1)}, u32[]{:S(2)}, u32[]{:S(2)}) collective-permute-start(bf16[384,256]{1,0:T(8,128)(2,1)} %maximum_select_fusion.3.refs_0_), channel_id=1, source_target_pairs={{0,4},{1,5},{2,6},{3,7},{4,0},{5,1},{6,2},{7,3},{8,12},{9,13},{10,... | collective-permute-start | bytes 589832 | tf_op jit(solution)/shard_map/ppermute | solution.py:21
  12.8 1.6 %collective-permute-start.2 = (bf16[384,256]{1,0:T(8,128)(2,1)}, bf16[384,256]{1,0:T(8,128)(2,1)}, u32[]{:S(2)}, u32[]{:S(2)}) collective-permute-start(bf16[384,256]{1,0:T(8,128)(2,1)} %maximum_select_fusion.3.refs_0_), channel_id=1, source_target_pairs={{0,2},{1,3},{2,0},{3,1},{4,6},{5,7},{6,4},{7,5},{8,10},{9,11},{10,... | collective-permute-start | bytes 589832 | tf_op jit(solution)/shard_map/ppermute | solution.py:21
  14.4 1.9 %copy.13 = bf16[24,4,8,2048]{3,2,0,1:T(8,128)(2,1)} copy(bf16[24,4,8,2048]{3,2,1,0:T(8,128)(2,1)S(1)} %bitcast.11) | data formatting | bytes 6291456 | tf_op jit(solution)/shard_map/reshape | solution.py:391
  16.3 4.8 %all-to-all-start = ((bf16[4,192,2048]{2,1,0:T(8,128)(2,1)}), bf16[4,192,2048]{2,1,0:T(8,128)(2,1)}, u32[]{:S(2)}, u32[]{:S(2)}) async-start(bf16[4,192,2048]{2,1,0:T(8,128)(2,1)} %bitcast.10), calls=%async_computation | async-start | bytes 6291456 | tf_op jit(solution)/shard_map/all_to_all | solution.py:397
  23.8 5.2 %collective-permute-done.4.refs_3_ = bf16[384,256]{1,0:T(8,128)(2,1)S(1)} collective-permute-done((bf16[384,256]{1,0:T(8,128)(2,1)}, bf16[384,256]{1,0:T(8,128)(2,1)S(1)}, u32[]{:S(2)}, u32[]{:S(2)}) %collective-permute-start.4) | collective-permute-done | bytes 196640 | tf_op jit(solution)/shard_map/ppermute | solution.py:21
  29.9 3.4 %collective-permute-start.7 = (bf16[384,256]{1,0:T(8,128)(2,1)}, bf16[384,256]{1,0:T(8,128)(2,1)}, u32[]{:S(2)}, u32[]{:S(2)}) collective-permute-start(bf16[384,256]{1,0:T(8,128)(2,1)} %maximum_select_fusion.4.refs_0_), channel_id=1, source_target_pairs={{0,4},{1,5},{2,6},{3,7},{4,0},{5,1},{6,2},{7,3},{8,12},{9,13},{10,... | collective-permute-start | bytes 589832 | tf_op jit(solution)/shard_map/ppermute | solution.py:21
  33.4 8.5 %attention_grads.2 = (bf16[192,1024]{1,0:T(8,128)(2,1)}, bf16[192,1024]{1,0:T(8,128)(2,1)}, f32[384,256]{1,0:T(8,128)}, bf16[384,256]{1,0:T(8,128)(2,1)}, bf16[3...) custom-call(s32[3]{0:T(128)} %pad_add_fusion.pos_ref, bf16[192,4096]{1,0:T(8,128)(2,1)} %q_own.3, bf16[192,4096]{1,0:T(8,128)(2,1)} %g_own.3, ...), custom_call_target="tpu_custom_call" | custom-call | flops 241591910400 | bytes 2359296 | tf_op jit(solution)/shard_map/attention_grads/pallas_call | solution.py:204
  41.8 9.9 %collective-permute-start.10 = (bf16[384,256]{1,0:T(8,128)(2,1)}, bf16[384,256]{1,0:T(8,128)(2,1)}, u32[]{:S(2)}, u32[]{:S(2)}) collective-permute-start(bf16[384,256]{1,0:T(8,128)(2,1)} %get-tuple-element.79), channel_id=1, source_target_pairs={{0,4},{1,5},{2,6},{3,7},{4,0},{5,1},{6,2},{7,3},{8,12},{9,13},{10,... | collective-permute-start | bytes 589832 | tf_op jit(solution)/shard_map/ppermute | solution.py:21
  51.8 6.4 %collective-permute-start.11 = (bf16[384,256]{1,0:T(8,128)(2,1)}, bf16[384,256]{1,0:T(8,128)(2,1)}, u32[]{:S(2)}, u32[]{:S(2)}) collective-permute-start(bf16[384,256]{1,0:T(8,128)(2,1)} %get-tuple-element.80), channel_id=1, source_target_pairs={{0,6},{1,7},{2,4},{3,5},{4,2},{5,3},{6,0},{7,1},{8,14},{9,15},{10,... | collective-permute-start | bytes 589832 | tf_op jit(solution)/shard_map/ppermute | solution.py:21
  58.8 8.7 %attention_grads.3 = (bf16[192,1024]{1,0:T(8,128)(2,1)}, bf16[192,1024]{1,0:T(8,128)(2,1)}, f32[384,128]{1,0:T(8,128)}, bf16[768,128]{1,0:T(8,128)(2,1)}, bf16[3...) custom-call(s32[3]{0:T(128)} %pad_add_fusion.pos_ref, ...), custom_call_target="tpu_custom_call" | custom-call | flops 241591910400 | bytes 2359296 | tf_op jit(solution)/shard_map/attention_grads/pallas_call | solution.py:204
  67.5 5.8 %collective-permute-start.12 = (bf16[768,128]{1,0:T(8,128)(2,1)}, bf16[768,128]{1,0:T(8,128)(2,1)S(1)}, u32[]{:S(2)}, u32[]{:S(2)}) collective-permute-start(bf16[768,128]{1,0:T(8,128)(2,1)} %get-tuple-element.88), channel_id=1, source_target_pairs={{0,2},{1,3},{2,0},{3,1},{4,6},{5,7},{6,4},{7,5},{8,10},{9,11},{10,... | collective-permute-start | bytes 589832 | tf_op jit(solution)/shard_map/ppermute | solution.py:21
  74.8 1.6 %collective-permute-start.14 = (bf16[384,256]{1,0:T(8,128)(2,1)S(1)}, bf16[384,256]{1,0:T(8,128)(2,1)S(1)}, u32[]{:S(2)}, u32[]{:S(2)}) collective-permute-start(bf16[384,256]{1,0:T(8,128)(2,1)S(1)} %maximum_select_fusion.5.refs_0_), channel_id=1, source_target_pairs={{0,8},{8,0},{16,24},{24,16},{1,9},{9,1},{17,25},{25,17},{2,10},{10... | collective-permute-start | bytes 589832 | tf_op jit(solution)/shard_map/ppermute | solution.py:21
  76.3 1.5 %collective-permute-start.15 = (bf16[384,256]{1,0:T(8,128)(2,1)S(1)}, bf16[384,256]{1,0:T(8,128)(2,1)S(1)}, u32[]{:S(2)}, u32[]{:S(2)}) collective-permute-start(bf16[384,256]{1,0:T(8,128)(2,1)S(1)} %maximum_select_fusion.5.refs_0_), channel_id=1, source_target_pairs={{0,16},{8,24},{16,0},{24,8},{1,17},{9,25},{17,1},{25,9},{2,18},{10... | collective-permute-start | bytes 589832 | tf_op jit(solution)/shard_map/ppermute | solution.py:21
  79.3 2.4 %collective-permute-start.16 = (bf16[384,256]{1,0:T(8,128)(2,1)S(1)}, bf16[384,256]{1,0:T(8,128)(2,1)S(1)}, u32[]{:S(2)}, u32[]{:S(2)}) collective-permute-start(bf16[384,256]{1,0:T(8,128)(2,1)S(1)} %maximum_select_fusion.5.refs_0_), channel_id=1, source_target_pairs={{0,24},{8,16},{16,8},{24,0},{1,25},{9,17},{17,9},{25,1},{2,26},{10... | collective-permute-start | bytes 589832 | tf_op jit(solution)/shard_map/ppermute | solution.py:21
  81.8 1.5 %collective-permute-done.17 = bf16[768,128]{1,0:T(8,128)(2,1)S(1)} collective-permute-done((bf16[768,128]{1,0:T(8,128)(2,1)}, bf16[768,128]{1,0:T(8,128)(2,1)S(1)}, u32[]{:S(2)}, u32[]{:S(2)}) %collective-permute-start.17) | collective-permute-done | bytes 196640 | tf_op jit(solution)/shard_map/ppermute | solution.py:21
  83.3 10.5 %collective-permute-start.13 = (bf16[384,128]{1,0:T(8,128)(2,1)S(1)}, bf16[384,128]{1,0:T(8,128)(2,1)S(1)}, u32[]{:S(2)}, u32[]{:S(2)}) collective-permute-start(bf16[384,128]{1,0:T(8,128)(2,1)S(1)} %get-tuple-element.163), channel_id=1, source_target_pairs={{0,4},{1,5},{2,6},{3,7},{4,0},{5,1},{6,2},{7,3},{8,12},{9,13},{10,... | collective-permute-start | bytes 294920 | tf_op jit(solution)/shard_map/ppermute | solution.py:21
  93.9 5.8 %weight_products.3 = (bf16[1024,256]{1,0:T(8,128)(2,1)S(1)}, bf16[512,256]{1,0:T(8,128)(2,1)S(1)}, f32[512,256]{1,0:T(8,128)S(1)}) custom-call(s32[3]{0:T(128)S(1)} %copy-done, bf16[384,256]{1,0:T(8,128)(2,1)S(1)} %maximum_select_fusion.5.refs_0_, bf16[384,256]{1,0:T(8,128)(2,1)S(1)} %collective-permute-done.14.refs_1_, ...), custom_call_target="tpu_custom_call" | custom-call | flops 1 | bytes 1 | tf_op jit(solution)/shard_map/weight_products/pallas_call | solution.py:276
  99.7 1.9 %collective-permute-done.13 = bf16[384,128]{1,0:T(8,128)(2,1)S(1)} collective-permute-done((bf16[384,128]{1,0:T(8,128)(2,1)S(1)}, bf16[384,128]{1,0:T(8,128)(2,1)S(1)}, u32[]{:S(2)}, u32[]{:S(2)}) %collective-permute-start.13) | collective-permute-done | bytes 98336 | tf_op jit(solution)/shard_map/ppermute | solution.py:21
  101.7 1.6 %collective-permute-start.24 = (bf16[384,128]{1,0:T(8,128)(2,1)S(1)}, bf16[384,128]{1,0:T(8,128)(2,1)S(1)}, u32[]{:S(2)}, u32[]{:S(2)}) collective-permute-start(bf16[384,128]{1,0:T(8,128)(2,1)S(1)} %maximum_select_fusion.8.refs_0_), channel_id=1, source_target_pairs={{0,8},{8,0},{16,24},{24,16},{1,9},{9,1},{17,25},{25,17},{2,10},{10... | collective-permute-start | bytes 294920 | tf_op jit(solution)/shard_map/ppermute | solution.py:21
  103.2 1.5 %collective-permute-start.25 = (bf16[384,128]{1,0:T(8,128)(2,1)S(1)}, bf16[384,128]{1,0:T(8,128)(2,1)S(1)}, u32[]{:S(2)}, u32[]{:S(2)}) collective-permute-start(bf16[384,128]{1,0:T(8,128)(2,1)S(1)} %maximum_select_fusion.8.refs_0_), channel_id=1, source_target_pairs={{0,16},{8,24},{16,0},{24,8},{1,17},{9,25},{17,1},{25,9},{2,18},{10... | collective-permute-start | bytes 294920 | tf_op jit(solution)/shard_map/ppermute | solution.py:21
  105.4 1.6 %collective-permute-start.20 = (bf16[384,128]{1,0:T(8,128)(2,1)S(1)}, bf16[384,128]{1,0:T(8,128)(2,1)S(1)}, u32[]{:S(2)}, u32[]{:S(2)}) collective-permute-start(bf16[384,128]{1,0:T(8,128)(2,1)S(1)} %maximum_select_fusion.9.refs_0_), channel_id=1, source_target_pairs={{0,8},{8,0},{16,24},{24,16},{1,9},{9,1},{17,25},{25,17},{2,10},{10... | collective-permute-start | bytes 294920 | tf_op jit(solution)/shard_map/ppermute | solution.py:21
  106.9 1.5 %collective-permute-start.21 = (bf16[384,128]{1,0:T(8,128)(2,1)S(1)}, bf16[384,128]{1,0:T(8,128)(2,1)S(1)}, u32[]{:S(2)}, u32[]{:S(2)}) collective-permute-start(bf16[384,128]{1,0:T(8,128)(2,1)S(1)} %maximum_select_fusion.9.refs_0_), channel_id=1, source_target_pairs={{0,16},{8,24},{16,0},{24,8},{1,17},{9,25},{17,1},{25,9},{2,18},{10... | collective-permute-start | bytes 294920 | tf_op jit(solution)/shard_map/ppermute | solution.py:21
  110.3 5.3 %weight_products.4 = (bf16[1024,128]{1,0:T(8,128)(2,1)S(1)}, bf16[512,128]{1,0:T(8,128)(2,1)S(1)}, f32[512,128]{1,0:T(8,128)S(1)}) custom-call(s32[3]{0:T(128)S(1)} %copy-done, bf16[384,128]{1,0:T(8,128)(2,1)S(1)} %maximum_select_fusion.8.refs_0_, bf16[384,128]{1,0:T(8,128)(2,1)S(1)} %collective-permute-done.24.refs_1_, ...), custom_call_target="tpu_custom_call" | custom-call | flops 1 | bytes 1 | tf_op jit(solution)/shard_map/weight_products/pallas_call | solution.py:276
  118.0 3.5 %collective-permute-start.29 = (bf16[512,256]{1,0:T(8,128)(2,1)S(1)}, bf16[512,256]{1,0:T(8,128)(2,1)S(1)}, u32[]{:S(2)}, u32[]{:S(2)}) collective-permute-start(bf16[512,256]{1,0:T(8,128)(2,1)S(1)} %get-tuple-element.143), channel_id=1, source_target_pairs={{0,4},{1,5},{2,6},{3,7},{4,0},{5,1},{6,2},{7,3},{8,12},{9,13},{10,... | collective-permute-start | bytes 786440 | tf_op jit(solution)/shard_map/ppermute | solution.py:21
  121.5 5.4 %weight_products.5 = (bf16[1024,128]{1,0:T(8,128)(2,1)S(1)}, bf16[512,128]{1,0:T(8,128)(2,1)S(1)}, f32[512,128]{1,0:T(8,128)S(1)}) custom-call(s32[3]{0:T(128)S(1)} %copy-done, bf16[384,128]{1,0:T(8,128)(2,1)S(1)} %maximum_select_fusion.9.refs_0_, bf16[384,128]{1,0:T(8,128)(2,1)S(1)} %collective-permute-done.20.refs_1_, ...), custom_call_target="tpu_custom_call" | custom-call | flops 1 | bytes 1 | tf_op jit(solution)/shard_map/weight_products/pallas_call | solution.py:276
  126.9 1.8 %collective-permute-start.30 = (bf16[1024,128]{1,0:T(8,128)(2,1)S(1)}, bf16[1024,128]{1,0:T(8,128)(2,1)S(1)}, u32[]{:S(2)}, u32[]{:S(2)}) collective-permute-start(bf16[1024,128]{1,0:T(8,128)(2,1)S(1)} %get-tuple-element.130), channel_id=1, source_target_pairs={{0,2},{1,3},{2,0},{3,1},{4,6},{5,7},{6,4},{7,5},{8,10},{9,11},{10,... | collective-permute-start | bytes 786440 | tf_op jit(solution)/shard_map/ppermute | solution.py:21
  128.8 2.4 %collective-permute-start.33 = (bf16[512,128]{1,0:T(8,128)(2,1)S(1)}, bf16[512,128]{1,0:T(8,128)(2,1)S(1)}, u32[]{:S(2)}, u32[]{:S(2)}) collective-permute-start(bf16[512,128]{1,0:T(8,128)(2,1)S(1)} %get-tuple-element.153), channel_id=1, source_target_pairs={{0,4},{1,5},{2,6},{3,7},{4,0},{5,1},{6,2},{7,3},{8,12},{9,13},{10,... | collective-permute-start | bytes 393224 | tf_op jit(solution)/shard_map/ppermute | solution.py:21
  134.3 1.9 %collective-permute-done.30 = bf16[1024,128]{1,0:T(8,128)(2,1)S(1)} collective-permute-done((bf16[1024,128]{1,0:T(8,128)(2,1)S(1)}, bf16[1024,128]{1,0:T(8,128)(2,1)S(1)}, u32[]{:S(2)}, u32[]{:S(2)}) %collective-permute-start.30) | collective-permute-done | bytes 262176 | tf_op jit(solution)/shard_map/ppermute | solution.py:21
  136.2 2.1 %collective-permute-start.32 = (bf16[512,128]{1,0:T(8,128)(2,1)S(1)}, bf16[512,128]{1,0:T(8,128)(2,1)S(1)}, u32[]{:S(2)}, u32[]{:S(2)}) collective-permute-start(bf16[512,128]{1,0:T(8,128)(2,1)S(1)} %get-tuple-element.151), channel_id=1, source_target_pairs={{0,4},{1,5},{2,6},{3,7},{4,0},{5,1},{6,2},{7,3},{8,12},{9,13},{10,... | collective-permute-start | bytes 393224 | tf_op jit(solution)/shard_map/ppermute | solution.py:21
  141.0 1.7 %maximum_select_fusion = bf16[192,4096]{1,0:T(8,128)(2,1)} fusion(bf16[192,2048]{1,0:T(8,128)(2,1)S(1)} %collective-permute-done.27, bf16[192,1024]{1,0:T(8,128)(2,1)S(1)} %copy-done.8, bf16[192,1024]{1,0:T(8,128)(2,1)S(1)} %copy-done.7, pred[]{:T(512)S(6)} %eq.5), kind=kLoop, calls=%fused_computation.1 | loop fusion | flops 10223616 | bytes 3145729 | tf_op jit(solution)/shard_map/jit(_where)/select_n | solution.py:322
  142.7 2.2 %collective-permute-done.32 = bf16[512,128]{1,0:T(8,128)(2,1)S(1)} collective-permute-done((bf16[512,128]{1,0:T(8,128)(2,1)S(1)}, bf16[512,128]{1,0:T(8,128)(2,1)S(1)}, u32[]{:S(2)}, u32[]{:S(2)}) %collective-permute-start.32) | collective-permute-done | bytes 131104 | tf_op jit(solution)/shard_map/ppermute | solution.py:21
  (122 shorter events, 26.7 us)
Async XLA Ops:
  8.1 25.3 %collective-permute-start.1 = (bf16[192,2048]{1,0:T(8,128)(2,1)}, bf16[192,2048]{1,0:T(8,128)(2,1)}, u32[]{:S(2)}, u32[]{:S(2)}) collective-permute-start(bf16[192,2048]{1,0:T(8,128)(2,1)} %pad_maximum_fusion), channel_id=1, source_target_pairs={{0,1},{1,0},{2,3},{3,2},{4,5},{5,4},{6,7},{7,6},{8,9},{9,8},{10,11... | collective-permute-start | bytes 2359304 | tf_op jit(solution)/shard_map/ppermute | solution.py:21
  8.4 13.8 %collective-permute-start.3 = (bf16[384,256]{1,0:T(8,128)(2,1)}, bf16[384,256]{1,0:T(8,128)(2,1)}, u32[]{:S(2)}, u32[]{:S(2)}) collective-permute-start(bf16[384,256]{1,0:T(8,128)(2,1)} %maximum_select_fusion.3.refs_0_), channel_id=1, source_target_pairs={{0,4},{1,5},{2,6},{3,7},{4,0},{5,1},{6,2},{7,3},{8,12},{9,13},{10,... | collective-permute-start | bytes 589832 | tf_op jit(solution)/shard_map/ppermute | solution.py:21
  12.8 11.0 %collective-permute-start.2 = (bf16[384,256]{1,0:T(8,128)(2,1)}, bf16[384,256]{1,0:T(8,128)(2,1)}, u32[]{:S(2)}, u32[]{:S(2)}) collective-permute-start(bf16[384,256]{1,0:T(8,128)(2,1)} %maximum_select_fusion.3.refs_0_), channel_id=1, source_target_pairs={{0,2},{1,3},{2,0},{3,1},{4,6},{5,7},{6,4},{7,5},{8,10},{9,11},{10,... | collective-permute-start | bytes 589832 | tf_op jit(solution)/shard_map/ppermute | solution.py:21
  16.3 42.4 %all-to-all-start = ((bf16[4,192,2048]{2,1,0:T(8,128)(2,1)}), bf16[4,192,2048]{2,1,0:T(8,128)(2,1)}, u32[]{:S(2)}, u32[]{:S(2)}) async-start(bf16[4,192,2048]{2,1,0:T(8,128)(2,1)} %bitcast.10), calls=%async_computation | async-start | bytes 6291456 | tf_op jit(solution)/shard_map/all_to_all | solution.py:397
  22.2 6.7 %collective-permute-start.4 = (bf16[384,256]{1,0:T(8,128)(2,1)}, bf16[384,256]{1,0:T(8,128)(2,1)S(1)}, u32[]{:S(2)}, u32[]{:S(2)}) collective-permute-start(bf16[384,256]{1,0:T(8,128)(2,1)} %collective-permute-done.3.refs_2_), channel_id=1, source_target_pairs={{0,2},{1,3},{2,0},{3,1},{4,6},{5,7},{6,4},{7,5},{8,10},{9,11},{10,... | collective-permute-start | bytes 589832 | tf_op jit(solution)/shard_map/ppermute | solution.py:21
  23.8 34.9 %collective-permute-start.5 = (bf16[192,2048]{1,0:T(8,128)(2,1)}, bf16[192,2048]{1,0:T(8,128)(2,1)}, u32[]{:S(2)}, u32[]{:S(2)}) collective-permute-start(bf16[192,2048]{1,0:T(8,128)(2,1)} %pad_maximum_fusion.1), channel_id=1, source_target_pairs={{0,1},{1,0},{2,3},{3,2},{4,5},{5,4},{6,7},{7,6},{8,9},{9,8},{10,11... | collective-permute-start | bytes 2359304 | tf_op jit(solution)/shard_map/ppermute | solution.py:21
  29.0 22.8 %collective-permute-start.6 = (bf16[384,256]{1,0:T(8,128)(2,1)}, bf16[384,256]{1,0:T(8,128)(2,1)}, u32[]{:S(2)}, u32[]{:S(2)}) collective-permute-start(bf16[384,256]{1,0:T(8,128)(2,1)} %maximum_select_fusion.4.refs_0_), channel_id=1, source_target_pairs={{0,2},{1,3},{2,0},{3,1},{4,6},{5,7},{6,4},{7,5},{8,10},{9,11},{10,... | collective-permute-start | bytes 589832 | tf_op jit(solution)/shard_map/ppermute | solution.py:21
  29.9 28.2 %collective-permute-start.7 = (bf16[384,256]{1,0:T(8,128)(2,1)}, bf16[384,256]{1,0:T(8,128)(2,1)}, u32[]{:S(2)}, u32[]{:S(2)}) collective-permute-start(bf16[384,256]{1,0:T(8,128)(2,1)} %maximum_select_fusion.4.refs_0_), channel_id=1, source_target_pairs={{0,4},{1,5},{2,6},{3,7},{4,0},{5,1},{6,2},{7,3},{8,12},{9,13},{10,... | collective-permute-start | bytes 589832 | tf_op jit(solution)/shard_map/ppermute | solution.py:21
  33.3 25.4 %collective-permute-start.8 = (bf16[384,256]{1,0:T(8,128)(2,1)}, bf16[384,256]{1,0:T(8,128)(2,1)}, u32[]{:S(2)}, u32[]{:S(2)}) collective-permute-start(bf16[384,256]{1,0:T(8,128)(2,1)} %maximum_select_fusion.4.refs_0_), channel_id=1, source_target_pairs={{0,6},{1,7},{2,4},{3,5},{4,2},{5,3},{6,0},{7,1},{8,14},{9,15},{10,... | collective-permute-start | bytes 589832 | tf_op jit(solution)/shard_map/ppermute | solution.py:21
  41.8 31.5 %collective-permute-start.10 = (bf16[384,256]{1,0:T(8,128)(2,1)}, bf16[384,256]{1,0:T(8,128)(2,1)}, u32[]{:S(2)}, u32[]{:S(2)}) collective-permute-start(bf16[384,256]{1,0:T(8,128)(2,1)} %get-tuple-element.79), channel_id=1, source_target_pairs={{0,4},{1,5},{2,6},{3,7},{4,0},{5,1},{6,2},{7,3},{8,12},{9,13},{10,... | collective-permute-start | bytes 589832 | tf_op jit(solution)/shard_map/ppermute | solution.py:21
  51.8 21.7 %collective-permute-start.11 = (bf16[384,256]{1,0:T(8,128)(2,1)}, bf16[384,256]{1,0:T(8,128)(2,1)}, u32[]{:S(2)}, u32[]{:S(2)}) collective-permute-start(bf16[384,256]{1,0:T(8,128)(2,1)} %get-tuple-element.80), channel_id=1, source_target_pairs={{0,6},{1,7},{2,4},{3,5},{4,2},{5,3},{6,0},{7,1},{8,14},{9,15},{10,... | collective-permute-start | bytes 589832 | tf_op jit(solution)/shard_map/ppermute | solution.py:21
  58.2 15.3 %collective-permute-start.9 = (bf16[384,256]{1,0:T(8,128)(2,1)}, bf16[384,256]{1,0:T(8,128)(2,1)}, u32[]{:S(2)}, u32[]{:S(2)}) collective-permute-start(bf16[384,256]{1,0:T(8,128)(2,1)} %get-tuple-element.78), channel_id=1, source_target_pairs={{0,2},{1,3},{2,0},{3,1},{4,6},{5,7},{6,4},{7,5},{8,10},{9,11},{10,... | collective-permute-start | bytes 589832 | tf_op jit(solution)/shard_map/ppermute | solution.py:21
  58.7 35.2 %collective-permute-start.18 = (bf16[768,2048]{1,0:T(8,128)(2,1)}, bf16[768,2048]{1,0:T(8,128)(2,1)}, u32[]{:S(2)}, u32[]{:S(2)}) collective-permute-start(bf16[768,2048]{1,0:T(8,128)(2,1)} %bitcast.4.refs_4_), channel_id=1, source_target_pairs={{0,1},{1,0},{2,3},{3,2},{4,5},{5,4},{6,7},{7,6},{8,9},{9,8},{10,11... | collective-permute-start | bytes 9437192 | tf_op jit(solution)/shard_map/ppermute | solution.py:21
  67.5 11.8 %collective-permute-start.12 = (bf16[768,128]{1,0:T(8,128)(2,1)}, bf16[768,128]{1,0:T(8,128)(2,1)S(1)}, u32[]{:S(2)}, u32[]{:S(2)}) collective-permute-start(bf16[768,128]{1,0:T(8,128)(2,1)} %get-tuple-element.88), channel_id=1, source_target_pairs={{0,2},{1,3},{2,0},{3,1},{4,6},{5,7},{6,4},{7,5},{8,10},{9,11},{10,... | collective-permute-start | bytes 589832 | tf_op jit(solution)/shard_map/ppermute | solution.py:21
  73.3 10.0 %collective-permute-start.17 = (bf16[768,128]{1,0:T(8,128)(2,1)}, bf16[768,128]{1,0:T(8,128)(2,1)S(1)}, u32[]{:S(2)}, u32[]{:S(2)}) collective-permute-start(bf16[768,128]{1,0:T(8,128)(2,1)} %get-tuple-element.91), channel_id=1, source_target_pairs={{0,2},{1,3},{2,0},{3,1},{4,6},{5,7},{6,4},{7,5},{8,10},{9,11},{10,... | collective-permute-start | bytes 589832 | tf_op jit(solution)/shard_map/ppermute | solution.py:21
  74.8 19.1 %collective-permute-start.14 = (bf16[384,256]{1,0:T(8,128)(2,1)S(1)}, bf16[384,256]{1,0:T(8,128)(2,1)S(1)}, u32[]{:S(2)}, u32[]{:S(2)}) collective-permute-start(bf16[384,256]{1,0:T(8,128)(2,1)S(1)} %maximum_select_fusion.5.refs_0_), channel_id=1, source_target_pairs={{0,8},{8,0},{16,24},{24,16},{1,9},{9,1},{17,25},{25,17},{2,10},{10... | collective-permute-start | bytes 589832 | tf_op jit(solution)/shard_map/ppermute | solution.py:21
  76.3 17.6 %collective-permute-start.15 = (bf16[384,256]{1,0:T(8,128)(2,1)S(1)}, bf16[384,256]{1,0:T(8,128)(2,1)S(1)}, u32[]{:S(2)}, u32[]{:S(2)}) collective-permute-start(bf16[384,256]{1,0:T(8,128)(2,1)S(1)} %maximum_select_fusion.5.refs_0_), channel_id=1, source_target_pairs={{0,16},{8,24},{16,0},{24,8},{1,17},{9,25},{17,1},{25,9},{2,18},{10... | collective-permute-start | bytes 589832 | tf_op jit(solution)/shard_map/ppermute | solution.py:21
  79.3 14.6 %collective-permute-start.16 = (bf16[384,256]{1,0:T(8,128)(2,1)S(1)}, bf16[384,256]{1,0:T(8,128)(2,1)S(1)}, u32[]{:S(2)}, u32[]{:S(2)}) collective-permute-start(bf16[384,256]{1,0:T(8,128)(2,1)S(1)} %maximum_select_fusion.5.refs_0_), channel_id=1, source_target_pairs={{0,24},{8,16},{16,8},{24,0},{1,25},{9,17},{17,9},{25,1},{2,26},{10... | collective-permute-start | bytes 589832 | tf_op jit(solution)/shard_map/ppermute | solution.py:21
  83.3 18.3 %collective-permute-start.13 = (bf16[384,128]{1,0:T(8,128)(2,1)S(1)}, bf16[384,128]{1,0:T(8,128)(2,1)S(1)}, u32[]{:S(2)}, u32[]{:S(2)}) collective-permute-start(bf16[384,128]{1,0:T(8,128)(2,1)S(1)} %get-tuple-element.163), channel_id=1, source_target_pairs={{0,4},{1,5},{2,6},{3,7},{4,0},{5,1},{6,2},{7,3},{8,12},{9,13},{10,... | collective-permute-start | bytes 294920 | tf_op jit(solution)/shard_map/ppermute | solution.py:21
  93.8 11.5 %collective-permute-start.19 = (bf16[384,128]{1,0:T(8,128)(2,1)S(1)}, bf16[384,128]{1,0:T(8,128)(2,1)S(1)}, u32[]{:S(2)}, u32[]{:S(2)}) collective-permute-start(bf16[384,128]{1,0:T(8,128)(2,1)S(1)} %get-tuple-element.161), channel_id=1, source_target_pairs={{0,4},{1,5},{2,6},{3,7},{4,0},{5,1},{6,2},{7,3},{8,12},{9,13},{10,... | collective-permute-start | bytes 294920 | tf_op jit(solution)/shard_map/ppermute | solution.py:21
  101.7 5.3 %collective-permute-start.24 = (bf16[384,128]{1,0:T(8,128)(2,1)S(1)}, bf16[384,128]{1,0:T(8,128)(2,1)S(1)}, u32[]{:S(2)}, u32[]{:S(2)}) collective-permute-start(bf16[384,128]{1,0:T(8,128)(2,1)S(1)} %maximum_select_fusion.8.refs_0_), channel_id=1, source_target_pairs={{0,8},{8,0},{16,24},{24,16},{1,9},{9,1},{17,25},{25,17},{2,10},{10... | collective-permute-start | bytes 294920 | tf_op jit(solution)/shard_map/ppermute | solution.py:21
  104.7 5.6 %collective-permute-start.26 = (bf16[384,128]{1,0:T(8,128)(2,1)S(1)}, bf16[384,128]{1,0:T(8,128)(2,1)S(1)}, u32[]{:S(2)}, u32[]{:S(2)}) collective-permute-start(bf16[384,128]{1,0:T(8,128)(2,1)S(1)} %maximum_select_fusion.8.refs_0_), channel_id=1, source_target_pairs={{0,24},{8,16},{16,8},{24,0},{1,25},{9,17},{17,9},{25,1},{2,26},{10... | collective-permute-start | bytes 294920 | tf_op jit(solution)/shard_map/ppermute | solution.py:21
  105.2 12.7 %collective-permute-start.23 = (bf16[1024,256]{1,0:T(8,128)(2,1)S(1)}, bf16[1024,256]{1,0:T(8,128)(2,1)S(1)}, u32[]{:S(2)}, u32[]{:S(2)}) collective-permute-start(bf16[1024,256]{1,0:T(8,128)(2,1)S(1)} %get-tuple-element.106), channel_id=1, source_target_pairs={{0,2},{1,3},{2,0},{3,1},{4,6},{5,7},{6,4},{7,5},{8,10},{9,11},{10,... | collective-permute-start | bytes 1572872 | tf_op jit(solution)/shard_map/ppermute | solution.py:21
  105.4 16.1 %collective-permute-start.20 = (bf16[384,128]{1,0:T(8,128)(2,1)S(1)}, bf16[384,128]{1,0:T(8,128)(2,1)S(1)}, u32[]{:S(2)}, u32[]{:S(2)}) collective-permute-start(bf16[384,128]{1,0:T(8,128)(2,1)S(1)} %maximum_select_fusion.9.refs_0_), channel_id=1, source_target_pairs={{0,8},{8,0},{16,24},{24,16},{1,9},{9,1},{17,25},{25,17},{2,10},{10... | collective-permute-start | bytes 294920 | tf_op jit(solution)/shard_map/ppermute | solution.py:21
  106.9 14.6 %collective-permute-start.21 = (bf16[384,128]{1,0:T(8,128)(2,1)S(1)}, bf16[384,128]{1,0:T(8,128)(2,1)S(1)}, u32[]{:S(2)}, u32[]{:S(2)}) collective-permute-start(bf16[384,128]{1,0:T(8,128)(2,1)S(1)} %maximum_select_fusion.9.refs_0_), channel_id=1, source_target_pairs={{0,16},{8,24},{16,0},{24,8},{1,17},{9,25},{17,1},{25,9},{2,18},{10... | collective-permute-start | bytes 294920 | tf_op jit(solution)/shard_map/ppermute | solution.py:21
  108.5 13.0 %collective-permute-start.22 = (bf16[384,128]{1,0:T(8,128)(2,1)S(1)}, bf16[384,128]{1,0:T(8,128)(2,1)S(1)}, u32[]{:S(2)}, u32[]{:S(2)}) collective-permute-start(bf16[384,128]{1,0:T(8,128)(2,1)S(1)} %maximum_select_fusion.9.refs_0_), channel_id=1, source_target_pairs={{0,24},{8,16},{16,8},{24,0},{1,25},{9,17},{17,9},{25,1},{2,26},{10... | collective-permute-start | bytes 294920 | tf_op jit(solution)/shard_map/ppermute | solution.py:21
  115.7 13.0 %collective-permute-start.31 = (bf16[1024,128]{1,0:T(8,128)(2,1)S(1)}, bf16[1024,128]{1,0:T(8,128)(2,1)S(1)}, u32[]{:S(2)}, u32[]{:S(2)}) collective-permute-start(bf16[1024,128]{1,0:T(8,128)(2,1)S(1)} %get-tuple-element.117), channel_id=1, source_target_pairs={{0,2},{1,3},{2,0},{3,1},{4,6},{5,7},{6,4},{7,5},{8,10},{9,11},{10,... | collective-permute-start | bytes 786440 | tf_op jit(solution)/shard_map/ppermute | solution.py:21
  118.0 20.3 %collective-permute-start.29 = (bf16[512,256]{1,0:T(8,128)(2,1)S(1)}, bf16[512,256]{1,0:T(8,128)(2,1)S(1)}, u32[]{:S(2)}, u32[]{:S(2)}) collective-permute-start(bf16[512,256]{1,0:T(8,128)(2,1)S(1)} %get-tuple-element.143), channel_id=1, source_target_pairs={{0,4},{1,5},{2,6},{3,7},{4,0},{5,1},{6,2},{7,3},{8,12},{9,13},{10,... | collective-permute-start | bytes 786440 | tf_op jit(solution)/shard_map/ppermute | solution.py:21
  126.9 9.2 %collective-permute-start.30 = (bf16[1024,128]{1,0:T(8,128)(2,1)S(1)}, bf16[1024,128]{1,0:T(8,128)(2,1)S(1)}, u32[]{:S(2)}, u32[]{:S(2)}) collective-permute-start(bf16[1024,128]{1,0:T(8,128)(2,1)S(1)} %get-tuple-element.130), channel_id=1, source_target_pairs={{0,2},{1,3},{2,0},{3,1},{4,6},{5,7},{6,4},{7,5},{8,10},{9,11},{10,... | collective-permute-start | bytes 786440 | tf_op jit(solution)/shard_map/ppermute | solution.py:21
  128.8 9.7 %collective-permute-start.33 = (bf16[512,128]{1,0:T(8,128)(2,1)S(1)}, bf16[512,128]{1,0:T(8,128)(2,1)S(1)}, u32[]{:S(2)}, u32[]{:S(2)}) collective-permute-start(bf16[512,128]{1,0:T(8,128)(2,1)S(1)} %get-tuple-element.153), channel_id=1, source_target_pairs={{0,4},{1,5},{2,6},{3,7},{4,0},{5,1},{6,2},{7,3},{8,12},{9,13},{10,... | collective-permute-start | bytes 393224 | tf_op jit(solution)/shard_map/ppermute | solution.py:21
  131.4 9.6 %collective-permute-start.27 = (bf16[192,2048]{1,0:T(8,128)(2,1)S(1)}, bf16[192,2048]{1,0:T(8,128)(2,1)S(1)}, u32[]{:S(2)}, u32[]{:S(2)}) collective-permute-start(bf16[192,2048]{1,0:T(8,128)(2,1)S(1)} %pad_maximum_fusion.2), channel_id=1, source_target_pairs={{0,1},{1,0},{2,3},{3,2},{4,5},{5,4},{6,7},{7,6},{8,9},{9,8},{10,11... | collective-permute-start | bytes 2359304 | tf_op jit(solution)/shard_map/ppermute | solution.py:21
  136.2 8.7 %collective-permute-start.32 = (bf16[512,128]{1,0:T(8,128)(2,1)S(1)}, bf16[512,128]{1,0:T(8,128)(2,1)S(1)}, u32[]{:S(2)}, u32[]{:S(2)}) collective-permute-start(bf16[512,128]{1,0:T(8,128)(2,1)S(1)} %get-tuple-element.151), channel_id=1, source_target_pairs={{0,4},{1,5},{2,6},{3,7},{4,0},{5,1},{6,2},{7,3},{8,12},{9,13},{10,... | collective-permute-start | bytes 393224 | tf_op jit(solution)/shard_map/ppermute | solution.py:21
  (20 other events, 166.7 us)

commit v5 on v4

--- a/solution.py
+++ b/solution.py
@@ -50,7 +50,7 @@
     for c in started:
         c.start()
     acc[...] = jnp.zeros_like(acc)
-    for c in started:
+    for c in started[:5]:
         c.wait()
     scale = 1.0 / math.sqrt(HD)
     log_scale = scale * math.log2(math.e)
@@ -58,8 +58,6 @@
     def turn(j, _):
         kt[j] = kv[j, :, :HD].T
         return 0
-
-    lax.fori_loop(0, chip + 1, turn, 0)
 
     def columns_of(u):
         return pl.ds(pl.multiple_of(u * UNIT * HD, UNIT * HD), UNIT * HD)
@@ -110,6 +108,13 @@
         zero = jnp.zeros((1, LANES), F32)
         start = (jnp.full((1, LANES), -jnp.inf, F32), zero, zero)
         carry = scores(chip, (start,) * (rows // LANES), True)
+
+        @pl.when(u == 0)
+        def _():
+            for c in started[5:]:
+                c.wait()
+            lax.fori_loop(0, chip + 1, turn, 0)
+
         carry = lax.fori_loop(0, chip, lambda j, c: scores(j, c, False), carry)
         top, total, weighted = (jnp.concatenate(x, 1) for x in zip(*carry))
         inv = 1.0 / total

time: 148 us -> 147 us (level)
  no operation moved by 1% of the time
where the time goes in v5:
time: 147 us
  starting transfers between devices  74.6 us (51%)
  Pallas kernels  33.3 us (23%)
  waiting for transfers between devices  21.6 us (15%)
  other arithmetic  10.8 us (7%)
  local copies, waits for them, and re-layouts  5.44 us (4%)
    ppermute x37, starting transfers between devices, xor_permute(): return lax.ppermute(array, axis, [(i, i ^ mask) for i in range(size)])  69.8 us
    ppermute x37, waiting for transfers between devices, xor_permute(): return lax.ppermute(array, axis, [(i, i ^ mask) for i in range(size)])  21.6 us
    pallas_call x2, Pallas kernels, attention(): pl.pallas_call(functools.partial(attention_kernel, chips, tok, group, hea...  16.9 us
    pallas_call x3, Pallas kernels, weight_products(): pl.pallas_call(functools.partial(product_kernel, chips, n_dp, span // PAI...  16.5 us
    select_n x7, other arithmetic, in_order(): jnp.where(first, jnp.concatenate([mine, theirs], axis), jnp.concatenate([...  6.36 us
    all_to_all x1, starting transfers between devices, on_device(): lax.all_to_all(shares, 'dp', split_axis=0, concat_axis=0, tiled=True)  4.83 us
    dynamic_slice x3, local copies, waits for them, and re-layouts, columns(): return lax.dynamic_slice_in_dim(x, head * size, size, 1)  3.24 us
  transfers between devices with their start and end apart: 38, of which 14 were waited for; matrix products, arithmetic and copies ran while one was open for 6% of the time, Pallas kernels for 23%

profile of v5, /device:TPU:0, one launch (start us, length us, event | category | flops | bytes accessed | tf_op | source)
XLA Modules:
  0.0 146.9 jit_solution(14812224594548115054)
XLA Ops:
  5.0 2.1 %constant_dynamic-slice_fusion.6 = (bf16[192,1024]{1,0:T(8,128)(2,1)}, bf16[192,1024]{1,0:T(8,128)(2,1)S(1)}) fusion(bf16[192,4096]{1,0:T(8,128)(2,1)} %g_own.3, s32[]{:T(128)S(6)} %select_n.112, s32[]{:T(128)S(6)} %select_n.111), kind=kLoop, calls=%fused_computation.38 | loop fusion | bytes 1572872 | tf_op jit(solution)/shard_map/dynamic_slice | solution.py:334
  8.4 3.7 %collective-permute-start.3 = (bf16[384,256]{1,0:T(8,128)(2,1)}, bf16[384,256]{1,0:T(8,128)(2,1)}, u32[]{:S(2)}, u32[]{:S(2)}) collective-permute-start(bf16[384,256]{1,0:T(8,128)(2,1)} %maximum_select_fusion.3.refs_0_), channel_id=1, source_target_pairs={{0,4},{1,5},{2,6},{3,7},{4,0},{5,1},{6,2},{7,3},{8,12},{9,13},{10,... | collective-permute-start | bytes 589832 | tf_op jit(solution)/shard_map/ppermute | solution.py:21
  12.8 1.6 %collective-permute-start.2 = (bf16[384,256]{1,0:T(8,128)(2,1)}, bf16[384,256]{1,0:T(8,128)(2,1)}, u32[]{:S(2)}, u32[]{:S(2)}) collective-permute-start(bf16[384,256]{1,0:T(8,128)(2,1)} %maximum_select_fusion.3.refs_0_), channel_id=1, source_target_pairs={{0,2},{1,3},{2,0},{3,1},{4,6},{5,7},{6,4},{7,5},{8,10},{9,11},{10,... | collective-permute-start | bytes 589832 | tf_op jit(solution)/shard_map/ppermute | solution.py:21
  14.4 1.9 %copy.13 = bf16[24,4,8,2048]{3,2,0,1:T(8,128)(2,1)} copy(bf16[24,4,8,2048]{3,2,1,0:T(8,128)(2,1)S(1)} %bitcast.11) | data formatting | bytes 6291456 | tf_op jit(solution)/shard_map/reshape | solution.py:396
  16.3 4.8 %all-to-all-start = ((bf16[4,192,2048]{2,1,0:T(8,128)(2,1)}), bf16[4,192,2048]{2,1,0:T(8,128)(2,1)}, u32[]{:S(2)}, u32[]{:S(2)}) async-start(bf16[4,192,2048]{2,1,0:T(8,128)(2,1)} %bitcast.10), calls=%async_computation | async-start | bytes 6291456 | tf_op jit(solution)/shard_map/all_to_all | solution.py:402
  23.8 5.2 %collective-permute-done.4.refs_3_ = bf16[384,256]{1,0:T(8,128)(2,1)S(1)} collective-permute-done((bf16[384,256]{1,0:T(8,128)(2,1)}, bf16[384,256]{1,0:T(8,128)(2,1)S(1)}, u32[]{:S(2)}, u32[]{:S(2)}) %collective-permute-start.4) | collective-permute-done | bytes 196640 | tf_op jit(solution)/shard_map/ppermute | solution.py:21
  29.9 3.4 %collective-permute-start.7 = (bf16[384,256]{1,0:T(8,128)(2,1)}, bf16[384,256]{1,0:T(8,128)(2,1)}, u32[]{:S(2)}, u32[]{:S(2)}) collective-permute-start(bf16[384,256]{1,0:T(8,128)(2,1)} %maximum_select_fusion.4.refs_0_), channel_id=1, source_target_pairs={{0,4},{1,5},{2,6},{3,7},{4,0},{5,1},{6,2},{7,3},{8,12},{9,13},{10,... | collective-permute-start | bytes 589832 | tf_op jit(solution)/shard_map/ppermute | solution.py:21
  33.4 8.3 %attention_grads.2 = (bf16[192,1024]{1,0:T(8,128)(2,1)}, bf16[192,1024]{1,0:T(8,128)(2,1)}, f32[384,256]{1,0:T(8,128)}, bf16[384,256]{1,0:T(8,128)(2,1)}, bf16[3...) custom-call(s32[3]{0:T(128)} %pad_add_fusion.pos_ref, bf16[192,4096]{1,0:T(8,128)(2,1)} %q_own.3, bf16[192,4096]{1,0:T(8,128)(2,1)} %g_own.3, ...), custom_call_target="tpu_custom_call" | custom-call | flops 241591910400 | bytes 2359296 | tf_op jit(solution)/shard_map/attention_grads/pallas_call | solution.py:209
  41.7 9.9 %collective-permute-start.10 = (bf16[384,256]{1,0:T(8,128)(2,1)}, bf16[384,256]{1,0:T(8,128)(2,1)}, u32[]{:S(2)}, u32[]{:S(2)}) collective-permute-start(bf16[384,256]{1,0:T(8,128)(2,1)} %get-tuple-element.79), channel_id=1, source_target_pairs={{0,4},{1,5},{2,6},{3,7},{4,0},{5,1},{6,2},{7,3},{8,12},{9,13},{10,... | collective-permute-start | bytes 589832 | tf_op jit(solution)/shard_map/ppermute | solution.py:21
  51.6 6.4 %collective-permute-start.11 = (bf16[384,256]{1,0:T(8,128)(2,1)}, bf16[384,256]{1,0:T(8,128)(2,1)}, u32[]{:S(2)}, u32[]{:S(2)}) collective-permute-start(bf16[384,256]{1,0:T(8,128)(2,1)} %get-tuple-element.80), channel_id=1, source_target_pairs={{0,6},{1,7},{2,4},{3,5},{4,2},{5,3},{6,0},{7,1},{8,14},{9,15},{10,... | collective-permute-start | bytes 589832 | tf_op jit(solution)/shard_map/ppermute | solution.py:21
  58.7 8.5 %attention_grads.3 = (bf16[192,1024]{1,0:T(8,128)(2,1)}, bf16[192,1024]{1,0:T(8,128)(2,1)}, f32[384,128]{1,0:T(8,128)}, bf16[768,128]{1,0:T(8,128)(2,1)}, bf16[3...) custom-call(s32[3]{0:T(128)} %pad_add_fusion.pos_ref, ...), custom_call_target="tpu_custom_call" | custom-call | flops 241591910400 | bytes 2359296 | tf_op jit(solution)/shard_map/attention_grads/pallas_call | solution.py:209
  67.2 5.8 %collective-permute-start.12 = (bf16[768,128]{1,0:T(8,128)(2,1)}, bf16[768,128]{1,0:T(8,128)(2,1)S(1)}, u32[]{:S(2)}, u32[]{:S(2)}) collective-permute-start(bf16[768,128]{1,0:T(8,128)(2,1)} %get-tuple-element.88), channel_id=1, source_target_pairs={{0,2},{1,3},{2,0},{3,1},{4,6},{5,7},{6,4},{7,5},{8,10},{9,11},{10,... | collective-permute-start | bytes 589832 | tf_op jit(solution)/shard_map/ppermute | solution.py:21
  74.4 1.5 %collective-permute-start.14 = (bf16[384,256]{1,0:T(8,128)(2,1)S(1)}, bf16[384,256]{1,0:T(8,128)(2,1)S(1)}, u32[]{:S(2)}, u32[]{:S(2)}) collective-permute-start(bf16[384,256]{1,0:T(8,128)(2,1)S(1)} %maximum_select_fusion.5.refs_0_), channel_id=1, source_target_pairs={{0,8},{8,0},{16,24},{24,16},{1,9},{9,1},{17,25},{25,17},{2,10},{10... | collective-permute-start | bytes 589832 | tf_op jit(solution)/shard_map/ppermute | solution.py:21
  76.0 1.5 %collective-permute-start.15 = (bf16[384,256]{1,0:T(8,128)(2,1)S(1)}, bf16[384,256]{1,0:T(8,128)(2,1)S(1)}, u32[]{:S(2)}, u32[]{:S(2)}) collective-permute-start(bf16[384,256]{1,0:T(8,128)(2,1)S(1)} %maximum_select_fusion.5.refs_0_), channel_id=1, source_target_pairs={{0,16},{8,24},{16,0},{24,8},{1,17},{9,25},{17,1},{25,9},{2,18},{10... | collective-permute-start | bytes 589832 | tf_op jit(solution)/shard_map/ppermute | solution.py:21
  79.0 2.4 %collective-permute-start.16 = (bf16[384,256]{1,0:T(8,128)(2,1)S(1)}, bf16[384,256]{1,0:T(8,128)(2,1)S(1)}, u32[]{:S(2)}, u32[]{:S(2)}) collective-permute-start(bf16[384,256]{1,0:T(8,128)(2,1)S(1)} %maximum_select_fusion.5.refs_0_), channel_id=1, source_target_pairs={{0,24},{8,16},{16,8},{24,0},{1,25},{9,17},{17,9},{25,1},{2,26},{10... | collective-permute-start | bytes 589832 | tf_op jit(solution)/shard_map/ppermute | solution.py:21
  81.5 1.5 %collective-permute-done.17 = bf16[768,128]{1,0:T(8,128)(2,1)S(1)} collective-permute-done((bf16[768,128]{1,0:T(8,128)(2,1)}, bf16[768,128]{1,0:T(8,128)(2,1)S(1)}, u32[]{:S(2)}, u32[]{:S(2)}) %collective-permute-start.17) | collective-permute-done | bytes 196640 | tf_op jit(solution)/shard_map/ppermute | solution.py:21
  83.0 10.5 %collective-permute-start.13 = (bf16[384,128]{1,0:T(8,128)(2,1)S(1)}, bf16[384,128]{1,0:T(8,128)(2,1)S(1)}, u32[]{:S(2)}, u32[]{:S(2)}) collective-permute-start(bf16[384,128]{1,0:T(8,128)(2,1)S(1)} %get-tuple-element.163), channel_id=1, source_target_pairs={{0,4},{1,5},{2,6},{3,7},{4,0},{5,1},{6,2},{7,3},{8,12},{9,13},{10,... | collective-permute-start | bytes 294920 | tf_op jit(solution)/shard_map/ppermute | solution.py:21
  93.6 5.8 %weight_products.3 = (bf16[1024,256]{1,0:T(8,128)(2,1)S(1)}, bf16[512,256]{1,0:T(8,128)(2,1)S(1)}, f32[512,256]{1,0:T(8,128)S(1)}) custom-call(s32[3]{0:T(128)S(1)} %copy-done, bf16[384,256]{1,0:T(8,128)(2,1)S(1)} %maximum_select_fusion.5.refs_0_, bf16[384,256]{1,0:T(8,128)(2,1)S(1)} %collective-permute-done.14.refs_1_, ...), custom_call_target="tpu_custom_call" | custom-call | flops 1 | bytes 1 | tf_op jit(solution)/shard_map/weight_products/pallas_call | solution.py:281
  99.4 1.9 %collective-permute-done.13 = bf16[384,128]{1,0:T(8,128)(2,1)S(1)} collective-permute-done((bf16[384,128]{1,0:T(8,128)(2,1)S(1)}, bf16[384,128]{1,0:T(8,128)(2,1)S(1)}, u32[]{:S(2)}, u32[]{:S(2)}) %collective-permute-start.13) | collective-permute-done | bytes 98336 | tf_op jit(solution)/shard_map/ppermute | solution.py:21
  101.4 1.5 %collective-permute-start.24 = (bf16[384,128]{1,0:T(8,128)(2,1)S(1)}, bf16[384,128]{1,0:T(8,128)(2,1)S(1)}, u32[]{:S(2)}, u32[]{:S(2)}) collective-permute-start(bf16[384,128]{1,0:T(8,128)(2,1)S(1)} %maximum_select_fusion.8.refs_0_), channel_id=1, source_target_pairs={{0,8},{8,0},{16,24},{24,16},{1,9},{9,1},{17,25},{25,17},{2,10},{10... | collective-permute-start | bytes 294920 | tf_op jit(solution)/shard_map/ppermute | solution.py:21
  102.9 1.5 %collective-permute-start.25 = (bf16[384,128]{1,0:T(8,128)(2,1)S(1)}, bf16[384,128]{1,0:T(8,128)(2,1)S(1)}, u32[]{:S(2)}, u32[]{:S(2)}) collective-permute-start(bf16[384,128]{1,0:T(8,128)(2,1)S(1)} %maximum_select_fusion.8.refs_0_), channel_id=1, source_target_pairs={{0,16},{8,24},{16,0},{24,8},{1,17},{9,25},{17,1},{25,9},{2,18},{10... | collective-permute-start | bytes 294920 | tf_op jit(solution)/shard_map/ppermute | solution.py:21
  105.1 1.5 %collective-permute-start.20 = (bf16[384,128]{1,0:T(8,128)(2,1)S(1)}, bf16[384,128]{1,0:T(8,128)(2,1)S(1)}, u32[]{:S(2)}, u32[]{:S(2)}) collective-permute-start(bf16[384,128]{1,0:T(8,128)(2,1)S(1)} %maximum_select_fusion.9.refs_0_), channel_id=1, source_target_pairs={{0,8},{8,0},{16,24},{24,16},{1,9},{9,1},{17,25},{25,17},{2,10},{10... | collective-permute-start | bytes 294920 | tf_op jit(solution)/shard_map/ppermute | solution.py:21
  106.6 1.5 %collective-permute-start.21 = (bf16[384,128]{1,0:T(8,128)(2,1)S(1)}, bf16[384,128]{1,0:T(8,128)(2,1)S(1)}, u32[]{:S(2)}, u32[]{:S(2)}) collective-permute-start(bf16[384,128]{1,0:T(8,128)(2,1)S(1)} %maximum_select_fusion.9.refs_0_), channel_id=1, source_target_pairs={{0,16},{8,24},{16,0},{24,8},{1,17},{9,25},{17,1},{25,9},{2,18},{10... | collective-permute-start | bytes 294920 | tf_op jit(solution)/shard_map/ppermute | solution.py:21
  110.0 5.4 %weight_products.4 = (bf16[1024,128]{1,0:T(8,128)(2,1)S(1)}, bf16[512,128]{1,0:T(8,128)(2,1)S(1)}, f32[512,128]{1,0:T(8,128)S(1)}) custom-call(s32[3]{0:T(128)S(1)} %copy-done, bf16[384,128]{1,0:T(8,128)(2,1)S(1)} %maximum_select_fusion.8.refs_0_, bf16[384,128]{1,0:T(8,128)(2,1)S(1)} %collective-permute-done.24.refs_1_, ...), custom_call_target="tpu_custom_call" | custom-call | flops 1 | bytes 1 | tf_op jit(solution)/shard_map/weight_products/pallas_call | solution.py:281
  117.7 3.4 %collective-permute-start.29 = (bf16[512,256]{1,0:T(8,128)(2,1)S(1)}, bf16[512,256]{1,0:T(8,128)(2,1)S(1)}, u32[]{:S(2)}, u32[]{:S(2)}) collective-permute-start(bf16[512,256]{1,0:T(8,128)(2,1)S(1)} %get-tuple-element.143), channel_id=1, source_target_pairs={{0,4},{1,5},{2,6},{3,7},{4,0},{5,1},{6,2},{7,3},{8,12},{9,13},{10,... | collective-permute-start | bytes 786440 | tf_op jit(solution)/shard_map/ppermute | solution.py:21
  121.2 5.4 %weight_products.5 = (bf16[1024,128]{1,0:T(8,128)(2,1)S(1)}, bf16[512,128]{1,0:T(8,128)(2,1)S(1)}, f32[512,128]{1,0:T(8,128)S(1)}) custom-call(s32[3]{0:T(128)S(1)} %copy-done, bf16[384,128]{1,0:T(8,128)(2,1)S(1)} %maximum_select_fusion.9.refs_0_, bf16[384,128]{1,0:T(8,128)(2,1)S(1)} %collective-permute-done.20.refs_1_, ...), custom_call_target="tpu_custom_call" | custom-call | flops 1 | bytes 1 | tf_op jit(solution)/shard_map/weight_products/pallas_call | solution.py:281
  126.6 1.8 %collective-permute-start.30 = (bf16[1024,128]{1,0:T(8,128)(2,1)S(1)}, bf16[1024,128]{1,0:T(8,128)(2,1)S(1)}, u32[]{:S(2)}, u32[]{:S(2)}) collective-permute-start(bf16[1024,128]{1,0:T(8,128)(2,1)S(1)} %get-tuple-element.130), channel_id=1, source_target_pairs={{0,2},{1,3},{2,0},{3,1},{4,6},{5,7},{6,4},{7,5},{8,10},{9,11},{10,... | collective-permute-start | bytes 786440 | tf_op jit(solution)/shard_map/ppermute | solution.py:21
  128.5 2.4 %collective-permute-start.33 = (bf16[512,128]{1,0:T(8,128)(2,1)S(1)}, bf16[512,128]{1,0:T(8,128)(2,1)S(1)}, u32[]{:S(2)}, u32[]{:S(2)}) collective-permute-start(bf16[512,128]{1,0:T(8,128)(2,1)S(1)} %get-tuple-element.153), channel_id=1, source_target_pairs={{0,4},{1,5},{2,6},{3,7},{4,0},{5,1},{6,2},{7,3},{8,12},{9,13},{10,... | collective-permute-start | bytes 393224 | tf_op jit(solution)/shard_map/ppermute | solution.py:21
  134.0 1.8 %collective-permute-done.30 = bf16[1024,128]{1,0:T(8,128)(2,1)S(1)} collective-permute-done((bf16[1024,128]{1,0:T(8,128)(2,1)S(1)}, bf16[1024,128]{1,0:T(8,128)(2,1)S(1)}, u32[]{:S(2)}, u32[]{:S(2)}) %collective-permute-start.30) | collective-permute-done | bytes 262176 | tf_op jit(solution)/shard_map/ppermute | solution.py:21
  135.9 2.1 %collective-permute-start.32 = (bf16[512,128]{1,0:T(8,128)(2,1)S(1)}, bf16[512,128]{1,0:T(8,128)(2,1)S(1)}, u32[]{:S(2)}, u32[]{:S(2)}) collective-permute-start(bf16[512,128]{1,0:T(8,128)(2,1)S(1)} %get-tuple-element.151), channel_id=1, source_target_pairs={{0,4},{1,5},{2,6},{3,7},{4,0},{5,1},{6,2},{7,3},{8,12},{9,13},{10,... | collective-permute-start | bytes 393224 | tf_op jit(solution)/shard_map/ppermute | solution.py:21
  140.7 1.7 %maximum_select_fusion = bf16[192,4096]{1,0:T(8,128)(2,1)} fusion(bf16[192,2048]{1,0:T(8,128)(2,1)S(1)} %collective-permute-done.27, bf16[192,1024]{1,0:T(8,128)(2,1)S(1)} %copy-done.8, bf16[192,1024]{1,0:T(8,128)(2,1)S(1)} %copy-done.7, pred[]{:T(512)S(6)} %eq.5), kind=kLoop, calls=%fused_computation.1 | loop fusion | flops 10223616 | bytes 3145729 | tf_op jit(solution)/shard_map/jit(_where)/select_n | solution.py:327
  142.4 2.2 %collective-permute-done.32 = bf16[512,128]{1,0:T(8,128)(2,1)S(1)} collective-permute-done((bf16[512,128]{1,0:T(8,128)(2,1)S(1)}, bf16[512,128]{1,0:T(8,128)(2,1)S(1)}, u32[]{:S(2)}, u32[]{:S(2)}) %collective-permute-start.32) | collective-permute-done | bytes 131104 | tf_op jit(solution)/shard_map/ppermute | solution.py:21
  (122 shorter events, 26.7 us)
Async XLA Ops:
  8.1 25.3 %collective-permute-start.1 = (bf16[192,2048]{1,0:T(8,128)(2,1)}, bf16[192,2048]{1,0:T(8,128)(2,1)}, u32[]{:S(2)}, u32[]{:S(2)}) collective-permute-start(bf16[192,2048]{1,0:T(8,128)(2,1)} %pad_maximum_fusion), channel_id=1, source_target_pairs={{0,1},{1,0},{2,3},{3,2},{4,5},{5,4},{6,7},{7,6},{8,9},{9,8},{10,11... | collective-permute-start | bytes 2359304 | tf_op jit(solution)/shard_map/ppermute | solution.py:21
  8.4 13.8 %collective-permute-start.3 = (bf16[384,256]{1,0:T(8,128)(2,1)}, bf16[384,256]{1,0:T(8,128)(2,1)}, u32[]{:S(2)}, u32[]{:S(2)}) collective-permute-start(bf16[384,256]{1,0:T(8,128)(2,1)} %maximum_select_fusion.3.refs_0_), channel_id=1, source_target_pairs={{0,4},{1,5},{2,6},{3,7},{4,0},{5,1},{6,2},{7,3},{8,12},{9,13},{10,... | collective-permute-start | bytes 589832 | tf_op jit(solution)/shard_map/ppermute | solution.py:21
  12.8 11.0 %collective-permute-start.2 = (bf16[384,256]{1,0:T(8,128)(2,1)}, bf16[384,256]{1,0:T(8,128)(2,1)}, u32[]{:S(2)}, u32[]{:S(2)}) collective-permute-start(bf16[384,256]{1,0:T(8,128)(2,1)} %maximum_select_fusion.3.refs_0_), channel_id=1, source_target_pairs={{0,2},{1,3},{2,0},{3,1},{4,6},{5,7},{6,4},{7,5},{8,10},{9,11},{10,... | collective-permute-start | bytes 589832 | tf_op jit(solution)/shard_map/ppermute | solution.py:21
  16.3 42.3 %all-to-all-start = ((bf16[4,192,2048]{2,1,0:T(8,128)(2,1)}), bf16[4,192,2048]{2,1,0:T(8,128)(2,1)}, u32[]{:S(2)}, u32[]{:S(2)}) async-start(bf16[4,192,2048]{2,1,0:T(8,128)(2,1)} %bitcast.10), calls=%async_computation | async-start | bytes 6291456 | tf_op jit(solution)/shard_map/all_to_all | solution.py:402
  22.2 6.7 %collective-permute-start.4 = (bf16[384,256]{1,0:T(8,128)(2,1)}, bf16[384,256]{1,0:T(8,128)(2,1)S(1)}, u32[]{:S(2)}, u32[]{:S(2)}) collective-permute-start(bf16[384,256]{1,0:T(8,128)(2,1)} %collective-permute-done.3.refs_2_), channel_id=1, source_target_pairs={{0,2},{1,3},{2,0},{3,1},{4,6},{5,7},{6,4},{7,5},{8,10},{9,11},{10,... | collective-permute-start | bytes 589832 | tf_op jit(solution)/shard_map/ppermute | solution.py:21
  23.8 34.8 %collective-permute-start.5 = (bf16[192,2048]{1,0:T(8,128)(2,1)}, bf16[192,2048]{1,0:T(8,128)(2,1)}, u32[]{:S(2)}, u32[]{:S(2)}) collective-permute-start(bf16[192,2048]{1,0:T(8,128)(2,1)} %pad_maximum_fusion.1), channel_id=1, source_target_pairs={{0,1},{1,0},{2,3},{3,2},{4,5},{5,4},{6,7},{7,6},{8,9},{9,8},{10,11... | collective-permute-start | bytes 2359304 | tf_op jit(solution)/shard_map/ppermute | solution.py:21
  29.0 22.7 %collective-permute-start.6 = (bf16[384,256]{1,0:T(8,128)(2,1)}, bf16[384,256]{1,0:T(8,128)(2,1)}, u32[]{:S(2)}, u32[]{:S(2)}) collective-permute-start(bf16[384,256]{1,0:T(8,128)(2,1)} %maximum_select_fusion.4.refs_0_), channel_id=1, source_target_pairs={{0,2},{1,3},{2,0},{3,1},{4,6},{5,7},{6,4},{7,5},{8,10},{9,11},{10,... | collective-permute-start | bytes 589832 | tf_op jit(solution)/shard_map/ppermute | solution.py:21
  29.9 28.1 %collective-permute-start.7 = (bf16[384,256]{1,0:T(8,128)(2,1)}, bf16[384,256]{1,0:T(8,128)(2,1)}, u32[]{:S(2)}, u32[]{:S(2)}) collective-permute-start(bf16[384,256]{1,0:T(8,128)(2,1)} %maximum_select_fusion.4.refs_0_), channel_id=1, source_target_pairs={{0,4},{1,5},{2,6},{3,7},{4,0},{5,1},{6,2},{7,3},{8,12},{9,13},{10,... | collective-permute-start | bytes 589832 | tf_op jit(solution)/shard_map/ppermute | solution.py:21
  33.3 25.3 %collective-permute-start.8 = (bf16[384,256]{1,0:T(8,128)(2,1)}, bf16[384,256]{1,0:T(8,128)(2,1)}, u32[]{:S(2)}, u32[]{:S(2)}) collective-permute-start(bf16[384,256]{1,0:T(8,128)(2,1)} %maximum_select_fusion.4.refs_0_), channel_id=1, source_target_pairs={{0,6},{1,7},{2,4},{3,5},{4,2},{5,3},{6,0},{7,1},{8,14},{9,15},{10,... | collective-permute-start | bytes 589832 | tf_op jit(solution)/shard_map/ppermute | solution.py:21
  41.7 31.3 %collective-permute-start.10 = (bf16[384,256]{1,0:T(8,128)(2,1)}, bf16[384,256]{1,0:T(8,128)(2,1)}, u32[]{:S(2)}, u32[]{:S(2)}) collective-permute-start(bf16[384,256]{1,0:T(8,128)(2,1)} %get-tuple-element.79), channel_id=1, source_target_pairs={{0,4},{1,5},{2,6},{3,7},{4,0},{5,1},{6,2},{7,3},{8,12},{9,13},{10,... | collective-permute-start | bytes 589832 | tf_op jit(solution)/shard_map/ppermute | solution.py:21
  51.6 21.5 %collective-permute-start.11 = (bf16[384,256]{1,0:T(8,128)(2,1)}, bf16[384,256]{1,0:T(8,128)(2,1)}, u32[]{:S(2)}, u32[]{:S(2)}) collective-permute-start(bf16[384,256]{1,0:T(8,128)(2,1)} %get-tuple-element.80), channel_id=1, source_target_pairs={{0,6},{1,7},{2,4},{3,5},{4,2},{5,3},{6,0},{7,1},{8,14},{9,15},{10,... | collective-permute-start | bytes 589832 | tf_op jit(solution)/shard_map/ppermute | solution.py:21
  58.0 15.1 %collective-permute-start.9 = (bf16[384,256]{1,0:T(8,128)(2,1)}, bf16[384,256]{1,0:T(8,128)(2,1)}, u32[]{:S(2)}, u32[]{:S(2)}) collective-permute-start(bf16[384,256]{1,0:T(8,128)(2,1)} %get-tuple-element.78), channel_id=1, source_target_pairs={{0,2},{1,3},{2,0},{3,1},{4,6},{5,7},{6,4},{7,5},{8,10},{9,11},{10,... | collective-permute-start | bytes 589832 | tf_op jit(solution)/shard_map/ppermute | solution.py:21
  58.6 35.1 %collective-permute-start.18 = (bf16[768,2048]{1,0:T(8,128)(2,1)}, bf16[768,2048]{1,0:T(8,128)(2,1)}, u32[]{:S(2)}, u32[]{:S(2)}) collective-permute-start(bf16[768,2048]{1,0:T(8,128)(2,1)} %bitcast.4.refs_4_), channel_id=1, source_target_pairs={{0,1},{1,0},{2,3},{3,2},{4,5},{5,4},{6,7},{7,6},{8,9},{9,8},{10,11... | collective-permute-start | bytes 9437192 | tf_op jit(solution)/shard_map/ppermute | solution.py:21
  67.2 11.7 %collective-permute-start.12 = (bf16[768,128]{1,0:T(8,128)(2,1)}, bf16[768,128]{1,0:T(8,128)(2,1)S(1)}, u32[]{:S(2)}, u32[]{:S(2)}) collective-permute-start(bf16[768,128]{1,0:T(8,128)(2,1)} %get-tuple-element.88), channel_id=1, source_target_pairs={{0,2},{1,3},{2,0},{3,1},{4,6},{5,7},{6,4},{7,5},{8,10},{9,11},{10,... | collective-permute-start | bytes 589832 | tf_op jit(solution)/shard_map/ppermute | solution.py:21
  73.0 10.0 %collective-permute-start.17 = (bf16[768,128]{1,0:T(8,128)(2,1)}, bf16[768,128]{1,0:T(8,128)(2,1)S(1)}, u32[]{:S(2)}, u32[]{:S(2)}) collective-permute-start(bf16[768,128]{1,0:T(8,128)(2,1)} %get-tuple-element.91), channel_id=1, source_target_pairs={{0,2},{1,3},{2,0},{3,1},{4,6},{5,7},{6,4},{7,5},{8,10},{9,11},{10,... | collective-permute-start | bytes 589832 | tf_op jit(solution)/shard_map/ppermute | solution.py:21
  74.4 19.1 %collective-permute-start.14 = (bf16[384,256]{1,0:T(8,128)(2,1)S(1)}, bf16[384,256]{1,0:T(8,128)(2,1)S(1)}, u32[]{:S(2)}, u32[]{:S(2)}) collective-permute-start(bf16[384,256]{1,0:T(8,128)(2,1)S(1)} %maximum_select_fusion.5.refs_0_), channel_id=1, source_target_pairs={{0,8},{8,0},{16,24},{24,16},{1,9},{9,1},{17,25},{25,17},{2,10},{10... | collective-permute-start | bytes 589832 | tf_op jit(solution)/shard_map/ppermute | solution.py:21
  76.0 17.6 %collective-permute-start.15 = (bf16[384,256]{1,0:T(8,128)(2,1)S(1)}, bf16[384,256]{1,0:T(8,128)(2,1)S(1)}, u32[]{:S(2)}, u32[]{:S(2)}) collective-permute-start(bf16[384,256]{1,0:T(8,128)(2,1)S(1)} %maximum_select_fusion.5.refs_0_), channel_id=1, source_target_pairs={{0,16},{8,24},{16,0},{24,8},{1,17},{9,25},{17,1},{25,9},{2,18},{10... | collective-permute-start | bytes 589832 | tf_op jit(solution)/shard_map/ppermute | solution.py:21
  79.0 14.6 %collective-permute-start.16 = (bf16[384,256]{1,0:T(8,128)(2,1)S(1)}, bf16[384,256]{1,0:T(8,128)(2,1)S(1)}, u32[]{:S(2)}, u32[]{:S(2)}) collective-permute-start(bf16[384,256]{1,0:T(8,128)(2,1)S(1)} %maximum_select_fusion.5.refs_0_), channel_id=1, source_target_pairs={{0,24},{8,16},{16,8},{24,0},{1,25},{9,17},{17,9},{25,1},{2,26},{10... | collective-permute-start | bytes 589832 | tf_op jit(solution)/shard_map/ppermute | solution.py:21
  83.0 18.3 %collective-permute-start.13 = (bf16[384,128]{1,0:T(8,128)(2,1)S(1)}, bf16[384,128]{1,0:T(8,128)(2,1)S(1)}, u32[]{:S(2)}, u32[]{:S(2)}) collective-permute-start(bf16[384,128]{1,0:T(8,128)(2,1)S(1)} %get-tuple-element.163), channel_id=1, source_target_pairs={{0,4},{1,5},{2,6},{3,7},{4,0},{5,1},{6,2},{7,3},{8,12},{9,13},{10,... | collective-permute-start | bytes 294920 | tf_op jit(solution)/shard_map/ppermute | solution.py:21
  93.5 11.5 %collective-permute-start.19 = (bf16[384,128]{1,0:T(8,128)(2,1)S(1)}, bf16[384,128]{1,0:T(8,128)(2,1)S(1)}, u32[]{:S(2)}, u32[]{:S(2)}) collective-permute-start(bf16[384,128]{1,0:T(8,128)(2,1)S(1)} %get-tuple-element.161), channel_id=1, source_target_pairs={{0,4},{1,5},{2,6},{3,7},{4,0},{5,1},{6,2},{7,3},{8,12},{9,13},{10,... | collective-permute-start | bytes 294920 | tf_op jit(solution)/shard_map/ppermute | solution.py:21
  101.4 5.3 %collective-permute-start.24 = (bf16[384,128]{1,0:T(8,128)(2,1)S(1)}, bf16[384,128]{1,0:T(8,128)(2,1)S(1)}, u32[]{:S(2)}, u32[]{:S(2)}) collective-permute-start(bf16[384,128]{1,0:T(8,128)(2,1)S(1)} %maximum_select_fusion.8.refs_0_), channel_id=1, source_target_pairs={{0,8},{8,0},{16,24},{24,16},{1,9},{9,1},{17,25},{25,17},{2,10},{10... | collective-permute-start | bytes 294920 | tf_op jit(solution)/shard_map/ppermute | solution.py:21
  104.4 5.6 %collective-permute-start.26 = (bf16[384,128]{1,0:T(8,128)(2,1)S(1)}, bf16[384,128]{1,0:T(8,128)(2,1)S(1)}, u32[]{:S(2)}, u32[]{:S(2)}) collective-permute-start(bf16[384,128]{1,0:T(8,128)(2,1)S(1)} %maximum_select_fusion.8.refs_0_), channel_id=1, source_target_pairs={{0,24},{8,16},{16,8},{24,0},{1,25},{9,17},{17,9},{25,1},{2,26},{10... | collective-permute-start | bytes 294920 | tf_op jit(solution)/shard_map/ppermute | solution.py:21
  104.9 12.7 %collective-permute-start.23 = (bf16[1024,256]{1,0:T(8,128)(2,1)S(1)}, bf16[1024,256]{1,0:T(8,128)(2,1)S(1)}, u32[]{:S(2)}, u32[]{:S(2)}) collective-permute-start(bf16[1024,256]{1,0:T(8,128)(2,1)S(1)} %get-tuple-element.106), channel_id=1, source_target_pairs={{0,2},{1,3},{2,0},{3,1},{4,6},{5,7},{6,4},{7,5},{8,10},{9,11},{10,... | collective-permute-start | bytes 1572872 | tf_op jit(solution)/shard_map/ppermute | solution.py:21
  105.1 16.1 %collective-permute-start.20 = (bf16[384,128]{1,0:T(8,128)(2,1)S(1)}, bf16[384,128]{1,0:T(8,128)(2,1)S(1)}, u32[]{:S(2)}, u32[]{:S(2)}) collective-permute-start(bf16[384,128]{1,0:T(8,128)(2,1)S(1)} %maximum_select_fusion.9.refs_0_), channel_id=1, source_target_pairs={{0,8},{8,0},{16,24},{24,16},{1,9},{9,1},{17,25},{25,17},{2,10},{10... | collective-permute-start | bytes 294920 | tf_op jit(solution)/shard_map/ppermute | solution.py:21
  106.6 14.5 %collective-permute-start.21 = (bf16[384,128]{1,0:T(8,128)(2,1)S(1)}, bf16[384,128]{1,0:T(8,128)(2,1)S(1)}, u32[]{:S(2)}, u32[]{:S(2)}) collective-permute-start(bf16[384,128]{1,0:T(8,128)(2,1)S(1)} %maximum_select_fusion.9.refs_0_), channel_id=1, source_target_pairs={{0,16},{8,24},{16,0},{24,8},{1,17},{9,25},{17,1},{25,9},{2,18},{10... | collective-permute-start | bytes 294920 | tf_op jit(solution)/shard_map/ppermute | solution.py:21
  108.1 13.0 %collective-permute-start.22 = (bf16[384,128]{1,0:T(8,128)(2,1)S(1)}, bf16[384,128]{1,0:T(8,128)(2,1)S(1)}, u32[]{:S(2)}, u32[]{:S(2)}) collective-permute-start(bf16[384,128]{1,0:T(8,128)(2,1)S(1)} %maximum_select_fusion.9.refs_0_), channel_id=1, source_target_pairs={{0,24},{8,16},{16,8},{24,0},{1,25},{9,17},{17,9},{25,1},{2,26},{10... | collective-permute-start | bytes 294920 | tf_op jit(solution)/shard_map/ppermute | solution.py:21
  115.4 13.0 %collective-permute-start.31 = (bf16[1024,128]{1,0:T(8,128)(2,1)S(1)}, bf16[1024,128]{1,0:T(8,128)(2,1)S(1)}, u32[]{:S(2)}, u32[]{:S(2)}) collective-permute-start(bf16[1024,128]{1,0:T(8,128)(2,1)S(1)} %get-tuple-element.117), channel_id=1, source_target_pairs={{0,2},{1,3},{2,0},{3,1},{4,6},{5,7},{6,4},{7,5},{8,10},{9,11},{10,... | collective-permute-start | bytes 786440 | tf_op jit(solution)/shard_map/ppermute | solution.py:21
  117.7 20.2 %collective-permute-start.29 = (bf16[512,256]{1,0:T(8,128)(2,1)S(1)}, bf16[512,256]{1,0:T(8,128)(2,1)S(1)}, u32[]{:S(2)}, u32[]{:S(2)}) collective-permute-start(bf16[512,256]{1,0:T(8,128)(2,1)S(1)} %get-tuple-element.143), channel_id=1, source_target_pairs={{0,4},{1,5},{2,6},{3,7},{4,0},{5,1},{6,2},{7,3},{8,12},{9,13},{10,... | collective-permute-start | bytes 786440 | tf_op jit(solution)/shard_map/ppermute | solution.py:21
  126.6 9.2 %collective-permute-start.30 = (bf16[1024,128]{1,0:T(8,128)(2,1)S(1)}, bf16[1024,128]{1,0:T(8,128)(2,1)S(1)}, u32[]{:S(2)}, u32[]{:S(2)}) collective-permute-start(bf16[1024,128]{1,0:T(8,128)(2,1)S(1)} %get-tuple-element.130), channel_id=1, source_target_pairs={{0,2},{1,3},{2,0},{3,1},{4,6},{5,7},{6,4},{7,5},{8,10},{9,11},{10,... | collective-permute-start | bytes 786440 | tf_op jit(solution)/shard_map/ppermute | solution.py:21
  128.5 9.7 %collective-permute-start.33 = (bf16[512,128]{1,0:T(8,128)(2,1)S(1)}, bf16[512,128]{1,0:T(8,128)(2,1)S(1)}, u32[]{:S(2)}, u32[]{:S(2)}) collective-permute-start(bf16[512,128]{1,0:T(8,128)(2,1)S(1)} %get-tuple-element.153), channel_id=1, source_target_pairs={{0,4},{1,5},{2,6},{3,7},{4,0},{5,1},{6,2},{7,3},{8,12},{9,13},{10,... | collective-permute-start | bytes 393224 | tf_op jit(solution)/shard_map/ppermute | solution.py:21
  131.1 9.6 %collective-permute-start.27 = (bf16[192,2048]{1,0:T(8,128)(2,1)S(1)}, bf16[192,2048]{1,0:T(8,128)(2,1)S(1)}, u32[]{:S(2)}, u32[]{:S(2)}) collective-permute-start(bf16[192,2048]{1,0:T(8,128)(2,1)S(1)} %pad_maximum_fusion.2), channel_id=1, source_target_pairs={{0,1},{1,0},{2,3},{3,2},{4,5},{5,4},{6,7},{7,6},{8,9},{9,8},{10,11... | collective-permute-start | bytes 2359304 | tf_op jit(solution)/shard_map/ppermute | solution.py:21
  135.9 8.7 %collective-permute-start.32 = (bf16[512,128]{1,0:T(8,128)(2,1)S(1)}, bf16[512,128]{1,0:T(8,128)(2,1)S(1)}, u32[]{:S(2)}, u32[]{:S(2)}) collective-permute-start(bf16[512,128]{1,0:T(8,128)(2,1)S(1)} %get-tuple-element.151), channel_id=1, source_target_pairs={{0,4},{1,5},{2,6},{3,7},{4,0},{5,1},{6,2},{7,3},{8,12},{9,13},{10,... | collective-permute-start | bytes 393224 | tf_op jit(solution)/shard_map/ppermute | solution.py:21
  (20 other events, 166.6 us)
